TPU v7x, 32 devices: a whole 2x2x4 slice. The times are simulated.
32 devices in a mesh: tm: 16 (over z, y, x), span: 2 (over core).
Axes of the slice: x: 2, y: 2, z: 4, core: 2. Of those that a mesh axis runs over, the one named last changes fastest.
Arguments:
- frames: bfloat16 [16, 64, 64, 128], P('tm', None, 'span'), may hold values from -6 to 6
- cotangent: bfloat16 [16, 64, 64, 128], P('tm', None, 'span'), may hold values from -6 to 6
- spatial_weight: bfloat16 [3, 3, 64, 64], replicated, may hold values from -0.25 to 0.25
- temporal_kernel: bfloat16 [64, 16], replicated, may hold values from -1.5 to 1.5
Outputs:
- block_output: bfloat16 [16, 64, 64, 128], P('tm', None, 'span')
- input_grad: bfloat16 [16, 64, 64, 128], P('tm', None, 'span')
- weight_grad: float32 [3, 3, 64, 64], replicated
- kernel_grad: float32 [64, 16], replicated
All inputs are finite; a program needn't handle non-finite values.
Results may differ from a plain program's by a relative error of at most 0.0051.
Values may be sent and summed in bfloat16 or wider, within the bound.
No kernel may reach another device: no remote copies, remote signals or barrier semaphores. Data moves between devices by JAX's collectives and lax.ppermute only.
A program may use at most 64 MiB of HBM per device.

v0:
```python
import jax
import jax.numpy as jnp
from jax import lax
from jax.sharding import PartitionSpec as P


def padded_2(x, sides, width):
    for axis, dim in sides:
        size, length = (lax.axis_size(axis), x.shape[dim])
        up = [(i, (i + 1) % size) for i in range(size - 1)]
        down = [(j, i) for i, j in up]
        last = lax.slice_in_dim(x, length - width, length, axis=dim)
        first = lax.slice_in_dim(x, 0, width, axis=dim)
        before = lax.ppermute(last, axis, up)
        after = lax.ppermute(first, axis, down)
        x = jnp.concatenate([before, x, after], axis=dim)
    return x


def toeplitz(kernel):
    count = kernel.shape[1]
    chans = kernel.shape[0]
    vector = jnp.concatenate(
        [
            jnp.zeros((chans, 1), kernel.dtype),
            kernel[:, ::-1],
            jnp.zeros((chans, count - 1), kernel.dtype),
        ],
        axis=1,
    )
    tiled = jnp.tile(vector, (1, count))
    skewed = tiled[:, count : count + count * (2 * count - 1)].reshape(chans, count, 2 * count - 1)
    return skewed[:, :, :count]


def diagonal_sums(products):
    chans = products.shape[0]
    count = products.shape[1]
    flipped = products[:, :, ::-1]
    wide = jnp.concatenate([flipped, jnp.zeros_like(flipped)], axis=2)
    skewed = wide.reshape(chans, 2 * count * count)[:, : count * (2 * count - 1)].reshape(
        chans, count, 2 * count - 1
    )
    return jnp.sum(skewed[:, :, count - 1 :], axis=1)


def pad_chord(field):
    return jnp.pad(field, ((0, 0), (0, 0), (0, 0), (1, 1)))


def local(frames, cotangent, spatial_weight, temporal_kernel):
    local_steps, channels, rows, width = frames.shape
    frame_count = local_steps * lax.axis_size("tm")
    gscale = float(frame_count * rows * lax.axis_size("span") * width) ** (-0.5)
    padded = pad_chord(padded_2(frames, (("span", 2),), 1))
    hidden = jnp.zeros((local_steps, channels, rows, width), jnp.float32)
    for row_off in range(3):
        for col_off in range(3):
            slab = padded[:, :, row_off : row_off + rows, col_off : col_off + width]
            hidden = hidden + jnp.einsum(
                "oi,tisw->tosw",
                spatial_weight[row_off, col_off],
                slab,
                preferred_element_type=jnp.float32,
            )
    sigma = jax.nn.sigmoid(hidden)
    active = (hidden * sigma).astype(jnp.bfloat16)
    flat_act = active.reshape(local_steps, channels, rows * width)
    flat_cot = cotangent.reshape(local_steps, channels, rows * width)
    toe = toeplitz(temporal_kernel)
    tile_act = lax.all_to_all(flat_act, "tm", split_axis=2, concat_axis=0, tiled=True)
    back_along = lax.all_to_all(
        jnp.einsum("cts,scn->tcn", toe, tile_act, preferred_element_type=jnp.float32).astype(
            jnp.bfloat16
        ),
        "tm",
        split_axis=0,
        concat_axis=2,
        tiled=True,
    )
    tile_cot = lax.all_to_all(flat_cot, "tm", split_axis=2, concat_axis=0, tiled=True)
    back_grad = lax.all_to_all(
        jnp.einsum("cts,tcn->scn", toe, tile_cot, preferred_element_type=jnp.float32).astype(
            jnp.bfloat16
        ),
        "tm",
        split_axis=0,
        concat_axis=2,
        tiled=True,
    )
    lag_terms = diagonal_sums(
        jnp.einsum("tcn,scn->cts", tile_cot, tile_act, preferred_element_type=jnp.float32)
    )
    block_output = (
        frames.astype(jnp.float32) + back_along.reshape(frames.shape).astype(jnp.float32)
    ).astype(jnp.bfloat16)
    dhidden = (
        back_grad.reshape(frames.shape).astype(jnp.float32) * sigma * (1.0 + hidden * (1.0 - sigma))
    ).astype(jnp.bfloat16)
    dpadded = pad_chord(padded_2(dhidden, (("span", 2),), 1))
    grad_sum = cotangent.astype(jnp.float32)
    weight_terms = []
    for row_off in range(3):
        for col_off in range(3):
            dslab = dpadded[
                :, :, 2 - row_off : 2 - row_off + rows, 2 - col_off : 2 - col_off + width
            ]
            grad_sum = grad_sum + jnp.einsum(
                "oi,tosw->tisw",
                spatial_weight[row_off, col_off],
                dslab,
                preferred_element_type=jnp.float32,
            )
            slab = padded[:, :, row_off : row_off + rows, col_off : col_off + width]
            weight_terms.append(
                jnp.einsum("tosw,tisw->oi", dhidden, slab, preferred_element_type=jnp.float32)
            )
    input_grad = grad_sum.astype(jnp.bfloat16)
    weight_local = jnp.stack(weight_terms).reshape(3, 3, channels, channels)
    weight_total, kernel_total = lax.psum((weight_local, lag_terms), ("tm", "span"))
    return (block_output, input_grad, weight_total * gscale, kernel_total * gscale)


def solution(mesh):
    placed = (P("tm", None, "span", None), P("tm", None, "span", None), P(), P())
    return jax.shard_map(
        local,
        mesh=mesh,
        in_specs=placed,
        out_specs=(P("tm", None, "span", None), P("tm", None, "span", None), P(), P()),
        check_vma=False,
    )
```

profile of v0, /device:TPU:0, one launch (start us, length us, event | category | flops | bytes accessed | tf_op | source)
XLA Modules:
  0.0 291.8 jit_solution(6347026564273147947)
XLA Ops:
  7.2 1.3 copy.81
  8.5 2.4 collective-permute-start
  10.9 1.3 collective-permute-start.1
  12.4 2.8 copy.94
  15.2 0.5 broadcast.43
  15.7 23.4 %reduce = bf16[4096,64]{1,0:T(8,128)(2,1)} reduce(bf16[4096,1,64]{2,1,0:T(2,128)(2,1)S(1)} %bitcast.335, bf16[]{:T(256)} %broadcast.43), dimensions={1}, to_apply=%bitcast.317.reduce_sub_computation | reduce | bytes 1048578
  39.1 3.0 %reshape.223 = bf16[16,2,8192]{2,1,0:T(2,128)(2,1)} reshape(bf16[4096,64]{1,0:T(8,128)(2,1)} %reduce) | data formatting | bytes 1048576
  42.1 7.7 %all-to-all-start.2 = ((bf16[16,2,8192]{2,1,0:T(2,128)(2,1)}), bf16[16,2,8192]{2,1,0:T(2,128)(2,1)}, u32[]{:S(2)}, u32[]{:S(2)}) async-start(bf16[16,2,8192]{2,1,0:T(2,128)(2,1)} %reshape.223), calls=%async_computation.2 | async-start | bytes 1048576 | tf_op jit(solution)/shard_map/all_to_all | solution.py:81
  50.5 0.6 select_maximum_fusion.2
  51.0 1.0 fusion.45
  52.0 1.0 convolution_add_fusion.6
  53.0 1.1 convolution_add_fusion.5
  54.1 2.0 convolution_add_fusion.4
  56.1 9.1 %all-to-all-done.2 = bf16[16,2,8192]{2,1,0:T(2,128)(2,1)} async-done(((bf16[16,2,8192]{2,1,0:T(2,128)(2,1)}), bf16[16,2,8192]{2,1,0:T(2,128)(2,1)}, u32[]{:S(2)}, u32[]{:S(2)}) %all-to-all-start.2) | async-done | bytes 524320 | tf_op jit(solution)/shard_map/all_to_all | solution.py:81
  65.3 4.1 %reshape.224 = bf16[4096,1,64]{2,1,0:T(2,128)(2,1)S(1)} reshape(bf16[16,2,8192]{2,1,0:T(2,128)(2,1)} %all-to-all-done.2) | data formatting | bytes 1048576
  69.4 3.6 %copy.95 = bf16[1,64,4096]{2,1,0:T(8,128)(2,1)} copy(bf16[1,64,4096]{1,0,2:T(2,128)(2,1)S(1)} %bitcast.333) | data formatting | bytes 1048576 | tf_op jit(solution)/shard_map/all_to_all | solution.py:81
  73.0 1.1 copy.136
  74.2 0.3 fusion.13
  74.5 1.0 copy.97
  75.5 5.4 %all-to-all-start.3 = ((bf16[16,64,256]{2,1,0:T(8,128)(2,1)}), bf16[16,64,256]{2,1,0:T(8,128)(2,1)}, u32[]{:S(2)}, u32[]{:S(2)}) async-start(bf16[16,64,256]{2,1,0:T(8,128)(2,1)} %copy.97), calls=%async_computation.3 | async-start | bytes 1048576 | tf_op jit(solution)/shard_map/all_to_all | solution.py:82
  81.1 2.1 fusion.46
  83.2 1.0 convolution_add_fusion.3
  84.2 1.1 convolution_add_fusion.2
  85.3 2.0 convolution_add_fusion.1
  87.3 8.9 %all-to-all-done.3 = bf16[16,64,256]{2,1,0:T(8,128)(2,1)} async-done(((bf16[16,64,256]{2,1,0:T(8,128)(2,1)}), bf16[16,64,256]{2,1,0:T(8,128)(2,1)}, u32[]{:S(2)}, u32[]{:S(2)}) %all-to-all-start.3) | async-done | bytes 524320 | tf_op jit(solution)/shard_map/all_to_all | solution.py:82
  96.2 1.1 convert_bitcast_fusion
  97.4 1.6 copy.98
  99.0 2.3 reshape.185
  101.3 3.6 %fusion.26 = (bf16[1,64,32,128]{3,1,2,0:T(8,128)(2,1)S(1)}, bf16[1,64,32,128]{3,1,2,0:T(8,128)(2,1)}) fusion(f32[1,64,32,128]{3,2,1,0:T(8,128)} %reshape.185, f32[32,128,64]{1,2,0:T(8,128)} %fusion.46, f32[32,128,64]{1,2,0:T(8,128)} %convolution_add_fusion.1, bf16[1,64,1,128]{3,1,2,0:T(8,128)(2,1)S(1)} %collective-permute-done.1, ...), kind=kOutput, calls=%fused_computation.63 | convolution fusion | flops 38010880 | bytes 4751360 | tf_op jit(solution)/shard_map/oi,tisw->tosw/dot_general | solution.py:60
  105.5 0.4 fusion.22
  106.2 0.3 fusion.20
  106.5 0.4 fusion.19
  107.5 0.4 fusion.16
  107.9 1.4 collective-permute-start.2
  109.3 1.3 collective-permute-start.3
  110.6 1.1 convolution_bitcast_fusion.4
  111.7 1.3 copy.122
  113.0 6.9 %reshape.219 = bf16[1,64,4096]{1,0,2:T(2,128)(2,1)} reshape(bf16[1,64,32,128]{1,3,2,0:T(8,128)(2,1)} %copy.122) | data formatting | bytes 1048576 | tf_op jit(solution)/shard_map/reshape | solution.py:68
  119.9 24.4 %reduce.1 = bf16[4096,64]{1,0:T(8,128)(2,1)} reduce(bf16[4096,1,64]{2,1,0:T(2,128)(2,1)} %bitcast.336, bf16[]{:T(256)} %broadcast.43), dimensions={1}, to_apply=%bitcast.315.reduce_sub_computation | reduce | bytes 1048578
  144.3 3.0 %reshape.221 = bf16[16,2,8192]{2,1,0:T(2,128)(2,1)} reshape(bf16[4096,64]{1,0:T(8,128)(2,1)} %reduce.1) | data formatting | bytes 1048576
  147.3 3.9 %all-to-all-start = ((bf16[16,2,8192]{2,1,0:T(2,128)(2,1)}), bf16[16,2,8192]{2,1,0:T(2,128)(2,1)S(1)}, u32[]{:S(2)}, u32[]{:S(2)}) async-start(bf16[16,2,8192]{2,1,0:T(2,128)(2,1)} %reshape.221), calls=%async_computation | async-start | bytes 1048576 | tf_op jit(solution)/shard_map/all_to_all | solution.py:71
  151.3 0.6 select_maximum_fusion
  152.2 1.3 convolution_bitcast_fusion
  153.5 1.3 convolution_bitcast_fusion.1
  154.8 1.4 convolution_bitcast_fusion.2
  156.2 1.4 convolution_bitcast_fusion.3
  157.5 1.4 convolution_bitcast_fusion.5
  158.9 1.4 convolution_bitcast_fusion.6
  160.3 1.5 fusion.3
  161.8 4.8 %all-to-all-done = bf16[16,2,8192]{2,1,0:T(2,128)(2,1)S(1)} async-done(((bf16[16,2,8192]{2,1,0:T(2,128)(2,1)}), bf16[16,2,8192]{2,1,0:T(2,128)(2,1)S(1)}, u32[]{:S(2)}, u32[]{:S(2)}) %all-to-all-start) | async-done | bytes 524320 | tf_op jit(solution)/shard_map/all_to_all | solution.py:71
  166.6 3.6 %reshape.222 = bf16[4096,1,64]{2,1,0:T(2,128)(2,1)} reshape(bf16[16,2,8192]{2,1,0:T(2,128)(2,1)S(1)} %all-to-all-done) | data formatting | bytes 1048576
  170.2 5.2 %copy.89 = bf16[1,64,4096]{2,1,0:T(8,128)(2,1)} copy(bf16[1,64,4096]{1,0,2:T(2,128)(2,1)} %bitcast.334) | data formatting | bytes 1048576 | tf_op jit(solution)/shard_map/all_to_all | solution.py:71
  175.4 1.1 copy.135
  176.9 1.0 copy.91
  177.8 5.4 %all-to-all-start.1 = ((bf16[16,64,256]{2,1,0:T(8,128)(2,1)}), bf16[16,64,256]{2,1,0:T(8,128)(2,1)}, u32[]{:S(2)}, u32[]{:S(2)}) async-start(bf16[16,64,256]{2,1,0:T(8,128)(2,1)} %copy.91), calls=%async_computation.1 | async-start | bytes 1048576 | tf_op jit(solution)/shard_map/all_to_all | solution.py:72
  183.3 3.8 %fusion.12 = bf16[1,64,32,128]{3,1,2,0:T(8,128)(2,1)S(1)} fusion(f32[1,64,32,128]{3,1,2,0:T(8,128)} %convolution_bitcast_fusion, f32[1,64,32,128]{3,1,2,0:T(8,128)} %convolution_bitcast_fusion.1, f32[1,64,32,128]{3,1,2,0:T(8,128)} %convolution_bitcast_fusion.2, f32[1,64,32,128]{3,1,2,0:T(8,128)} %convolution_bitcast_fusion.3, ...), kind=kOutput, calls=%fused_computation.30 | convolution fusion | flops 36175872 | bytes 9469952 | tf_op jit(solution)/shard_map/oi,tosw->tisw/dot_general | solution.py:108
  187.1 1.1 copy.111
  188.2 49.6 %all-reduce.5.cloned.1.call-done = f32[3,3,64,64]{3,2,1,0:T(8,128)} async-done(((f32[3,3,64,64]{3,2,1,0:T(8,128)}), f32[3,3,64,64]{3,2,1,0:T(8,128)}) %all-reduce.5.cloned.1.call-update) | async-done | bytes 147472 | tf_op jit(solution)/shard_map/psum | solution.py:120
  237.8 1.7 broadcast_multiply_fusion
  240.3 41.3 %psum.15 = f32[64,16]{0,1:T(8,128)S(1)} all-reduce(f32[64,16]{0,1:T(8,128)S(1)} %slice_reduce_fusion), channel_id=1, replica_groups=mesh['tm'=16,'span'=2] {'tm','span'}, use_global_device_ids=true, to_apply=%region_2.3 | all-reduce | flops 1024 | bytes 8192 | tf_op jit(solution)/shard_map/psum | solution.py:120
  281.5 0.6 broadcast_multiply_fusion.1
  282.1 1.1 convert_bitcast_fusion.1
  283.3 0.6 copy.92
  284.0 0.9 add_convert_fusion
  (54 shorter events, 3.8 us)
Async XLA Ops:
  7.2 5.0 %copy-start.4 = (bf16[1,64,32,128]{3,2,1,0:T(8,128)(2,1)S(1)}, bf16[1,64,32,128]{3,2,1,0:T(8,128)(2,1)}, u32[]{:S(2)}) copy-start(bf16[1,64,32,128]{3,2,1,0:T(8,128)(2,1)} %param.5) | copy-start | bytes 1572868
  8.5 43.5 %copy-start = (bf16[1,64,32,128]{3,1,2,0:T(8,128)(2,1)}, bf16[1,64,32,128]{3,1,2,0:T(8,128)(2,1)S(1)}, u32[]{:S(2)}) copy-start(bf16[1,64,32,128]{3,1,2,0:T(8,128)(2,1)S(1)} %copy.81) | copy-start | bytes 1572868
  8.5 41.9 %collective-permute-start = (bf16[1,64,1,128]{3,1,2,0:T(8,128)(2,1)S(1)}, bf16[1,64,1,128]{3,1,2,0:T(8,128)(2,1)S(1)}, u32[]{:S(2)}, u32[]{:S(2)}) collective-permute-start(bf16[1,64,1,128]{3,1,2,0:T(8,128)(2,1)S(1)} %get-tuple-element.24), channel_id=1, source_target_pairs={{0,1},{2,3},{4,5},{6,7},{8,9},{10,11},{12,13},{14,15},{16,17},{18,... | collective-permute-start | bytes 49160 | tf_op jit(solution)/shard_map/ppermute | solution.py:14
  10.9 39.6 %collective-permute-start.1 = (bf16[1,64,1,128]{3,1,2,0:T(8,128)(2,1)S(1)}, bf16[1,64,1,128]{3,1,2,0:T(8,128)(2,1)S(1)}, u32[]{:S(2)}, u32[]{:S(2)}) collective-permute-start(bf16[1,64,1,128]{3,1,2,0:T(8,128)(2,1)S(1)} %get-tuple-element.25), channel_id=1, source_target_pairs={{1,0},{3,2},{5,4},{7,6},{9,8},{11,10},{13,12},{15,14},{17,16},{19,... | collective-permute-start | bytes 49160 | tf_op jit(solution)/shard_map/ppermute | solution.py:15
  39.1 10.8 %copy-start.9 = (bf16[64,16]{0,1:T(8,128)(2,1)S(1)}, bf16[64,16]{0,1:T(8,128)(2,1)}, u32[]{:S(2)}) copy-start(bf16[64,16]{0,1:T(8,128)(2,1)} %param.7) | copy-start | bytes 6148
  42.1 23.1 %all-to-all-start.2 = ((bf16[16,2,8192]{2,1,0:T(2,128)(2,1)}), bf16[16,2,8192]{2,1,0:T(2,128)(2,1)}, u32[]{:S(2)}, u32[]{:S(2)}) async-start(bf16[16,2,8192]{2,1,0:T(2,128)(2,1)} %reshape.223), calls=%async_computation.2 | async-start | bytes 1048576 | tf_op jit(solution)/shard_map/all_to_all | solution.py:81
  75.5 7.7 %copy-start.2 = (bf16[1,64,32,128]{3,2,1,0:T(8,128)(2,1)S(1)}, bf16[1,64,32,128]{3,2,1,0:T(8,128)(2,1)}, u32[]{:S(2)}) copy-start(bf16[1,64,32,128]{3,2,1,0:T(8,128)(2,1)} %param.4) | copy-start | bytes 1572868
  75.5 7.7 %copy-start.3 = (f32[32,128,64]{1,2,0:T(8,128)S(1)}, f32[32,128,64]{1,2,0:T(8,128)}, u32[]{:S(2)}) copy-start(f32[32,128,64]{1,2,0:T(8,128)} %convolution_add_fusion.4) | copy-start | bytes 3145732
  75.5 20.8 %all-to-all-start.3 = ((bf16[16,64,256]{2,1,0:T(8,128)(2,1)}), bf16[16,64,256]{2,1,0:T(8,128)(2,1)}, u32[]{:S(2)}, u32[]{:S(2)}) async-start(bf16[16,64,256]{2,1,0:T(8,128)(2,1)} %copy.97), calls=%async_computation.3 | async-start | bytes 1048576 | tf_op jit(solution)/shard_map/all_to_all | solution.py:82
  80.9 156.9 %all-reduce.5.cloned.1.call-start = ((), (), s32[]{:S(2)}) async-start(), calls=%async_computation.4 | async-start | bytes 589824 | tf_op jit(solution)/shard_map/psum | solution.py:120
  99.0 2.3 copy-start.1
  107.8 1.5 copy-start.8
  107.9 3.8 %copy-start.7 = (bf16[1,64,32,128]{3,1,2,0:T(8,128)(2,1)S(1)}, bf16[1,64,32,128]{3,1,2,0:T(8,128)(2,1)}, u32[]{:S(2)}) copy-start(bf16[1,64,32,128]{3,1,2,0:T(8,128)(2,1)} %get-tuple-element.21) | copy-start | bytes 1572868
  107.9 43.4 %collective-permute-start.2 = (bf16[1,64,1,128]{3,1,2,0:T(8,128)(2,1)S(1)}, bf16[1,64,1,128]{3,1,2,0:T(8,128)(2,1)S(1)}, u32[]{:S(2)}, u32[]{:S(2)}) collective-permute-start(bf16[1,64,1,128]{3,1,2,0:T(8,128)(2,1)S(1)} %get-tuple-element.22), channel_id=1, source_target_pairs={{0,1},{2,3},{4,5},{6,7},{8,9},{10,11},{12,13},{14,15},{16,17},{18,... | collective-permute-start | bytes 49160 | tf_op jit(solution)/shard_map/ppermute | solution.py:14
  109.3 42.0 %collective-permute-start.3 = (bf16[1,64,1,128]{3,1,2,0:T(8,128)(2,1)S(1)}, bf16[1,64,1,128]{3,1,2,0:T(8,128)(2,1)S(1)}, u32[]{:S(2)}, u32[]{:S(2)}) collective-permute-start(bf16[1,64,1,128]{3,1,2,0:T(8,128)(2,1)S(1)} %get-tuple-element.23), channel_id=1, source_target_pairs={{1,0},{3,2},{5,4},{7,6},{9,8},{11,10},{13,12},{15,14},{17,16},{19,... | collective-permute-start | bytes 49160 | tf_op jit(solution)/shard_map/ppermute | solution.py:15
  147.3 19.3 %all-to-all-start = ((bf16[16,2,8192]{2,1,0:T(2,128)(2,1)}), bf16[16,2,8192]{2,1,0:T(2,128)(2,1)S(1)}, u32[]{:S(2)}, u32[]{:S(2)}) async-start(bf16[16,2,8192]{2,1,0:T(2,128)(2,1)} %reshape.221), calls=%async_computation | async-start | bytes 1048576 | tf_op jit(solution)/shard_map/all_to_all | solution.py:71
  151.3 0.9 copy-start.6
  158.9 1.4 copy-start.5
  177.8 104.3 %all-to-all-start.1 = ((bf16[16,64,256]{2,1,0:T(8,128)(2,1)}), bf16[16,64,256]{2,1,0:T(8,128)(2,1)}, u32[]{:S(2)}, u32[]{:S(2)}) async-start(bf16[16,64,256]{2,1,0:T(8,128)(2,1)} %copy.91), calls=%async_computation.1 | async-start | bytes 1048576 | tf_op jit(solution)/shard_map/all_to_all | solution.py:72
Sparse Core Ops, SparseCore 0:
  111.8 125.9 all-reduce.4
where the time goes:
time: 294 us; the launch traced here: 292 us
  waiting for transfers between devices  72.6 us (25%)
  other arithmetic  54.6 us (19%)
  local copies, waits for them, and re-layouts  46.7 us (16%)
  blocking collectives  41.3 us (14%)
  matrix products  33 us (11%)
  starting transfers between devices  29.1 us (10%)
  between operations  14.5 us (5%)
    psum x1, waiting for transfers between devices, local(): lax.psum((weight_local, lag_terms), ('tm', 'span'))  49.6 us
    unnamed x2, other arithmetic  47.8 us
    psum x1, blocking collectives, local(): lax.psum((weight_local, lag_terms), ('tm', 'span'))  41.3 us
    unnamed x31, local copies, waits for them, and re-layouts  19.9 us
    dot_general x9, matrix products, local(): jnp.einsum('oi,tisw->tosw', spatial_weight[row_off, col_off], slab, prefe...  14.9 us
    dot_general x9, matrix products, local(): jnp.einsum('oi,tosw->tisw', spatial_weight[row_off, col_off], dslab, pref...  14.5 us
    all_to_all x1, waiting for transfers between devices, local(): lax.all_to_all(flat_cot, 'tm', split_axis=2, concat_axis=0, tiled=True)  9.15 us
    all_to_all x1, waiting for transfers between devices, local(): lax.all_to_all(jnp.einsum('cts,tcn->scn', toe, tile_cot, preferred_elemen...  8.9 us
  transfers between devices with their start and end apart: 9, of which 4 were waited for; matrix products, arithmetic and copies ran while one was open for 37% of the time, Pallas kernels for 0%

commit v1 on v0

v1 whole, which is shorter than its diff:
```python
import functools

import jax
import jax.numpy as jnp
from jax import lax
from jax.experimental import pallas as pl
from jax.experimental.pallas import tpu as pltpu
from jax.sharding import PartitionSpec as P

F32 = jnp.float32
BF16 = jnp.bfloat16
VMEM_LIMIT = 40 * 1024 * 1024


def call(body, out, scratch, flops, nbytes):
    return pl.pallas_call(
        body,
        out_shape=out,
        scratch_shapes=scratch,
        compiler_params=pltpu.CompilerParams(vmem_limit_bytes=VMEM_LIMIT),
        cost_estimate=pl.CostEstimate(flops=flops, bytes_accessed=nbytes, transcendentals=0),
    )


def shifted(x, back):
    width = x.shape[-1]
    lane = lax.broadcasted_iota(jnp.int32, x.shape, x.ndim - 1)
    wide = x.astype(F32)
    if back:
        moved = jnp.where(lane == 0, 0.0, pltpu.roll(wide, 1, x.ndim - 1))
    else:
        moved = jnp.where(lane == width - 1, 0.0, pltpu.roll(wide, width - 1, x.ndim - 1))
    return moved.astype(x.dtype)


def fill_padded(pad_ref, before_ref, x_ref, after_ref):
    rows = x_ref.shape[0]
    pad_ref[0] = before_ref[...]
    pad_ref[pl.ds(1, rows)] = x_ref[...]
    pad_ref[rows + 1] = after_ref[...]


def conv_partials(pad_ref, weight_ref, part_ref, flip):
    weight = weight_ref[...]

    def two(step, carry):
        rows = []
        for k in range(2):
            x = pad_ref[2 * step + k]
            rows.append(jnp.concatenate([shifted(x, not flip), x, shifted(x, flip)], axis=0))
        both = jnp.concatenate(rows, axis=1)
        got = jnp.dot(weight, both, preferred_element_type=F32)
        width = got.shape[1] // 2
        part_ref[2 * step] = got[:, :width]
        part_ref[2 * step + 1] = got[:, width:]
        return carry

    lax.fori_loop(0, pad_ref.shape[0] // 2, two, 0, unroll=True)


def forward_body(before_ref, x_ref, after_ref, weight_ref, active_ref, slope_ref, pad_ref, part_ref):
    rows, channels, width = x_ref.shape
    fill_padded(pad_ref, before_ref, x_ref, after_ref)
    conv_partials(pad_ref, weight_ref, part_ref, False)

    def one(row, carry):
        hidden = (
            part_ref[row, :channels]
            + part_ref[row + 1, channels : 2 * channels]
            + part_ref[row + 2, 2 * channels :]
        )
        sigma = 1.0 / (1.0 + jnp.exp(-hidden))
        active_ref[row] = (hidden * sigma).astype(BF16)
        slope_ref[row] = sigma * (1.0 + hidden * (1.0 - sigma))
        return carry

    lax.fori_loop(0, rows, one, 0, unroll=4)


def input_grad_body(before_ref, d_ref, after_ref, weight_ref, cot_ref, out_ref, pad_ref, part_ref):
    rows, channels, width = d_ref.shape
    fill_padded(pad_ref, before_ref, d_ref, after_ref)
    conv_partials(pad_ref, weight_ref, part_ref, True)

    def one(row, carry):
        total = (
            part_ref[row + 2, :channels]
            + part_ref[row + 1, channels : 2 * channels]
            + part_ref[row, 2 * channels :]
        )
        out_ref[row] = (cot_ref[row].astype(F32) + total).astype(BF16)
        return carry

    lax.fori_loop(0, rows, one, 0, unroll=4)


def chunk_place(index, channels):
    per_row = channels // 16
    start = pl.multiple_of((index % per_row) * 16, 16)
    return index // per_row, pl.ds(start, 16)


def back_body(cot_ref, coef_ref, back_ref):
    frames, tile_rows, channels, width = cot_ref.shape

    def one(index, carry):
        row, chans = chunk_place(index, channels)
        cot = [cot_ref[t, row, chans].astype(F32) for t in range(frames)]
        coef = [coef_ref[l, chans] for l in range(frames)]
        for r in range(frames):
            total = coef[0] * cot[r]
            for t in range(r + 1, frames):
                total = total + coef[t - r] * cot[t]
            back_ref[r, row, chans] = total.astype(BF16)
        return carry

    lax.fori_loop(0, tile_rows * (channels // 16), one, 0)


def along_body(act_ref, cot_ref, coef_ref, along_ref, grad_ref, sum_ref):
    frames, tile_rows, channels, width = cot_ref.shape
    sum_ref[...] = jnp.zeros_like(sum_ref)

    def one(index, carry):
        row, chans = chunk_place(index, channels)
        act = [act_ref[t, row, chans].astype(F32) for t in range(frames)]
        coef = [coef_ref[l, chans] for l in range(frames)]
        for t in range(frames):
            total = coef[0] * act[t]
            for r in range(t):
                total = total + coef[t - r] * act[r]
            along_ref[t, row, chans] = total.astype(BF16)
        cot = [cot_ref[t, row, chans].astype(F32) for t in range(frames)]
        for lag in range(frames):
            total = cot[lag] * act[0]
            for t in range(lag + 1, frames):
                total = total + cot[t] * act[t - lag]
            sum_ref[lag, chans] += total
        return carry

    lax.fori_loop(0, tile_rows * (channels // 16), one, 0)
    grad_ref[...] = jnp.sum(sum_ref[...], axis=2)


def weight_grad_body(
    back_ref, slope_ref, before_ref, x_ref, after_ref, dhid_ref, grad_ref, pad_ref, dpad_ref
):
    rows, channels, width = x_ref.shape
    fill_padded(pad_ref, before_ref, x_ref, after_ref)
    zero = jnp.zeros((2, channels, width), BF16)
    dpad_ref[pl.ds(0, 2)] = zero
    dpad_ref[pl.ds(rows + 2, 2)] = zero

    def one(row, carry):
        value = (back_ref[row].astype(F32) * slope_ref[row]).astype(BF16)
        dhid_ref[row] = value
        dpad_ref[row + 2] = value
        return carry

    lax.fori_loop(0, rows, one, 0, unroll=4)
    grad_ref[...] = jnp.zeros_like(grad_ref)

    def two(step, carry):
        left, right = [], []
        for k in range(2):
            row = 2 * step + k
            x = pad_ref[row]
            right.append(jnp.concatenate([shifted(x, True), x, shifted(x, False)], axis=0))
            left.append(jnp.concatenate([dpad_ref[row + 2], dpad_ref[row + 1], dpad_ref[row]], axis=0))
        grad_ref[...] += lax.dot_general(
            jnp.concatenate(left, axis=1),
            jnp.concatenate(right, axis=1),
            (((1,), (1,)), ((), ())),
            preferred_element_type=F32,
        )
        return carry

    lax.fori_loop(0, (rows + 2) // 2, two, 0, unroll=True)


def edges(x):
    size = lax.axis_size("span")
    up = [(i, (i + 1) % size) for i in range(size - 1)]
    down = [(j, i) for i, j in up]
    return lax.ppermute(x[-1], "span", up), lax.ppermute(x[0], "span", down)


def tree_sum(parts):
    while len(parts) > 1:
        parts = [parts[i] + parts[i + 1] for i in range(0, len(parts), 2)]
    return parts[0]


def xor_sum(x, axis, steps):
    size = lax.axis_size(axis)
    return tree_sum([x] + [lax.ppermute(x, axis, [(i, i ^ k) for i in range(size)]) for k in steps[1:]])


def total_over_all(x):
    size = lax.axis_size("span")
    count = lax.axis_size("tm")
    rows = x.shape[0]
    half = -(-rows // 16) * 8
    x = jnp.pad(x, ((0, 2 * half - rows), (0, 0)))
    low = lax.axis_index("span") % 2 == 0
    swap = [(i, i ^ 1) for i in range(size)]
    mine = jnp.where(low, x[:half], x[half:])
    other = jnp.where(low, x[half:], x[:half])
    mine = mine + lax.ppermute(other, "span", swap)
    if size > 2:
        mine = xor_sum(mine, "span", list(range(0, size, 2)))
    plane = min(4, count)
    mine = xor_sum(mine, "tm", list(range(plane)))
    if count > plane:
        mine = xor_sum(mine, "tm", list(range(0, count, plane)))
    other = lax.ppermute(mine, "span", swap)
    first = jnp.where(low, mine, other)
    second = jnp.where(low, other, mine)
    return jnp.concatenate([first, second], axis=0)[:rows]


def local(frames, cotangent, spatial_weight, temporal_kernel):
    channels, rows, width = frames.shape[1:]
    count = lax.axis_size("tm")
    gscale = float(count * rows * lax.axis_size("span") * width) ** (-0.5)
    share = rows // count
    shape = (rows, channels, width)
    tile = (count, share, channels, width)
    area = rows * width
    act_bytes = channels * area * 2

    def exchange(x):
        return lax.all_to_all(x.reshape(tile), "tm", split_axis=0, concat_axis=0, tiled=True)

    cot = cotangent[0].transpose(1, 0, 2)
    cot_tile = exchange(cot)
    x = frames[0].transpose(1, 0, 2)
    x_before, x_after = edges(x)
    weight = spatial_weight.transpose(0, 2, 1, 3).reshape(3 * channels, 3 * channels)
    weight_back = spatial_weight.transpose(0, 3, 1, 2).reshape(3 * channels, 3 * channels)
    coef = jnp.broadcast_to(temporal_kernel.T.astype(F32)[:, :, None], (count, channels, width))
    pad = pltpu.VMEM((rows + 2, channels, width), BF16)
    part = pltpu.VMEM((rows + 2, 3 * channels, width), F32)
    flops = 18 * channels * channels * area
    active, slope = call(
        forward_body,
        (jax.ShapeDtypeStruct(shape, BF16), jax.ShapeDtypeStruct(shape, F32)),
        [pad, part],
        flops,
        4 * act_bytes,
    )(x_before, x, x_after, weight)
    back = call(back_body, jax.ShapeDtypeStruct(tile, BF16), [], 17 * channels * area, 2 * act_bytes)(
        cot_tile, coef
    )
    back = exchange(back).reshape(shape)
    act_tile = exchange(active)
    along, kernel_local = call(
        along_body,
        (jax.ShapeDtypeStruct(tile, BF16), jax.ShapeDtypeStruct((count, channels), F32)),
        [pltpu.VMEM((count, channels, width), F32)],
        34 * channels * area,
        3 * act_bytes,
    )(act_tile, cot_tile, coef)
    along = exchange(along).reshape(shape)
    dhidden, weight_local = call(
        weight_grad_body,
        (
            jax.ShapeDtypeStruct(shape, BF16),
            jax.ShapeDtypeStruct((3 * channels, 3 * channels), F32),
        ),
        [pad, pltpu.VMEM((rows + 4, channels, width), BF16)],
        flops,
        5 * act_bytes,
    )(back, slope, x_before, x, x_after)
    d_before, d_after = edges(dhidden)
    input_grad = call(
        input_grad_body, jax.ShapeDtypeStruct(shape, BF16), [pad, part], flops, 4 * act_bytes
    )(d_before, dhidden, d_after, weight_back, cot)
    block_output = (x.astype(F32) + along.astype(F32)).astype(BF16)
    sums = jnp.concatenate([weight_local.reshape(-1), kernel_local.reshape(-1)])
    total = total_over_all(sums.reshape(-1, 128)).reshape(-1) * gscale
    weights = 9 * channels * channels
    weight_total = total[:weights].reshape(3, channels, 3, channels).transpose(0, 2, 1, 3)
    kernel_total = total[weights:].reshape(count, channels).T
    return (
        block_output.transpose(1, 0, 2)[None],
        input_grad.transpose(1, 0, 2)[None],
        weight_total,
        kernel_total,
    )


def solution(mesh):
    placed = (P("tm", None, "span", None), P("tm", None, "span", None), P(), P())
    return jax.shard_map(
        local,
        mesh=mesh,
        in_specs=placed,
        out_specs=(P("tm", None, "span", None), P("tm", None, "span", None), P(), P()),
        check_vma=False,
    )
```

time: 294 us -> 97.9 us (0.33)
  other arithmetic: 54.6 us -> 0.38 us
  blocking collectives: 41.3 us -> 0 us
  local copies, waits for them, and re-layouts: 46.7 us -> 10.1 us
  matrix products: 33 us -> 0 us
  waiting for transfers between devices: 72.6 us -> 43.5 us
  between operations: 14.5 us -> 0.94 us
  Pallas kernels: 0 us -> 8.36 us
  starting transfers between devices: 29.1 us -> 33.8 us
    psum x1 -> x0, waiting for transfers between devices: 49.6 us -> none  [local(): lax.psum((weight_local, lag_terms), ('tm', 'span'))]
    unnamed x2 -> x0, other arithmetic: 47.8 us -> none
    psum x1 -> x0, blocking collectives: 41.3 us -> none  [local(): lax.psum((weight_local, lag_terms), ('tm', 'span'))]
    dot_general x30 -> x0, matrix products: 33 us -> none  [the longest x9 14.9 us: local(): jnp.einsum('oi,tisw->tosw', spatial_weight[row_off, col_off], slab, prefe...]
    unnamed x31 -> x17, local copies, waits for them, and re-layouts: 19.9 us -> 8.1 us
    ppermute x4 -> x12, waiting for transfers between devices: 0.01 us -> 11.1 us  [the longest x6 9.63 us: xor_sum(): lax.ppermute(x, axis, [(i, i ^ k) for i in range(size)])]
    reshape x6 -> x5, local copies, waits for them, and re-layouts: 11.3 us -> 0.69 us  [the longest x2 0.19 us: local(): sums = jnp.concatenate([weight_local.reshape(-1), kernel_local.reshape(-1)])]
    all_to_all x4, waiting for transfers between devices: 22.9 us -> 32.4 us  [exchange(): lax.all_to_all(x.reshape(tile), 'tm', split_axis=0, concat_axis=0, tiled=...]
  transfers between devices with their start and end apart: 9 -> 16, of which waited for: 4 -> 6; matrix products, arithmetic and copies ran while one was open for 37% -> 4% of each run, Pallas kernels for 0% -> 8%
where the time goes in v1:
time: 97.9 us; the launch traced here: 97.1 us
  waiting for transfers between devices  43.5 us (44%)
  starting transfers between devices  33.8 us (35%)
  local copies, waits for them, and re-layouts  10.1 us (10%)
  Pallas kernels  8.36 us (9%)
    all_to_all x4, waiting for transfers between devices, exchange(): lax.all_to_all(x.reshape(tile), 'tm', split_axis=0, concat_axis=0, tiled=...  32.4 us
    all_to_all x4, starting transfers between devices, exchange(): lax.all_to_all(x.reshape(tile), 'tm', split_axis=0, concat_axis=0, tiled=...  20.2 us
    ppermute x6, waiting for transfers between devices, xor_sum(): lax.ppermute(x, axis, [(i, i ^ k) for i in range(size)])  9.63 us
    ppermute x6, starting transfers between devices, xor_sum(): lax.ppermute(x, axis, [(i, i ^ k) for i in range(size)])  8.15 us
    unnamed x17, local copies, waits for them, and re-layouts  8.1 us
    ppermute x4, starting transfers between devices, edges(): return (lax.ppermute(x[-1], 'span', up), lax.ppermute(x[0], 'span', down))  5.32 us
    pallas_call x1, Pallas kernels, local(): call(forward_body, (jax.ShapeDtypeStruct(shape, BF16), jax.ShapeDtypeStru...  2.02 us
  transfers between devices with their start and end apart: 16, of which 6 were waited for; matrix products, arithmetic and copies ran while one was open for 4% of the time, Pallas kernels for 8%

profile of v1, /device:TPU:0, one launch (start us, length us, event | category | flops | bytes accessed | tf_op | source)
XLA Modules:
  0.0 97.1 jit_solution(740295905714236894)
XLA Ops:
  0.6 2.0 %copy.27 = bf16[1,64,32,128]{3,1,2,0:T(8,128)(2,1)} copy(bf16[1,64,32,128]{3,2,1,0:T(8,128)(2,1)} %param.5) | data formatting | bytes 1048576 | tf_op args[1]
  2.7 0.0 copy-start.2
  2.7 8.4 %all-to-all-start.1 = ((bf16[16,2,64,128]{3,2,1,0:T(8,128)(2,1)}), bf16[16,2,64,128]{3,2,1,0:T(8,128)(2,1)S(1)}, u32[]{:S(2)}, u32[]{:S(2)}) async-start(bf16[16,2,64,128]{3,2,1,0:T(8,128)(2,1)} %bitcast.9), calls=%async_computation.1 | async-start | bytes 1048576 | tf_op jit(solution)/shard_map/all_to_all | solution.py:233
  11.1 0.0 copy-done.2
  11.1 0.0 copy-start.4
  11.2 0.2 copy.26
  11.4 1.5 %collective-permute-start = (bf16[64,128]{1,0:T(8,128)(2,1)S(1)}, bf16[64,128]{1,0:T(8,128)(2,1)S(1)}, u32[]{:S(2)}, u32[]{:S(2)}) collective-permute-start(bf16[64,128]{1,0:T(8,128)(2,1)S(1)} %get-tuple-element.29), channel_id=1, source_target_pairs={{0,1},{2,3},{4,5},{6,7},{8,9},{10,11},{12,13},{14,15},{16,17},{18,... | collective-permute-start | bytes 49160 | tf_op jit(solution)/shard_map/ppermute | solution.py:185
  12.8 1.3 %collective-permute-start.1 = (bf16[64,128]{1,0:T(8,128)(2,1)S(1)}, bf16[64,128]{1,0:T(8,128)(2,1)S(1)}, u32[]{:S(2)}, u32[]{:S(2)}) collective-permute-start(bf16[64,128]{1,0:T(8,128)(2,1)S(1)} %get-tuple-element.28), channel_id=1, source_target_pairs={{1,0},{3,2},{5,4},{7,6},{9,8},{11,10},{13,12},{15,14},{17,16},{19,... | collective-permute-start | bytes 49160 | tf_op jit(solution)/shard_map/ppermute | solution.py:185
  14.1 0.0 copy-done.4
  14.2 0.1 copy.15
  14.3 0.2 reshape.55.weight_ref
  14.5 0.0 collective-permute-done.before_ref
  14.5 1.5 %collective-permute-done.1.after_ref = bf16[64,128]{1,0:T(8,128)(2,1)S(1)} collective-permute-done((bf16[64,128]{1,0:T(8,128)(2,1)S(1)}, bf16[64,128]{1,0:T(8,128)(2,1)S(1)}, u32[]{:S(2)}, u32[]{:S(2)}) %collective-permute-start.1) | collective-permute-done | bytes 16416 | tf_op jit(solution)/shard_map/ppermute | solution.py:185
  15.9 2.0 %shard_map.75 = (bf16[32,64,128]{2,1,0:T(8,128)(2,1)}, f32[32,64,128]{2,1,0:T(8,128)S(1)}) custom-call(bf16[64,128]{1,0:T(8,128)(2,1)S(1)} %collective-permute-done.before_ref, bf16[32,64,128]{2,1,0:T(8,128)(2,1)S(1)} %bitcast.43, bf16[64,128]{1,0:T(8,128)(2,1)S(1)} %collective-permute-done.1.after_ref, bf16[192,192]{1,0:T(8,128)(2,1)S(1)} %reshape.55.weight_ref), custom_call_target="tpu_custom_call" | custom-call | flops 301989888 | bytes 2097152 | tf_op jit(solution)/shard_map/pallas_call | solution.py:245
  18.0 1.0 %copy-done = f32[32,64,128]{2,1,0:T(8,128)} copy-done((f32[32,64,128]{2,1,0:T(8,128)}, f32[32,64,128]{2,1,0:T(8,128)S(1)}, u32[]{:S(2)}) %copy-start) | copy-done | bytes 1048600
  18.9 7.3 %all-to-all-done.1.cot_ref = bf16[16,2,64,128]{3,2,1,0:T(8,128)(2,1)S(1)} async-done(((bf16[16,2,64,128]{3,2,1,0:T(8,128)(2,1)}), bf16[16,2,64,128]{3,2,1,0:T(8,128)(2,1)S(1)}, u32[]{:S(2)}, u32[]{:S(2)}) %all-to-all-start.1) | async-done | bytes 524320 | tf_op jit(solution)/shard_map/all_to_all | solution.py:233
  26.3 4.0 %all-to-all-start = ((bf16[16,2,64,128]{3,2,1,0:T(8,128)(2,1)}), bf16[16,2,64,128]{3,2,1,0:T(8,128)(2,1)S(1)}, u32[]{:S(2)}, u32[]{:S(2)}) async-start(bf16[16,2,64,128]{3,2,1,0:T(8,128)(2,1)} %bitcast.6), calls=%async_computation | async-start | bytes 1048576 | tf_op jit(solution)/shard_map/all_to_all | solution.py:233
  30.3 0.0 copy-done.5
  30.3 0.2 broadcast_in_dim.12.coef_ref
  30.5 1.5 %shard_map.77 = bf16[16,2,64,128]{3,2,1,0:T(8,128)(2,1)} custom-call(bf16[16,2,64,128]{3,2,1,0:T(8,128)(2,1)S(1)} %all-to-all-done.1.cot_ref, f32[16,64,128]{2,1,0:T(8,128)S(1)} %broadcast_in_dim.12.coef_ref), custom_call_target="tpu_custom_call" | custom-call | flops 4456448 | bytes 1048576 | tf_op jit(solution)/shard_map/pallas_call | solution.py:252
  32.0 12.7 %all-to-all-done.act_ref = bf16[16,2,64,128]{3,2,1,0:T(8,128)(2,1)S(1)} async-done(((bf16[16,2,64,128]{3,2,1,0:T(8,128)(2,1)}), bf16[16,2,64,128]{3,2,1,0:T(8,128)(2,1)S(1)}, u32[]{:S(2)}, u32[]{:S(2)}) %all-to-all-start) | async-done | bytes 524320 | tf_op jit(solution)/shard_map/all_to_all | solution.py:233
  44.7 3.8 %all-to-all-start.3 = ((bf16[16,2,64,128]{3,2,1,0:T(8,128)(2,1)}), bf16[16,2,64,128]{3,2,1,0:T(8,128)(2,1)S(1)}, u32[]{:S(2)}, u32[]{:S(2)}) async-start(bf16[16,2,64,128]{3,2,1,0:T(8,128)(2,1)} %shard_map.77), calls=%async_computation.3 | async-start | bytes 1048576 | tf_op jit(solution)/shard_map/all_to_all | solution.py:233
  48.6 1.9 %shard_map.76 = (bf16[16,2,64,128]{3,2,1,0:T(8,128)(2,1)}, f32[16,64]{1,0:T(8,128)S(1)}) custom-call(bf16[16,2,64,128]{3,2,1,0:T(8,128)(2,1)S(1)} %all-to-all-done.act_ref, bf16[16,2,64,128]{3,2,1,0:T(8,128)(2,1)S(1)} %all-to-all-done.1.cot_ref, f32[16,64,128]{2,1,0:T(8,128)S(1)} %broadcast_in_dim.12.coef_ref), custom_call_target="tpu_custom_call" | custom-call | flops 8912896 | bytes 1572864 | tf_op jit(solution)/shard_map/pallas_call | solution.py:257
  50.4 0.1 reshape.61
  50.5 12.4 %all-to-all-done.3 = bf16[16,2,64,128]{3,2,1,0:T(8,128)(2,1)S(1)} async-done(((bf16[16,2,64,128]{3,2,1,0:T(8,128)(2,1)}), bf16[16,2,64,128]{3,2,1,0:T(8,128)(2,1)S(1)}, u32[]{:S(2)}, u32[]{:S(2)}) %all-to-all-start.3) | async-done | bytes 524320 | tf_op jit(solution)/shard_map/all_to_all | solution.py:233
  62.9 1.2 %copy-done.1 = f32[32,64,128]{2,1,0:T(8,128)S(1)} copy-done((f32[32,64,128]{2,1,0:T(8,128)S(1)}, f32[32,64,128]{2,1,0:T(8,128)}, u32[]{:S(2)}) %copy-start.1) | copy-done | bytes 1048600
  64.1 1.0 %shard_map.78 = (bf16[32,64,128]{2,1,0:T(8,128)(2,1)S(1)}, f32[192,192]{1,0:T(8,128)S(1)}) custom-call(bf16[32,64,128]{2,1,0:T(8,128)(2,1)S(1)} %bitcast.46, f32[32,64,128]{2,1,0:T(8,128)S(1)} %copy-done.1, bf16[64,128]{1,0:T(8,128)(2,1)S(1)} %collective-permute-done.before_ref, bf16[32,64,128]{2,1,0:T(8,128)(2,1)S(1)} %bitcast.44, ...), custom_call_target="tpu_custom_call" | custom-call | flops 301989888 | bytes 2621440 | tf_op jit(solution)/shard_map/pallas_call | solution.py:265
  65.1 0.1 slice.46
  65.3 0.1 reshape.60
  65.4 0.1 collective-permute-start.4
  65.5 3.9 %all-to-all-start.2 = ((bf16[16,2,64,128]{3,2,1,0:T(8,128)(2,1)}), bf16[16,2,64,128]{3,2,1,0:T(8,128)(2,1)S(1)}, u32[]{:S(2)}, u32[]{:S(2)}) async-start(bf16[16,2,64,128]{3,2,1,0:T(8,128)(2,1)} %get-tuple-element.11), calls=%async_computation.2 | async-start | bytes 1048576 | tf_op jit(solution)/shard_map/all_to_all | solution.py:233
  69.4 0.0 collective-permute-done.4
  69.4 2.0 %collective-permute-start.6 = (f32[152,128]{1,0:T(8,128)S(1)}, f32[152,128]{1,0:T(8,128)S(1)}, u32[]{:S(2)}, u32[]{:S(2)}) collective-permute-start(f32[152,128]{1,0:T(8,128)S(1)} %select_add_fusion), channel_id=1, source_target_pairs={{0,4},{2,6},{4,0},{6,2},{8,12},{10,14},{12,8},{14,10},{16,20},{18,... | collective-permute-start | bytes 233480 | tf_op jit(solution)/shard_map/ppermute | solution.py:196
  71.4 1.5 %collective-permute-start.7 = (f32[152,128]{1,0:T(8,128)S(1)}, f32[152,128]{1,0:T(8,128)S(1)}, u32[]{:S(2)}, u32[]{:S(2)}) collective-permute-start(f32[152,128]{1,0:T(8,128)S(1)} %select_add_fusion), channel_id=1, source_target_pairs={{0,6},{2,4},{4,2},{6,0},{8,14},{10,12},{12,10},{14,8},{16,22},{18,... | collective-permute-start | bytes 233480 | tf_op jit(solution)/shard_map/ppermute | solution.py:196
  72.8 0.1 collective-permute-start.5
  73.0 0.2 copy.17
  73.1 0.2 reshape.59.weight_ref
  73.3 6.2 %collective-permute-done.6 = f32[152,128]{1,0:T(8,128)S(1)} collective-permute-done((f32[152,128]{1,0:T(8,128)S(1)}, f32[152,128]{1,0:T(8,128)S(1)}, u32[]{:S(2)}, u32[]{:S(2)}) %collective-permute-start.6) | collective-permute-done | bytes 77856 | tf_op jit(solution)/shard_map/ppermute | solution.py:196
  79.5 0.0 collective-permute-done.7
  79.5 0.0 collective-permute-done.5
  79.5 2.1 %collective-permute-start.9 = (f32[152,128]{1,0:T(8,128)S(1)}, f32[152,128]{1,0:T(8,128)S(1)}, u32[]{:S(2)}, u32[]{:S(2)}) collective-permute-start(f32[152,128]{1,0:T(8,128)S(1)} %add_add_fusion.1), channel_id=1, source_target_pairs={{0,16},{2,18},{4,20},{6,22},{8,24},{10,26},{12,28},{14,30},{16,0},... | collective-permute-start | bytes 233480 | tf_op jit(solution)/shard_map/ppermute | solution.py:196
  81.6 2.0 %collective-permute-start.10 = (f32[152,128]{1,0:T(8,128)S(1)}, f32[152,128]{1,0:T(8,128)S(1)}, u32[]{:S(2)}, u32[]{:S(2)}) collective-permute-start(f32[152,128]{1,0:T(8,128)S(1)} %add_add_fusion.1), channel_id=1, source_target_pairs={{0,24},{2,26},{4,28},{6,30},{8,16},{10,18},{12,20},{14,22},{16,8},... | collective-permute-start | bytes 233480 | tf_op jit(solution)/shard_map/ppermute | solution.py:196
  83.6 0.5 collective-permute-start.8
  84.1 1.3 %collective-permute-start.2 = (bf16[64,128]{1,0:T(8,128)(2,1)S(1)}, bf16[64,128]{1,0:T(8,128)(2,1)S(1)}, u32[]{:S(2)}, u32[]{:S(2)}) collective-permute-start(bf16[64,128]{1,0:T(8,128)(2,1)S(1)} %get-tuple-element.27), channel_id=1, source_target_pairs={{0,1},{2,3},{4,5},{6,7},{8,9},{10,11},{12,13},{14,15},{16,17},{18,... | collective-permute-start | bytes 49160 | tf_op jit(solution)/shard_map/ppermute | solution.py:185
  85.4 1.3 %collective-permute-start.3 = (bf16[64,128]{1,0:T(8,128)(2,1)S(1)}, bf16[64,128]{1,0:T(8,128)(2,1)S(1)}, u32[]{:S(2)}, u32[]{:S(2)}) collective-permute-start(bf16[64,128]{1,0:T(8,128)(2,1)S(1)} %get-tuple-element.26), channel_id=1, source_target_pairs={{1,0},{3,2},{5,4},{7,6},{9,8},{11,10},{13,12},{15,14},{17,16},{19,... | collective-permute-start | bytes 49160 | tf_op jit(solution)/shard_map/ppermute | solution.py:185
  86.7 3.4 %collective-permute-done.9 = f32[152,128]{1,0:T(8,128)S(1)} collective-permute-done((f32[152,128]{1,0:T(8,128)S(1)}, f32[152,128]{1,0:T(8,128)S(1)}, u32[]{:S(2)}, u32[]{:S(2)}) %collective-permute-start.9) | collective-permute-done | bytes 77856 | tf_op jit(solution)/shard_map/ppermute | solution.py:196
  90.1 0.0 collective-permute-done.10
  90.1 0.0 collective-permute-done.8
  90.2 0.1 collective-permute-start.11
  90.2 0.0 all-to-all-done.2
  90.3 0.3 fusion.1
  90.5 1.1 %copy.18 = bf16[1,64,32,128]{3,2,1,0:T(8,128)(2,1)} copy(bf16[1,64,32,128]{3,1,2,0:T(8,128)(2,1)S(1)} %fusion.1) | data formatting | bytes 1048576
  91.7 0.0 collective-permute-done.2.before_ref
  91.7 0.0 collective-permute-done.3.after_ref
  91.7 2.0 %shard_map.79 = bf16[32,64,128]{2,1,0:T(8,128)(2,1)S(1)} custom-call(bf16[64,128]{1,0:T(8,128)(2,1)S(1)} %collective-permute-done.2.before_ref, bf16[32,64,128]{2,1,0:T(8,128)(2,1)S(1)} %get-tuple-element.13.d_ref, bf16[64,128]{1,0:T(8,128)(2,1)S(1)} %collective-permute-done.3.after_ref, bf16[192,192]{1,0:T(8,128)(2,1)S(1)} %reshape.59.weight_ref, ...), custom_call_target="tpu_custom_call" | custom-call | flops 301989888 | bytes 2097152 | tf_op jit(solution)/shard_map/pallas_call | solution.py:276
  93.6 1.1 %copy.19 = bf16[1,64,32,128]{3,2,1,0:T(8,128)(2,1)} copy(bf16[1,64,32,128]{3,1,2,0:T(8,128)(2,1)S(1)} %bitcast.45) | data formatting | bytes 1048576
  94.8 0.0 collective-permute-done.11
  94.8 0.0 copy-start.3
  94.8 0.6 copy-done.3
  95.5 0.2 reshape.63
  95.7 0.0 slice-start
  95.7 0.7 copy.20
  96.4 0.0 slice-done
  96.4 0.7 slice.52
  (14 shorter events, 0.1 us)
Async XLA Ops:
  2.7 8.5 %copy-start.2 = (bf16[1,64,32,128]{3,2,1,0:T(8,128)(2,1)S(1)}, bf16[1,64,32,128]{3,2,1,0:T(8,128)(2,1)}, u32[]{:S(2)}) copy-start(bf16[1,64,32,128]{3,2,1,0:T(8,128)(2,1)} %param.4) | copy-start | bytes 1572868
  2.7 23.6 %all-to-all-start.1 = ((bf16[16,2,64,128]{3,2,1,0:T(8,128)(2,1)}), bf16[16,2,64,128]{3,2,1,0:T(8,128)(2,1)S(1)}, u32[]{:S(2)}, u32[]{:S(2)}) async-start(bf16[16,2,64,128]{3,2,1,0:T(8,128)(2,1)} %bitcast.9), calls=%async_computation.1 | async-start | bytes 1048576 | tf_op jit(solution)/shard_map/all_to_all | solution.py:233
  11.1 3.0 %copy-start.4 = (bf16[3,3,64,64]{3,2,1,0:T(8,128)(2,1)S(1)}, bf16[3,3,64,64]{3,2,1,0:T(8,128)(2,1)}, u32[]{:S(2)}) copy-start(bf16[3,3,64,64]{3,2,1,0:T(8,128)(2,1)} %param.6) | copy-start | bytes 221188
  11.4 3.1 %collective-permute-start = (bf16[64,128]{1,0:T(8,128)(2,1)S(1)}, bf16[64,128]{1,0:T(8,128)(2,1)S(1)}, u32[]{:S(2)}, u32[]{:S(2)}) collective-permute-start(bf16[64,128]{1,0:T(8,128)(2,1)S(1)} %get-tuple-element.29), channel_id=1, source_target_pairs={{0,1},{2,3},{4,5},{6,7},{8,9},{10,11},{12,13},{14,15},{16,17},{18,... | collective-permute-start | bytes 49160 | tf_op jit(solution)/shard_map/ppermute | solution.py:185
  12.8 3.1 %collective-permute-start.1 = (bf16[64,128]{1,0:T(8,128)(2,1)S(1)}, bf16[64,128]{1,0:T(8,128)(2,1)S(1)}, u32[]{:S(2)}, u32[]{:S(2)}) collective-permute-start(bf16[64,128]{1,0:T(8,128)(2,1)S(1)} %get-tuple-element.28), channel_id=1, source_target_pairs={{1,0},{3,2},{5,4},{7,6},{9,8},{11,10},{13,12},{15,14},{17,16},{19,... | collective-permute-start | bytes 49160 | tf_op jit(solution)/shard_map/ppermute | solution.py:185
  18.0 1.0 %copy-start = (f32[32,64,128]{2,1,0:T(8,128)}, f32[32,64,128]{2,1,0:T(8,128)S(1)}, u32[]{:S(2)}) copy-start(f32[32,64,128]{2,1,0:T(8,128)S(1)} %get-tuple-element.12.slope_ref) | copy-start | bytes 3145732
  26.3 4.0 %copy-start.5 = (bf16[64,16]{0,1:T(8,128)(2,1)S(1)}, bf16[64,16]{0,1:T(8,128)(2,1)}, u32[]{:S(2)}) copy-start(bf16[64,16]{0,1:T(8,128)(2,1)} %param.7) | copy-start | bytes 6148
  26.3 18.4 %all-to-all-start = ((bf16[16,2,64,128]{3,2,1,0:T(8,128)(2,1)}), bf16[16,2,64,128]{3,2,1,0:T(8,128)(2,1)S(1)}, u32[]{:S(2)}, u32[]{:S(2)}) async-start(bf16[16,2,64,128]{3,2,1,0:T(8,128)(2,1)} %bitcast.6), calls=%async_computation | async-start | bytes 1048576 | tf_op jit(solution)/shard_map/all_to_all | solution.py:233
  44.7 18.2 %all-to-all-start.3 = ((bf16[16,2,64,128]{3,2,1,0:T(8,128)(2,1)}), bf16[16,2,64,128]{3,2,1,0:T(8,128)(2,1)S(1)}, u32[]{:S(2)}, u32[]{:S(2)}) async-start(bf16[16,2,64,128]{3,2,1,0:T(8,128)(2,1)} %shard_map.77), calls=%async_computation.3 | async-start | bytes 1048576 | tf_op jit(solution)/shard_map/all_to_all | solution.py:233
  62.9 1.2 %copy-start.1 = (f32[32,64,128]{2,1,0:T(8,128)S(1)}, f32[32,64,128]{2,1,0:T(8,128)}, u32[]{:S(2)}) copy-start(f32[32,64,128]{2,1,0:T(8,128)} %copy-done) | copy-start | bytes 3145732
  65.4 3.9 %collective-permute-start.4 = (f32[152,128]{1,0:T(8,128)S(1)}, f32[152,128]{1,0:T(8,128)S(1)}, u32[]{:S(2)}, u32[]{:S(2)}) collective-permute-start(f32[152,128]{1,0:T(8,128)S(1)} %slice_select_fusion), channel_id=1, source_target_pairs={{0,1},{1,0},{2,3},{3,2},{4,5},{5,4},{6,7},{7,6},{8,9},{9,8},{10,11... | collective-permute-start | bytes 233480 | tf_op jit(solution)/shard_map/ppermute | solution.py:209
  65.5 24.8 %all-to-all-start.2 = ((bf16[16,2,64,128]{3,2,1,0:T(8,128)(2,1)}), bf16[16,2,64,128]{3,2,1,0:T(8,128)(2,1)S(1)}, u32[]{:S(2)}, u32[]{:S(2)}) async-start(bf16[16,2,64,128]{3,2,1,0:T(8,128)(2,1)} %get-tuple-element.11), calls=%async_computation.2 | async-start | bytes 1048576 | tf_op jit(solution)/shard_map/all_to_all | solution.py:233
  69.4 10.1 %collective-permute-start.6 = (f32[152,128]{1,0:T(8,128)S(1)}, f32[152,128]{1,0:T(8,128)S(1)}, u32[]{:S(2)}, u32[]{:S(2)}) collective-permute-start(f32[152,128]{1,0:T(8,128)S(1)} %select_add_fusion), channel_id=1, source_target_pairs={{0,4},{2,6},{4,0},{6,2},{8,12},{10,14},{12,8},{14,10},{16,20},{18,... | collective-permute-start | bytes 233480 | tf_op jit(solution)/shard_map/ppermute | solution.py:196
  71.4 8.1 %collective-permute-start.7 = (f32[152,128]{1,0:T(8,128)S(1)}, f32[152,128]{1,0:T(8,128)S(1)}, u32[]{:S(2)}, u32[]{:S(2)}) collective-permute-start(f32[152,128]{1,0:T(8,128)S(1)} %select_add_fusion), channel_id=1, source_target_pairs={{0,6},{2,4},{4,2},{6,0},{8,14},{10,12},{12,10},{14,8},{16,22},{18,... | collective-permute-start | bytes 233480 | tf_op jit(solution)/shard_map/ppermute | solution.py:196
  72.8 6.6 %collective-permute-start.5 = (f32[152,128]{1,0:T(8,128)S(1)}, f32[152,128]{1,0:T(8,128)S(1)}, u32[]{:S(2)}, u32[]{:S(2)}) collective-permute-start(f32[152,128]{1,0:T(8,128)S(1)} %select_add_fusion), channel_id=1, source_target_pairs={{0,2},{2,0},{4,6},{6,4},{8,10},{10,8},{12,14},{14,12},{16,18},{18,... | collective-permute-start | bytes 233480 | tf_op jit(solution)/shard_map/ppermute | solution.py:196
  79.5 10.6 %collective-permute-start.9 = (f32[152,128]{1,0:T(8,128)S(1)}, f32[152,128]{1,0:T(8,128)S(1)}, u32[]{:S(2)}, u32[]{:S(2)}) collective-permute-start(f32[152,128]{1,0:T(8,128)S(1)} %add_add_fusion.1), channel_id=1, source_target_pairs={{0,16},{2,18},{4,20},{6,22},{8,24},{10,26},{12,28},{14,30},{16,0},... | collective-permute-start | bytes 233480 | tf_op jit(solution)/shard_map/ppermute | solution.py:196
  81.6 8.6 %collective-permute-start.10 = (f32[152,128]{1,0:T(8,128)S(1)}, f32[152,128]{1,0:T(8,128)S(1)}, u32[]{:S(2)}, u32[]{:S(2)}) collective-permute-start(f32[152,128]{1,0:T(8,128)S(1)} %add_add_fusion.1), channel_id=1, source_target_pairs={{0,24},{2,26},{4,28},{6,30},{8,16},{10,18},{12,20},{14,22},{16,8},... | collective-permute-start | bytes 233480 | tf_op jit(solution)/shard_map/ppermute | solution.py:196
  83.6 6.5 %collective-permute-start.8 = (f32[152,128]{1,0:T(8,128)S(1)}, f32[152,128]{1,0:T(8,128)S(1)}, u32[]{:S(2)}, u32[]{:S(2)}) collective-permute-start(f32[152,128]{1,0:T(8,128)S(1)} %add_add_fusion.1), channel_id=1, source_target_pairs={{0,8},{2,10},{4,12},{6,14},{8,0},{10,2},{12,4},{14,6},{16,24},{18,... | collective-permute-start | bytes 233480 | tf_op jit(solution)/shard_map/ppermute | solution.py:196
  84.1 7.6 %collective-permute-start.2 = (bf16[64,128]{1,0:T(8,128)(2,1)S(1)}, bf16[64,128]{1,0:T(8,128)(2,1)S(1)}, u32[]{:S(2)}, u32[]{:S(2)}) collective-permute-start(bf16[64,128]{1,0:T(8,128)(2,1)S(1)} %get-tuple-element.27), channel_id=1, source_target_pairs={{0,1},{2,3},{4,5},{6,7},{8,9},{10,11},{12,13},{14,15},{16,17},{18,... | collective-permute-start | bytes 49160 | tf_op jit(solution)/shard_map/ppermute | solution.py:185
  85.4 6.3 %collective-permute-start.3 = (bf16[64,128]{1,0:T(8,128)(2,1)S(1)}, bf16[64,128]{1,0:T(8,128)(2,1)S(1)}, u32[]{:S(2)}, u32[]{:S(2)}) collective-permute-start(bf16[64,128]{1,0:T(8,128)(2,1)S(1)} %get-tuple-element.26), channel_id=1, source_target_pairs={{1,0},{3,2},{5,4},{7,6},{9,8},{11,10},{13,12},{15,14},{17,16},{19,... | collective-permute-start | bytes 49160 | tf_op jit(solution)/shard_map/ppermute | solution.py:185
  90.2 4.6 %collective-permute-start.11 = (f32[152,128]{1,0:T(8,128)S(1)}, f32[152,128]{1,0:T(8,128)S(1)}, u32[]{:S(2)}, u32[]{:S(2)}) collective-permute-start(f32[152,128]{1,0:T(8,128)S(1)} %add_add_fusion), channel_id=1, source_target_pairs={{0,1},{1,0},{2,3},{3,2},{4,5},{5,4},{6,7},{7,6},{8,9},{9,8},{10,11... | collective-permute-start | bytes 233480 | tf_op jit(solution)/shard_map/ppermute | solution.py:216
  94.8 0.7 copy-start.3
  95.7 0.8 slice-start

commit v2 on v1

v2 whole, which is shorter than its diff:
```python
import functools

import jax
import jax.numpy as jnp
from jax import lax
from jax.experimental import pallas as pl
from jax.experimental.pallas import tpu as pltpu
from jax.sharding import PartitionSpec as P

F32 = jnp.float32
BF16 = jnp.bfloat16
VMEM_LIMIT = 16 * 1024 * 1024


def call(body, out, scratch, flops, nbytes):
    return pl.pallas_call(
        body,
        out_shape=out,
        scratch_shapes=scratch,
        compiler_params=pltpu.CompilerParams(vmem_limit_bytes=VMEM_LIMIT),
        cost_estimate=pl.CostEstimate(flops=flops, bytes_accessed=nbytes, transcendentals=0),
    )


def shifted(x, back):
    width = x.shape[-1]
    lane = lax.broadcasted_iota(jnp.int32, x.shape, x.ndim - 1)
    wide = x.astype(F32)
    if back:
        moved = jnp.where(lane == 0, 0.0, pltpu.roll(wide, 1, x.ndim - 1))
    else:
        moved = jnp.where(lane == width - 1, 0.0, pltpu.roll(wide, width - 1, x.ndim - 1))
    return moved.astype(x.dtype)


def fill_padded(pad_ref, before_ref, x, after_ref):
    rows = x.shape[0]
    pad_ref[0] = before_ref[...]
    pad_ref[pl.ds(1, rows)] = x
    pad_ref[rows + 1] = after_ref[...]


def swapped(x):
    return jnp.transpose(x, (1, 0, 2))


def conv_partials(pad_ref, weight_ref, part_ref, flip):
    weight = weight_ref[...]

    def two(step, carry):
        rows = []
        for k in range(2):
            x = pad_ref[2 * step + k]
            rows.append(jnp.concatenate([shifted(x, not flip), x, shifted(x, flip)], axis=0))
        both = jnp.concatenate(rows, axis=1)
        got = jnp.dot(weight, both, preferred_element_type=F32)
        width = got.shape[1] // 2
        part_ref[2 * step] = got[:, :width]
        part_ref[2 * step + 1] = got[:, width:]
        return carry

    lax.fori_loop(0, pad_ref.shape[0] // 2, two, 0, unroll=True)


def forward_body(
    before_ref, x_ref, after_ref, weight_ref, active_ref, slope_ref, pad_ref, part_ref, act_ref
):
    channels, rows, width = x_ref.shape
    fill_padded(pad_ref, before_ref, swapped(x_ref[...]), after_ref)
    conv_partials(pad_ref, weight_ref, part_ref, False)

    def one(row, carry):
        hidden = (
            part_ref[row, :channels]
            + part_ref[row + 1, channels : 2 * channels]
            + part_ref[row + 2, 2 * channels :]
        )
        sigma = 1.0 / (1.0 + jnp.exp(-hidden))
        act_ref[row] = (hidden * sigma).astype(BF16)
        slope_ref[row] = sigma * (1.0 + hidden * (1.0 - sigma))
        return carry

    lax.fori_loop(0, rows, one, 0, unroll=4)
    active_ref[...] = swapped(act_ref[...])


def input_grad_body(before_ref, d_ref, after_ref, weight_ref, cot_ref, out_ref, pad_ref, part_ref, sum_ref):
    rows, channels, width = d_ref.shape
    fill_padded(pad_ref, before_ref, d_ref[...], after_ref)
    conv_partials(pad_ref, weight_ref, part_ref, True)

    def one(row, carry):
        total = (
            part_ref[row + 2, :channels]
            + part_ref[row + 1, channels : 2 * channels]
            + part_ref[row, 2 * channels :]
        )
        sum_ref[row] = total
        return carry

    lax.fori_loop(0, rows, one, 0, unroll=4)
    out_ref[...] = (cot_ref[...].astype(F32) + swapped(sum_ref[...])).astype(BF16)


def chunks_of(tile_shape, body):
    group, rows = tile_shape[1:3]
    per = rows // 16

    def one(index, carry):
        body(index // per, pl.ds(pl.multiple_of((index % per) * 16, 16), 16))
        return carry

    lax.fori_loop(0, group * per, one, 0)


def back_body(coef_ref, cot_ref, back_ref):
    frames, group = cot_ref.shape[:2]

    def one(chan, some):
        cot = [cot_ref[t, chan, some].astype(F32) for t in range(frames)]
        coef = [coef_ref[chan, pl.ds(l, 1)] for l in range(frames)]
        for r in range(frames):
            total = coef[0] * cot[r]
            for t in range(r + 1, frames):
                total = total + coef[t - r] * cot[t]
            back_ref[r, chan, some] = total.astype(BF16)

    chunks_of(cot_ref.shape, one)


def along_body(coef_ref, cot_ref, act_ref, out_ref, sum_ref):
    frames, group, rows, width = cot_ref.shape
    sum_ref[...] = jnp.zeros_like(sum_ref)

    def one(chan, some):
        act = [act_ref[t, chan, some].astype(F32) for t in range(frames)]
        coef = [coef_ref[chan, pl.ds(l, 1)] for l in range(frames)]
        to = pl.ds(pl.multiple_of(chan * rows + some.start, 16), 16)
        for t in range(frames):
            total = coef[0] * act[t]
            for r in range(t):
                total = total + coef[t - r] * act[r]
            out_ref[t, to] = total.astype(BF16)
        cot = [cot_ref[t, chan, some].astype(F32) for t in range(frames)]
        for lag in range(frames):
            total = cot[lag] * act[0]
            for t in range(lag + 1, frames):
                total = total + cot[t] * act[t - lag]
            sum_ref[chan, lag] += total[:8] + total[8:]

    chunks_of(cot_ref.shape, one)
    lane = lax.broadcasted_iota(jnp.int32, (frames, width), 1)
    both = jnp.zeros((frames, width), F32)
    for chan in range(group):
        sums = jnp.sum(jnp.sum(sum_ref[chan], axis=1), axis=1, keepdims=True)
        high = sums.astype(BF16).astype(F32)
        both = jnp.where(lane == chan, high, both)
        both = jnp.where(lane == width // 2 + chan, sums - high, both)
    both = both.astype(BF16)
    for t in range(frames):
        out_ref[t, pl.ds(group * rows, frames)] = both


def block_output_body(x_ref, got_ref, out_ref):
    channels, rows, width = x_ref.shape
    owners = got_ref.shape[0]
    group = channels // owners
    for owner in range(owners):
        for chan in range(group):
            here = owner * group + chan
            along = got_ref[owner, pl.ds(chan * rows, rows)].astype(F32)
            out_ref[here] = (x_ref[here].astype(F32) + along).astype(BF16)


def kernel_sums_body(got_ref, sums_ref):
    owners = got_ref.shape[0]
    lags, channels = sums_ref.shape
    width = got_ref.shape[2]
    group = channels // owners
    lane = lax.broadcasted_iota(jnp.int32, (lags, width), 1)
    total = jnp.zeros((lags, width), F32)
    for owner in range(owners):
        part = got_ref[owner, pl.ds(got_ref.shape[1] - lags, lags)].astype(F32)
        part = part + pltpu.roll(part, width // 2, 1)
        if owner > 0:
            part = pltpu.roll(part, owner * group, 1)
        total = jnp.where(lane // group == owner, part, total)
    sums_ref[...] = total[:, :channels]


def weight_grad_body(
    side_ref, back_ref, slope_ref, pad_ref, dhid_ref, keep_ref, give_ref,
    dpad_ref, grad_ref, pack_ref, turn_ref,
):
    rows, channels, width = slope_ref.shape
    turn_ref[...] = swapped(back_ref[...])
    zero = jnp.zeros((2, channels, width), BF16)
    dpad_ref[pl.ds(0, 2)] = zero
    dpad_ref[pl.ds(rows + 2, 2)] = zero

    def one(row, carry):
        value = (turn_ref[row].astype(F32) * slope_ref[row]).astype(BF16)
        dhid_ref[row] = value
        dpad_ref[row + 2] = value
        return carry

    lax.fori_loop(0, rows, one, 0, unroll=4)
    grad_ref[...] = jnp.zeros_like(grad_ref)

    def two(step, carry):
        left, right = [], []
        for k in range(2):
            row = 2 * step + k
            x = pad_ref[row]
            right.append(jnp.concatenate([shifted(x, True), x, shifted(x, False)], axis=0))
            left.append(jnp.concatenate([dpad_ref[row + 2], dpad_ref[row + 1], dpad_ref[row]], axis=0))
        grad_ref[...] += lax.dot_general(
            jnp.concatenate(left, axis=1),
            jnp.concatenate(right, axis=1),
            (((1,), (1,)), ((), ())),
            preferred_element_type=F32,
        )
        return carry

    lax.fori_loop(0, (rows + 2) // 2, two, 0, unroll=True)
    tall = 3 * channels
    pack_ref[pl.ds(0, tall)] = grad_ref[:, : 2 * channels]
    pack_ref[pl.ds(tall, tall // 2)] = jnp.concatenate(
        [grad_ref[: tall // 2, 2 * channels :], grad_ref[tall // 2 :, 2 * channels :]], axis=1
    )
    half = keep_ref.shape[0]
    done = tall + tall // 2
    if 2 * half > done:
        pack_ref[pl.ds(done, 2 * half - done)] = jnp.zeros((2 * half - done, 2 * channels), F32)
    first = side_ref[pl.ds(0, 1)] > 0
    low, high = pack_ref[pl.ds(0, half)], pack_ref[pl.ds(half, half)]
    keep_ref[...] = jnp.where(first, low, high)
    give_ref[...] = jnp.where(first, high, low)


def unpack_body(gscale, side_ref, mine_ref, other_ref, weight_ref, pack_ref):
    channels = weight_ref.shape[2]
    half = mine_ref.shape[0]
    first = side_ref[pl.ds(0, 1)] > 0
    mine, other = mine_ref[...] * gscale, other_ref[...] * gscale
    pack_ref[pl.ds(0, half)] = jnp.where(first, mine, other)
    pack_ref[pl.ds(half, half)] = jnp.where(first, other, mine)
    tall = 3 * channels
    for a in range(3):
        here = pack_ref[pl.ds(a * channels, channels)]
        weight_ref[a, 0] = here[:, :channels]
        weight_ref[a, 1] = here[:, channels:]
    last = pack_ref[pl.ds(tall, tall // 2)]
    last = jnp.concatenate([last[:, :channels], last[:, channels:]], axis=0)
    for a in range(3):
        weight_ref[a, 2] = last[a * channels : (a + 1) * channels]


def edges(first, last):
    size = lax.axis_size("span")
    if size == 2:
        low = lax.axis_index("span") == 0
        other = swap_cores(jnp.where(low, last, first))
        none = jnp.zeros_like(other)
        return jnp.where(low, none, other), jnp.where(low, other, none)
    up = [(i, (i + 1) % size) for i in range(size - 1)]
    down = [(j, i) for i, j in up]
    return lax.ppermute(last, "span", up), lax.ppermute(first, "span", down)


def tree_sum(parts):
    while len(parts) > 1:
        parts = [parts[i] + parts[i + 1] for i in range(0, len(parts), 2)]
    return parts[0]


def xor_sum(x, axis, steps):
    size = lax.axis_size(axis)
    return tree_sum([x] + [lax.ppermute(x, axis, [(i, i ^ k) for i in range(size)]) for k in steps[1:]])


def swap_cores(x):
    size = lax.axis_size("span")
    return lax.ppermute(x, "span", [(i, i ^ 1) for i in range(size)])


def far_parts(mine, plane):
    size = lax.axis_size("span")
    count = lax.axis_size("tm")
    if size > 2:
        mine = xor_sum(mine, "span", list(range(0, size, 2)))
    steps = range(plane, count, plane)
    return [mine] + [lax.ppermute(mine, "tm", [(i, i ^ k) for i in range(count)]) for k in steps]


def local(frames, cotangent, spatial_weight, temporal_kernel):
    channels, rows, width = frames.shape[1:]
    count = lax.axis_size("tm")
    plane = min(4, count)
    gscale = float(count * rows * lax.axis_size("span") * width) ** (-0.5)
    group = channels // count
    shape = (rows, channels, width)
    tile = (count, group, rows, width)
    area = rows * width
    act_bytes = channels * area * 2
    flops = 18 * channels * channels * area
    half = -(-(9 * channels * channels) // (128 * 16)) * 8
    side = jnp.full((8, 128), 1 - lax.axis_index("span") % 2, F32)
    part = pltpu.VMEM((rows + 2, 3 * channels, width), F32)
    whole = jax.ShapeDtypeStruct(shape, BF16)
    native = jax.ShapeDtypeStruct((channels, rows, width), BF16)
    padded = (rows + 2, channels, width)

    def exchange(x):
        return lax.all_to_all(x, "tm", split_axis=0, concat_axis=0, tiled=True)

    frame, cot = frames[0], cotangent[0]
    cot_tile = exchange(cot.reshape(tile))
    x_before, x_after = edges(frame[:, 0], frame[:, -1])
    weight = spatial_weight.transpose(0, 2, 1, 3).reshape(3 * channels, 3 * channels)
    weight_back = spatial_weight.transpose(0, 3, 1, 2).reshape(3 * channels, 3 * channels)
    coef = lax.dynamic_slice_in_dim(temporal_kernel, lax.axis_index("tm") * group, group, 0)
    coef = jnp.broadcast_to(coef.astype(F32)[:, :, None], (group, count, width))
    active, slope, x = call(
        forward_body,
        (native, jax.ShapeDtypeStruct(shape, F32), jax.ShapeDtypeStruct(padded, BF16)),
        [part, pltpu.VMEM(shape, BF16)],
        flops,
        4 * act_bytes,
    )(x_before, frame, x_after, weight)
    back = call(
        back_body, jax.ShapeDtypeStruct(tile, BF16), [], 17 * channels * area, 2 * act_bytes
    )(coef, cot_tile)
    back, slope = lax.optimization_barrier((back, slope))
    back = exchange(back)
    active, back = lax.optimization_barrier((active, back))
    act_tile = exchange(active.reshape(tile))
    dhidden, keep, give = call(
        weight_grad_body,
        (whole, *[jax.ShapeDtypeStruct((half, 128), F32)] * 2),
        [
            pltpu.VMEM((rows + 4, channels, width), BF16),
            pltpu.VMEM((3 * channels, 3 * channels), F32),
            pltpu.VMEM((2 * half, 128), F32),
            pltpu.VMEM(shape, BF16),
        ],
        flops,
        5 * act_bytes,
    )(side, back.reshape(native.shape), slope, x)
    d_before, d_after = edges(dhidden[0], dhidden[-1])
    input_grad = call(
        input_grad_body,
        native,
        [pltpu.VMEM(padded, BF16), part, pltpu.VMEM(shape, F32)],
        flops,
        4 * act_bytes,
    )(d_before, dhidden, d_after, weight_back, cot)
    weight_mine = keep + swap_cores(give)
    packed = jax.ShapeDtypeStruct((count, group * rows + count, width), BF16)
    along = call(
        along_body,
        packed,
        [pltpu.VMEM((group, count, 8, width), F32)],
        34 * channels * area,
        3 * act_bytes,
    )(coef, cot_tile, act_tile)
    weight_parts = far_parts(weight_mine, plane)
    along, *weight_parts = lax.optimization_barrier((along, *weight_parts))
    along = exchange(along)
    weight_mine = xor_sum(tree_sum(weight_parts), "tm", list(range(plane)))
    weight_mine, input_grad = lax.optimization_barrier((weight_mine, input_grad))
    weight_total = call(
        functools.partial(unpack_body, gscale),
        jax.ShapeDtypeStruct(spatial_weight.shape, F32),
        [pltpu.VMEM((2 * half, 128), F32)],
        0,
        act_bytes,
    )(side, weight_mine, swap_cores(weight_mine))
    kernel_sum = call(
        kernel_sums_body, jax.ShapeDtypeStruct((count, channels), F32), [], 0, 0
    )(along)
    block_output = call(block_output_body, native, [], 0, 0)(frame, along)
    kernel_total = xor_sum(kernel_sum, "span", list(range(lax.axis_size("span")))) * gscale
    return (
        block_output[None],
        input_grad[None],
        weight_total,
        kernel_total.T,
    )


def solution(mesh):
    placed = (P("tm", None, "span", None), P("tm", None, "span", None), P(), P())
    return jax.shard_map(
        local,
        mesh=mesh,
        in_specs=placed,
        out_specs=(P("tm", None, "span", None), P("tm", None, "span", None), P(), P()),
        check_vma=False,
    )
```

time: 97.9 us -> 89.4 us (0.913)
  blocking collectives: 0 us -> 18.1 us
  waiting for transfers between devices: 43.5 us -> 28.5 us
  starting transfers between devices: 33.8 us -> 25.7 us
  local copies, waits for them, and re-layouts: 10.1 us -> 5.64 us
    all_to_all x0 -> x1, blocking collectives: none -> 18.1 us  [exchange(): return lax.all_to_all(x, 'tm', split_axis=0, concat_axis=0, tiled=True)]
    all_to_all x4 -> x3, waiting for transfers between devices: 32.4 us -> 20.5 us  [exchange(): return lax.all_to_all(x, 'tm', split_axis=0, concat_axis=0, tiled=True)]
    ppermute x6 -> x4, starting transfers between devices: 8.15 us -> 3.62 us  [xor_sum(): lax.ppermute(x, axis, [(i, i ^ k) for i in range(size)])]
    ppermute x6 -> x4, waiting for transfers between devices: 9.63 us -> 5.49 us  [xor_sum(): lax.ppermute(x, axis, [(i, i ^ k) for i in range(size)])]
    unnamed x17 -> x20, local copies, waits for them, and re-layouts: 8.1 us -> 4.86 us
    all_to_all x4 -> x3, starting transfers between devices: 20.2 us -> 17.5 us  [exchange(): return lax.all_to_all(x, 'tm', split_axis=0, concat_axis=0, tiled=True)]
    pallas_call x4 -> x7, Pallas kernels: 6.84 us -> 8.52 us  [the longest x1 1.98 us: local(): call(along_body, packed, [pltpu.VMEM((group, count, 8, width), F32)], 34...]
    ppermute x6 -> x7, waiting for transfers between devices: 1.47 us -> 2.52 us  [the longest x4 1.55 us: swap_cores(): return lax.ppermute(x, 'span', [(i, i ^ 1) for i in range(size)])]
  transfers between devices with their start and end apart: 16 -> 14, of which waited for: 6 -> 9; matrix products, arithmetic and copies ran while one was open for 4% -> 1% of each run, Pallas kernels for 8% -> 10%
where the time goes in v2:
time: 89.4 us; the launch traced here: 88.8 us
  waiting for transfers between devices  28.5 us (32%)
  starting transfers between devices  25.7 us (29%)
  blocking collectives  18.1 us (20%)
  Pallas kernels  9.21 us (10%)
  local copies, waits for them, and re-layouts  5.64 us (6%)
    all_to_all x3, waiting for transfers between devices, exchange(): return lax.all_to_all(x, 'tm', split_axis=0, concat_axis=0, tiled=True)  20.5 us
    all_to_all x1, blocking collectives, exchange(): return lax.all_to_all(x, 'tm', split_axis=0, concat_axis=0, tiled=True)  18.1 us
    all_to_all x3, starting transfers between devices, exchange(): return lax.all_to_all(x, 'tm', split_axis=0, concat_axis=0, tiled=True)  17.5 us
    ppermute x4, waiting for transfers between devices, xor_sum(): lax.ppermute(x, axis, [(i, i ^ k) for i in range(size)])  5.49 us
    unnamed x20, local copies, waits for them, and re-layouts  4.86 us
    ppermute x3, starting transfers between devices, far_parts(): lax.ppermute(mine, 'tm', [(i, i ^ k) for i in range(count)])  4.45 us
    ppermute x4, starting transfers between devices, xor_sum(): lax.ppermute(x, axis, [(i, i ^ k) for i in range(size)])  3.62 us
    pallas_call x1, Pallas kernels, local(): call(along_body, packed, [pltpu.VMEM((group, count, 8, width), F32)], 34...  1.98 us
  transfers between devices with their start and end apart: 14, of which 9 were waited for; matrix products, arithmetic and copies ran while one was open for 1% of the time, Pallas kernels for 10%

profile of v2, /device:TPU:0, one launch (start us, length us, event | category | flops | bytes accessed | tf_op | source)
XLA Modules:
  0.0 88.8 jit_solution(11227453210567326680)
XLA Ops:
  0.6 0.0 copy-start
  0.6 0.0 copy-start.1
  0.7 8.5 %all-to-all-start = ((bf16[16,4,32,128]{3,2,1,0:T(8,128)(2,1)}), bf16[16,4,32,128]{3,2,1,0:T(8,128)(2,1)S(1)}, u32[]{:S(2)}, u32[]{:S(2)}) async-start(bf16[16,4,32,128]{3,2,1,0:T(8,128)(2,1)} %bitcast.20), calls=%async_computation | async-start | bytes 1048576 | tf_op jit(solution)/shard_map/all_to_all | solution.py:315
  9.1 0.0 copy-done.1
  9.1 0.0 copy-start.8
  9.1 0.2 copy.29
  9.4 0.1 collective-permute-start
  9.5 0.0 copy-done
  9.5 0.1 constant_dynamic-slice_fusion
  9.6 0.1 copy.27
  9.6 0.4 copy-done.8
  10.0 0.1 copy.22
  10.2 0.2 reshape.25.weight_ref
  10.3 0.3 collective-permute-done
  10.6 1.5 %shard_map.75 = (bf16[64,32,128]{2,1,0:T(8,128)(2,1)S(1)}, f32[32,64,128]{2,1,0:T(8,128)S(1)}, bf16[34,64,128]{2,1,0:T(8,128)(2,1)S(1)}) custom-call(bf16[64,128]{1,0:T(8,128)(2,1)S(1)} %get-tuple-element.41.before_ref, bf16[64,32,128]{2,1,0:T(8,128)(2,1)S(1)} %bitcast.18, bf16[64,128]{1,0:T(8,128)(2,1)S(1)} %get-tuple-element.40.after_ref, ...), custom_call_target="tpu_custom_call" | custom-call | flops 301989888 | bytes 2097152 | tf_op jit(solution)/shard_map/pallas_call | solution.py:324
  12.1 0.0 copy-start.5
  12.1 0.8 copy-done.5
  12.9 0.0 copy-start.7
  12.9 0.8 copy-done.7
  13.7 10.5 %all-to-all-done.cot_ref = bf16[16,4,32,128]{3,2,1,0:T(8,128)(2,1)S(1)} async-done(((bf16[16,4,32,128]{3,2,1,0:T(8,128)(2,1)}), bf16[16,4,32,128]{3,2,1,0:T(8,128)(2,1)S(1)}, u32[]{:S(2)}, u32[]{:S(2)}) %all-to-all-start) | async-done | bytes 524320 | tf_op jit(solution)/shard_map/all_to_all | solution.py:315
  24.3 0.1 broadcast_in_dim.15.coef_ref
  24.3 0.7 shard_map.76
  25.0 18.1 %all_to_all.20 = bf16[16,4,32,128]{3,2,1,0:T(8,128)(2,1)S(1)} all-to-all(bf16[16,4,32,128]{3,2,1,0:T(8,128)(2,1)S(1)} %shard_map.76), channel_id=1, replica_groups=mesh['tm'=16,'span'=2] {'tm'}, dimensions={0} | all-to-all | bytes 1048576 | tf_op jit(solution)/shard_map/all_to_all | solution.py:315
  43.1 3.8 %all-to-all-start.2 = ((bf16[16,4,32,128]{3,2,1,0:T(8,128)(2,1)}), bf16[16,4,32,128]{3,2,1,0:T(8,128)(2,1)S(1)}, u32[]{:S(2)}, u32[]{:S(2)}) async-start(bf16[16,4,32,128]{3,2,1,0:T(8,128)(2,1)} %bitcast.23), calls=%async_computation.2 | async-start | bytes 1048576 | tf_op jit(solution)/shard_map/all_to_all | solution.py:315
  47.0 0.0 copy-start.6
  47.0 1.0 %copy-done.6 = bf16[34,64,128]{2,1,0:T(8,128)(2,1)S(1)} copy-done((bf16[34,64,128]{2,1,0:T(8,128)(2,1)S(1)}, bf16[34,64,128]{2,1,0:T(8,128)(2,1)}, u32[]{:S(2)}) %copy-start.6) | copy-done | bytes 557080
  48.1 1.2 %shard_map.78 = (bf16[32,64,128]{2,1,0:T(8,128)(2,1)S(1)}, f32[144,128]{1,0:T(8,128)S(1)}, f32[144,128]{1,0:T(8,128)S(1)}) custom-call(f32[8,128]{1,0:T(8,128)S(1)} %broadcast_in_dim.16.side_ref, bf16[64,32,128]{2,1,0:T(8,128)(2,1)S(1)} %bitcast.22, f32[32,64,128]{2,1,0:T(8,128)S(1)} %get-tuple-element.26.slope_ref, bf16[34,64,128]{2,1,0:T(8,128)(2,1)S(1)} %copy-done.6), custom_call_target="tpu_custom_call" | custom-call | flops 301989888 | bytes 2621440 | tf_op jit(solution)/shard_map/pallas_call | solution.py:338
  49.3 0.0 copy-start.3
  49.3 0.8 copy-done.3
  50.1 0.0 collective-permute-start.1
  50.1 1.3 %collective-permute-done.1 = f32[144,128]{1,0:T(8,128)S(1)} collective-permute-done((f32[144,128]{1,0:T(8,128)S(1)}, f32[144,128]{1,0:T(8,128)S(1)}, u32[]{:S(2)}, u32[]{:S(2)}) %collective-permute-start.1) | collective-permute-done | bytes 73760 | tf_op jit(solution)/shard_map/ppermute | solution.py:284
  51.4 2.0 %collective-permute-start.2 = (f32[144,128]{1,0:T(8,128)S(1)}, f32[144,128]{1,0:T(8,128)S(1)}, u32[]{:S(2)}, u32[]{:S(2)}) collective-permute-start(f32[144,128]{1,0:T(8,128)S(1)} %add.33), channel_id=1, source_target_pairs={{0,8},{2,10},{4,12},{6,14},{8,0},{10,2},{12,4},{14,6},{16,24},{18,... | collective-permute-start | bytes 221192 | tf_op jit(solution)/shard_map/ppermute | solution.py:293
  53.3 2.4 %collective-permute-start.3 = (f32[144,128]{1,0:T(8,128)S(1)}, f32[144,128]{1,0:T(8,128)S(1)}, u32[]{:S(2)}, u32[]{:S(2)}) collective-permute-start(f32[144,128]{1,0:T(8,128)S(1)} %add.33), channel_id=1, source_target_pairs={{0,16},{2,18},{4,20},{6,22},{8,24},{10,26},{12,28},{14,30},{16,0},... | collective-permute-start | bytes 221192 | tf_op jit(solution)/shard_map/ppermute | solution.py:293
  55.7 0.1 collective-permute-start.4
  55.8 7.3 %all-to-all-done.2.act_ref = bf16[16,4,32,128]{3,2,1,0:T(8,128)(2,1)S(1)} async-done(((bf16[16,4,32,128]{3,2,1,0:T(8,128)(2,1)}), bf16[16,4,32,128]{3,2,1,0:T(8,128)(2,1)S(1)}, u32[]{:S(2)}, u32[]{:S(2)}) %all-to-all-start.2) | async-done | bytes 524320 | tf_op jit(solution)/shard_map/all_to_all | solution.py:315
  63.1 2.0 %shard_map.77 = bf16[16,144,128]{2,1,0:T(8,128)(2,1)} custom-call(f32[4,16,128]{2,1,0:T(8,128)S(1)} %broadcast_in_dim.15.coef_ref, bf16[16,4,32,128]{3,2,1,0:T(8,128)(2,1)S(1)} %all-to-all-done.cot_ref, bf16[16,4,32,128]{3,2,1,0:T(8,128)(2,1)S(1)} %all-to-all-done.2.act_ref), custom_call_target="tpu_custom_call" | custom-call | flops 8912896 | bytes 1572864 | tf_op jit(solution)/shard_map/pallas_call | solution.py:360
  65.1 0.0 collective-permute-done.2
  65.1 1.0 %collective-permute-done.3 = f32[144,128]{1,0:T(8,128)S(1)} collective-permute-done((f32[144,128]{1,0:T(8,128)S(1)}, f32[144,128]{1,0:T(8,128)S(1)}, u32[]{:S(2)}, u32[]{:S(2)}) %collective-permute-start.3) | collective-permute-done | bytes 73760 | tf_op jit(solution)/shard_map/ppermute | solution.py:293
  66.1 0.0 collective-permute-done.4
  66.1 5.2 %all-to-all-start.3 = ((bf16[16,144,128]{2,1,0:T(8,128)(2,1)}), bf16[16,144,128]{2,1,0:T(8,128)(2,1)S(1)}, u32[]{:S(2)}, u32[]{:S(2)}) async-start(bf16[16,144,128]{2,1,0:T(8,128)(2,1)} %shard_map.77), calls=%async_computation.3 | async-start | bytes 1179648 | tf_op jit(solution)/shard_map/all_to_all | solution.py:315
  71.3 0.0 copy-start.4
  71.3 0.0 copy-start.2
  71.3 0.2 copy.25
  71.5 0.2 reshape.28.weight_ref
  71.6 0.7 copy-done.4
  72.3 0.0 collective-permute-start.8
  72.4 2.0 %collective-permute-start.6 = (f32[144,128]{1,0:T(8,128)S(1)}, f32[144,128]{1,0:T(8,128)S(1)}, u32[]{:S(2)}, u32[]{:S(2)}) collective-permute-start(f32[144,128]{1,0:T(8,128)S(1)} %add_add_fusion.1), channel_id=1, source_target_pairs={{0,4},{2,6},{4,0},{6,2},{8,12},{10,14},{12,8},{14,10},{16,20},{18,... | collective-permute-start | bytes 221192 | tf_op jit(solution)/shard_map/ppermute | solution.py:279
  74.3 1.5 %collective-permute-start.7 = (f32[144,128]{1,0:T(8,128)S(1)}, f32[144,128]{1,0:T(8,128)S(1)}, u32[]{:S(2)}, u32[]{:S(2)}) collective-permute-start(f32[144,128]{1,0:T(8,128)S(1)} %add_add_fusion.1), channel_id=1, source_target_pairs={{0,6},{2,4},{4,2},{6,0},{8,14},{10,12},{12,10},{14,8},{16,22},{18,... | collective-permute-start | bytes 221192 | tf_op jit(solution)/shard_map/ppermute | solution.py:279
  75.8 0.1 collective-permute-start.5
  75.9 0.0 collective-permute-done.8
  75.9 0.0 copy-done.2
  75.9 2.0 %shard_map.80 = bf16[64,32,128]{2,1,0:T(8,128)(2,1)} custom-call(bf16[64,128]{1,0:T(8,128)(2,1)S(1)} %get-tuple-element.39.before_ref, bf16[32,64,128]{2,1,0:T(8,128)(2,1)S(1)} %copy-done.4, bf16[64,128]{1,0:T(8,128)(2,1)S(1)} %get-tuple-element.38.after_ref, bf16[192,192]{1,0:T(8,128)(2,1)S(1)} %reshape.28.weight_ref, bf16[64,32,128]{2,1,0:T(8,128)(2,1)S(1)} %bitcast.21), custom_call_target="tpu_custom_call" | custom-call | flops 301989888 | bytes 2097152 | tf_op jit(solution)/shard_map/pallas_call | solution.py:351
  77.9 2.2 %collective-permute-done.6 = f32[144,128]{1,0:T(8,128)S(1)} collective-permute-done((f32[144,128]{1,0:T(8,128)S(1)}, f32[144,128]{1,0:T(8,128)S(1)}, u32[]{:S(2)}, u32[]{:S(2)}) %collective-permute-start.6) | collective-permute-done | bytes 73760 | tf_op jit(solution)/shard_map/ppermute | solution.py:279
  80.1 1.6 %collective-permute-done.7 = f32[144,128]{1,0:T(8,128)S(1)} collective-permute-done((f32[144,128]{1,0:T(8,128)S(1)}, f32[144,128]{1,0:T(8,128)S(1)}, u32[]{:S(2)}, u32[]{:S(2)}) %collective-permute-start.7) | collective-permute-done | bytes 73760 | tf_op jit(solution)/shard_map/ppermute | solution.py:279
  81.7 1.7 %collective-permute-done.5 = f32[144,128]{1,0:T(8,128)S(1)} collective-permute-done((f32[144,128]{1,0:T(8,128)S(1)}, f32[144,128]{1,0:T(8,128)S(1)}, u32[]{:S(2)}, u32[]{:S(2)}) %collective-permute-start.5) | collective-permute-done | bytes 73760 | tf_op jit(solution)/shard_map/ppermute | solution.py:279
  83.4 0.1 collective-permute-start.9
  83.5 2.7 %all-to-all-done.3.got_ref = bf16[16,144,128]{2,1,0:T(8,128)(2,1)S(1)} async-done(((bf16[16,144,128]{2,1,0:T(8,128)(2,1)}), bf16[16,144,128]{2,1,0:T(8,128)(2,1)S(1)}, u32[]{:S(2)}, u32[]{:S(2)}) %all-to-all-start.3) | async-done | bytes 589856 | tf_op jit(solution)/shard_map/all_to_all | solution.py:315
  86.2 0.2 shard_map.82
  86.3 0.1 collective-permute-start.10
  86.4 0.0 collective-permute-done.9.other_ref
  86.4 0.8 shard_map.81
  87.3 0.9 %shard_map.79 = bf16[64,32,128]{2,1,0:T(8,128)(2,1)} custom-call(bf16[64,32,128]{2,1,0:T(8,128)(2,1)S(1)} %bitcast.19, bf16[16,144,128]{2,1,0:T(8,128)(2,1)S(1)} %all-to-all-done.3.got_ref), custom_call_target="tpu_custom_call" | custom-call | tf_op jit(solution)/shard_map/pallas_call | solution.py:382
  88.2 0.0 collective-permute-done.10
  88.2 0.6 multiply_bitcast_fusion
  (8 shorter events, 0.1 us)
Async XLA Ops:
  0.6 8.8 %copy-start = (bf16[64,16]{0,1:T(8,128)(2,1)S(1)}, bf16[64,16]{0,1:T(8,128)(2,1)}, u32[]{:S(2)}) copy-start(bf16[64,16]{0,1:T(8,128)(2,1)} %param.7) | copy-start | bytes 6148
  0.6 8.5 %copy-start.1 = (bf16[1,64,32,128]{3,2,1,0:T(8,128)(2,1)S(1)}, bf16[1,64,32,128]{3,2,1,0:T(8,128)(2,1)}, u32[]{:S(2)}) copy-start(bf16[1,64,32,128]{3,2,1,0:T(8,128)(2,1)} %param.4) | copy-start | bytes 1572868
  0.7 23.6 %all-to-all-start = ((bf16[16,4,32,128]{3,2,1,0:T(8,128)(2,1)}), bf16[16,4,32,128]{3,2,1,0:T(8,128)(2,1)S(1)}, u32[]{:S(2)}, u32[]{:S(2)}) async-start(bf16[16,4,32,128]{3,2,1,0:T(8,128)(2,1)} %bitcast.20), calls=%async_computation | async-start | bytes 1048576 | tf_op jit(solution)/shard_map/all_to_all | solution.py:315
  9.1 0.9 %copy-start.8 = (bf16[3,3,64,64]{3,2,1,0:T(8,128)(2,1)S(1)}, bf16[3,3,64,64]{3,2,1,0:T(8,128)(2,1)}, u32[]{:S(2)}) copy-start(bf16[3,3,64,64]{3,2,1,0:T(8,128)(2,1)} %param.6) | copy-start | bytes 221188
  9.4 1.2 %collective-permute-start = (bf16[64,128]{1,0:T(8,128)(2,1)S(1)}, bf16[64,128]{1,0:T(8,128)(2,1)S(1)}, u32[]{:S(2)}, u32[]{:S(2)}) collective-permute-start(bf16[64,128]{1,0:T(8,128)(2,1)S(1)} %fusion), channel_id=1, source_target_pairs={{0,1},{1,0},{2,3},{3,2},{4,5},{5,4},{6,7},{7,6},{8,9},{9,8},{10,11... | collective-permute-start | bytes 49160 | tf_op jit(solution)/shard_map/ppermute | solution.py:284
  12.1 0.8 copy-start.5
  12.9 0.8 copy-start.7
  43.1 20.0 %all-to-all-start.2 = ((bf16[16,4,32,128]{3,2,1,0:T(8,128)(2,1)}), bf16[16,4,32,128]{3,2,1,0:T(8,128)(2,1)S(1)}, u32[]{:S(2)}, u32[]{:S(2)}) async-start(bf16[16,4,32,128]{3,2,1,0:T(8,128)(2,1)} %bitcast.23), calls=%async_computation.2 | async-start | bytes 1048576 | tf_op jit(solution)/shard_map/all_to_all | solution.py:315
  47.0 1.1 %copy-start.6 = (bf16[34,64,128]{2,1,0:T(8,128)(2,1)S(1)}, bf16[34,64,128]{2,1,0:T(8,128)(2,1)}, u32[]{:S(2)}) copy-start(bf16[34,64,128]{2,1,0:T(8,128)(2,1)} %copy-done.5) | copy-start | bytes 1671172
  49.3 0.8 copy-start.3
  50.1 1.3 %collective-permute-start.1 = (f32[144,128]{1,0:T(8,128)S(1)}, f32[144,128]{1,0:T(8,128)S(1)}, u32[]{:S(2)}, u32[]{:S(2)}) collective-permute-start(f32[144,128]{1,0:T(8,128)S(1)} %get-tuple-element.29), channel_id=1, source_target_pairs={{0,1},{1,0},{2,3},{3,2},{4,5},{5,4},{6,7},{7,6},{8,9},{9,8},{10,11... | collective-permute-start | bytes 221192 | tf_op jit(solution)/shard_map/ppermute | solution.py:284
  51.4 13.7 %collective-permute-start.2 = (f32[144,128]{1,0:T(8,128)S(1)}, f32[144,128]{1,0:T(8,128)S(1)}, u32[]{:S(2)}, u32[]{:S(2)}) collective-permute-start(f32[144,128]{1,0:T(8,128)S(1)} %add.33), channel_id=1, source_target_pairs={{0,8},{2,10},{4,12},{6,14},{8,0},{10,2},{12,4},{14,6},{16,24},{18,... | collective-permute-start | bytes 221192 | tf_op jit(solution)/shard_map/ppermute | solution.py:293
  53.3 12.7 %collective-permute-start.3 = (f32[144,128]{1,0:T(8,128)S(1)}, f32[144,128]{1,0:T(8,128)S(1)}, u32[]{:S(2)}, u32[]{:S(2)}) collective-permute-start(f32[144,128]{1,0:T(8,128)S(1)} %add.33), channel_id=1, source_target_pairs={{0,16},{2,18},{4,20},{6,22},{8,24},{10,26},{12,28},{14,30},{16,0},... | collective-permute-start | bytes 221192 | tf_op jit(solution)/shard_map/ppermute | solution.py:293
  55.7 10.3 %collective-permute-start.4 = (f32[144,128]{1,0:T(8,128)S(1)}, f32[144,128]{1,0:T(8,128)S(1)}, u32[]{:S(2)}, u32[]{:S(2)}) collective-permute-start(f32[144,128]{1,0:T(8,128)S(1)} %add.33), channel_id=1, source_target_pairs={{0,24},{2,26},{4,28},{6,30},{8,16},{10,18},{12,20},{14,22},{16,8},... | collective-permute-start | bytes 221192 | tf_op jit(solution)/shard_map/ppermute | solution.py:293
  66.1 20.1 %all-to-all-start.3 = ((bf16[16,144,128]{2,1,0:T(8,128)(2,1)}), bf16[16,144,128]{2,1,0:T(8,128)(2,1)S(1)}, u32[]{:S(2)}, u32[]{:S(2)}) async-start(bf16[16,144,128]{2,1,0:T(8,128)(2,1)} %shard_map.77), calls=%async_computation.3 | async-start | bytes 1179648 | tf_op jit(solution)/shard_map/all_to_all | solution.py:315
  71.3 1.0 %copy-start.4 = (bf16[32,64,128]{2,1,0:T(8,128)(2,1)S(1)}, bf16[32,64,128]{2,1,0:T(8,128)(2,1)}, u32[]{:S(2)}) copy-start(bf16[32,64,128]{2,1,0:T(8,128)(2,1)} %copy-done.3) | copy-start | bytes 1572868
  71.3 4.6 %copy-start.2 = (bf16[1,64,32,128]{3,2,1,0:T(8,128)(2,1)S(1)}, bf16[1,64,32,128]{3,2,1,0:T(8,128)(2,1)}, u32[]{:S(2)}) copy-start(bf16[1,64,32,128]{3,2,1,0:T(8,128)(2,1)} %param.5) | copy-start | bytes 1572868
  72.3 3.6 %collective-permute-start.8 = (bf16[64,128]{1,0:T(8,128)(2,1)S(1)}, bf16[64,128]{1,0:T(8,128)(2,1)S(1)}, u32[]{:S(2)}, u32[]{:S(2)}) collective-permute-start(bf16[64,128]{1,0:T(8,128)(2,1)S(1)} %select_bitcast_fusion), channel_id=1, source_target_pairs={{0,1},{1,0},{2,3},{3,2},{4,5},{5,4},{6,7},{7,6},{8,9},{9,8},{10,11... | collective-permute-start | bytes 49160 | tf_op jit(solution)/shard_map/ppermute | solution.py:284
  72.4 7.7 %collective-permute-start.6 = (f32[144,128]{1,0:T(8,128)S(1)}, f32[144,128]{1,0:T(8,128)S(1)}, u32[]{:S(2)}, u32[]{:S(2)}) collective-permute-start(f32[144,128]{1,0:T(8,128)S(1)} %add_add_fusion.1), channel_id=1, source_target_pairs={{0,4},{2,6},{4,0},{6,2},{8,12},{10,14},{12,8},{14,10},{16,20},{18,... | collective-permute-start | bytes 221192 | tf_op jit(solution)/shard_map/ppermute | solution.py:279
  74.3 7.4 %collective-permute-start.7 = (f32[144,128]{1,0:T(8,128)S(1)}, f32[144,128]{1,0:T(8,128)S(1)}, u32[]{:S(2)}, u32[]{:S(2)}) collective-permute-start(f32[144,128]{1,0:T(8,128)S(1)} %add_add_fusion.1), channel_id=1, source_target_pairs={{0,6},{2,4},{4,2},{6,0},{8,14},{10,12},{12,10},{14,8},{16,22},{18,... | collective-permute-start | bytes 221192 | tf_op jit(solution)/shard_map/ppermute | solution.py:279
  75.8 7.6 %collective-permute-start.5 = (f32[144,128]{1,0:T(8,128)S(1)}, f32[144,128]{1,0:T(8,128)S(1)}, u32[]{:S(2)}, u32[]{:S(2)}) collective-permute-start(f32[144,128]{1,0:T(8,128)S(1)} %add_add_fusion.1), channel_id=1, source_target_pairs={{0,2},{2,0},{4,6},{6,4},{8,10},{10,8},{12,14},{14,12},{16,18},{18,... | collective-permute-start | bytes 221192 | tf_op jit(solution)/shard_map/ppermute | solution.py:279
  83.4 3.0 %collective-permute-start.9 = (f32[144,128]{1,0:T(8,128)S(1)}, f32[144,128]{1,0:T(8,128)S(1)}, u32[]{:S(2)}, u32[]{:S(2)}) collective-permute-start(f32[144,128]{1,0:T(8,128)S(1)} %add_add_fusion.mine_ref), channel_id=1, source_target_pairs={{0,1},{1,0},{2,3},{3,2},{4,5},{5,4},{6,7},{7,6},{8,9},{9,8},{10,11... | collective-permute-start | bytes 221192 | tf_op jit(solution)/shard_map/ppermute | solution.py:284
  86.3 1.8 %collective-permute-start.10 = (f32[16,64]{1,0:T(8,128)S(1)}, f32[16,64]{1,0:T(8,128)S(1)}, u32[]{:S(2)}, u32[]{:S(2)}) collective-permute-start(f32[16,64]{1,0:T(8,128)S(1)} %shard_map.82), channel_id=1, source_target_pairs={{0,1},{1,0},{2,3},{3,2},{4,5},{5,4},{6,7},{7,6},{8,9},{9,8},{10,11... | collective-permute-start | bytes 12296 | tf_op jit(solution)/shard_map/ppermute | solution.py:279

commit v3 on v2

--- a/solution.py
+++ b/solution.py
@@ -12,14 +12,25 @@
 VMEM_LIMIT = 16 * 1024 * 1024
 
 
-def call(body, out, scratch, flops, nbytes):
-    return pl.pallas_call(
-        body,
-        out_shape=out,
-        scratch_shapes=scratch,
-        compiler_params=pltpu.CompilerParams(vmem_limit_bytes=VMEM_LIMIT),
-        cost_estimate=pl.CostEstimate(flops=flops, bytes_accessed=nbytes, transcendentals=0),
-    )
+def call(body, out, scratch, flops, nbytes, hbm_in=(), hbm_out=()):
+    def specs(arrays, outside):
+        return [
+            pl.BlockSpec(memory_space=pltpu.HBM if k in outside else pltpu.VMEM)
+            for k in range(len(arrays))
+        ]
+
+    def run(*operands):
+        return pl.pallas_call(
+            body,
+            out_shape=out,
+            in_specs=specs(operands, hbm_in),
+            out_specs=specs(out, hbm_out),
+            scratch_shapes=scratch,
+            compiler_params=pltpu.CompilerParams(vmem_limit_bytes=VMEM_LIMIT),
+            cost_estimate=pl.CostEstimate(flops=flops, bytes_accessed=nbytes, transcendentals=0),
+        )(*operands)
+
+    return run
 
 
 def shifted(x, back):
@@ -63,7 +74,8 @@
 
 
 def forward_body(
-    before_ref, x_ref, after_ref, weight_ref, active_ref, slope_ref, pad_ref, part_ref, act_ref
+    before_ref, x_ref, after_ref, weight_ref,
+    active_ref, slope_ref, pad_ref, part_ref, act_ref,
 ):
     channels, rows, width = x_ref.shape
     fill_padded(pad_ref, before_ref, swapped(x_ref[...]), after_ref)
@@ -84,9 +96,14 @@
     active_ref[...] = swapped(act_ref[...])
 
 
-def input_grad_body(before_ref, d_ref, after_ref, weight_ref, cot_ref, out_ref, pad_ref, part_ref, sum_ref):
-    rows, channels, width = d_ref.shape
-    fill_padded(pad_ref, before_ref, d_ref[...], after_ref)
+def input_grad_body(
+    before_ref, after_ref, weight_ref, got_ref, slope_ref, cot_ref, out_ref,
+    pad_ref, part_ref, sum_ref, turn_ref,
+):
+    rows, channels, width = slope_ref.shape
+    dhidden_rows(got_ref, slope_ref, turn_ref, pad_ref, 1)
+    pad_ref[0] = before_ref[...]
+    pad_ref[rows + 1] = after_ref[...]
     conv_partials(pad_ref, weight_ref, part_ref, True)
 
     def one(row, carry):
@@ -113,8 +130,10 @@
     lax.fori_loop(0, group * per, one, 0)
 
 
-def back_body(coef_ref, cot_ref, back_ref):
+def back_body(coef_ref, cot_ref, active_ref, out_ref):
     frames, group = cot_ref.shape[:2]
+    for owner in range(frames):
+        out_ref[owner, 1] = active_ref[pl.ds(owner * group, group)]
 
     def one(chan, some):
         cot = [cot_ref[t, chan, some].astype(F32) for t in range(frames)]
@@ -123,24 +142,32 @@
             total = coef[0] * cot[r]
             for t in range(r + 1, frames):
                 total = total + coef[t - r] * cot[t]
-            back_ref[r, chan, some] = total.astype(BF16)
+            out_ref[r, 0, chan, some] = total.astype(BF16)
 
     chunks_of(cot_ref.shape, one)
 
 
-def along_body(coef_ref, cot_ref, act_ref, out_ref, sum_ref):
-    frames, group, rows, width = cot_ref.shape
-    sum_ref[...] = jnp.zeros_like(sum_ref)
+def along_body(coef_ref, got_ref, along_ref):
+    frames, _, group, rows, width = got_ref.shape
 
     def one(chan, some):
-        act = [act_ref[t, chan, some].astype(F32) for t in range(frames)]
+        act = [got_ref[t, 1, chan, some].astype(F32) for t in range(frames)]
         coef = [coef_ref[chan, pl.ds(l, 1)] for l in range(frames)]
-        to = pl.ds(pl.multiple_of(chan * rows + some.start, 16), 16)
         for t in range(frames):
             total = coef[0] * act[t]
             for r in range(t):
                 total = total + coef[t - r] * act[r]
-            out_ref[t, to] = total.astype(BF16)
+            along_ref[t, chan, some] = total.astype(BF16)
+
+    chunks_of(along_ref.shape, one)
+
+
+def kernel_sums(cot_ref, got_ref, mine_ref, sum_ref):
+    frames, group, rows, width = cot_ref.shape
+    sum_ref[...] = jnp.zeros_like(sum_ref)
+
+    def one(chan, some):
+        act = [got_ref[t, 1, chan, some].astype(F32) for t in range(frames)]
         cot = [cot_ref[t, chan, some].astype(F32) for t in range(frames)]
         for lag in range(frames):
             total = cot[lag] * act[0]
@@ -149,62 +176,44 @@
             sum_ref[chan, lag] += total[:8] + total[8:]
 
     chunks_of(cot_ref.shape, one)
-    lane = lax.broadcasted_iota(jnp.int32, (frames, width), 1)
     both = jnp.zeros((frames, width), F32)
+    lane = mine_ref[pl.ds(0, 1)]
     for chan in range(group):
         sums = jnp.sum(jnp.sum(sum_ref[chan], axis=1), axis=1, keepdims=True)
-        high = sums.astype(BF16).astype(F32)
-        both = jnp.where(lane == chan, high, both)
-        both = jnp.where(lane == width // 2 + chan, sums - high, both)
-    both = both.astype(BF16)
-    for t in range(frames):
-        out_ref[t, pl.ds(group * rows, frames)] = both
-
-
-def block_output_body(x_ref, got_ref, out_ref):
-    channels, rows, width = x_ref.shape
-    owners = got_ref.shape[0]
-    group = channels // owners
-    for owner in range(owners):
-        for chan in range(group):
-            here = owner * group + chan
-            along = got_ref[owner, pl.ds(chan * rows, rows)].astype(F32)
-            out_ref[here] = (x_ref[here].astype(F32) + along).astype(BF16)
-
-
-def kernel_sums_body(got_ref, sums_ref):
-    owners = got_ref.shape[0]
-    lags, channels = sums_ref.shape
-    width = got_ref.shape[2]
-    group = channels // owners
-    lane = lax.broadcasted_iota(jnp.int32, (lags, width), 1)
-    total = jnp.zeros((lags, width), F32)
-    for owner in range(owners):
-        part = got_ref[owner, pl.ds(got_ref.shape[1] - lags, lags)].astype(F32)
-        part = part + pltpu.roll(part, width // 2, 1)
-        if owner > 0:
-            part = pltpu.roll(part, owner * group, 1)
-        total = jnp.where(lane // group == owner, part, total)
-    sums_ref[...] = total[:, :channels]
+        both = jnp.where(lane == chan, sums, both)
+    return both
+
+
+def block_output_body(x_ref, even_ref, odd_ref, out_ref):
+    for chan in range(x_ref.shape[0]):
+        along = (even_ref, odd_ref)[chan % 2][chan]
+        out_ref[chan] = (x_ref[chan].astype(F32) + along.astype(F32)).astype(BF16)
+
+
+def dhidden_rows(got_ref, slope_ref, turn_ref, to_ref, first):
+    rows, channels, width = slope_ref.shape
+    turn_ref[...] = swapped(got_ref[:, 0].reshape(channels, rows, width))
+
+    def one(row, carry):
+        to_ref[row + first] = (turn_ref[row].astype(F32) * slope_ref[row]).astype(BF16)
+        return carry
+
+    lax.fori_loop(0, rows, one, 0, unroll=4)
 
 
 def weight_grad_body(
-    side_ref, back_ref, slope_ref, pad_ref, dhid_ref, keep_ref, give_ref,
-    dpad_ref, grad_ref, pack_ref, turn_ref,
+    side_ref, mine_ref, got_ref, slope_ref, before_ref, x_ref, after_ref, cot_ref,
+    edge_ref, keep_ref, give_ref,
+    dpad_ref, grad_ref, pack_ref, turn_ref, pad_ref, sum_ref,
 ):
     rows, channels, width = slope_ref.shape
-    turn_ref[...] = swapped(back_ref[...])
+    fill_padded(pad_ref, before_ref, swapped(x_ref[...]), after_ref)
     zero = jnp.zeros((2, channels, width), BF16)
     dpad_ref[pl.ds(0, 2)] = zero
     dpad_ref[pl.ds(rows + 2, 2)] = zero
-
-    def one(row, carry):
-        value = (turn_ref[row].astype(F32) * slope_ref[row]).astype(BF16)
-        dhid_ref[row] = value
-        dpad_ref[row + 2] = value
-        return carry
-
-    lax.fori_loop(0, rows, one, 0, unroll=4)
+    dhidden_rows(got_ref, slope_ref, turn_ref, dpad_ref, 2)
+    edge_ref[0] = dpad_ref[2]
+    edge_ref[1] = dpad_ref[rows + 1]
     grad_ref[...] = jnp.zeros_like(grad_ref)
 
     def two(step, carry):
@@ -230,6 +239,12 @@
     )
     half = keep_ref.shape[0]
     done = tall + tall // 2
+    sums = kernel_sums(cot_ref, got_ref, mine_ref, sum_ref)
+    lags = sums.shape[0] // 2
+    pack_ref[pl.ds(done, lags)] = jnp.concatenate(
+        [sums[:lags, :channels], sums[lags:, :channels]], axis=1
+    )
+    done += lags
     if 2 * half > done:
         pack_ref[pl.ds(done, 2 * half - done)] = jnp.zeros((2 * half - done, 2 * channels), F32)
     first = side_ref[pl.ds(0, 1)] > 0
@@ -238,7 +253,7 @@
     give_ref[...] = jnp.where(first, high, low)
 
 
-def unpack_body(gscale, side_ref, mine_ref, other_ref, weight_ref, pack_ref):
+def unpack_body(gscale, side_ref, mine_ref, other_ref, weight_ref, kernel_ref, pack_ref):
     channels = weight_ref.shape[2]
     half = mine_ref.shape[0]
     first = side_ref[pl.ds(0, 1)] > 0
@@ -254,6 +269,24 @@
     last = jnp.concatenate([last[:, :channels], last[:, channels:]], axis=0)
     for a in range(3):
         weight_ref[a, 2] = last[a * channels : (a + 1) * channels]
+    lags = kernel_ref.shape[0] // 2
+    sums = pack_ref[pl.ds(tall + tall // 2, lags)]
+    kernel_ref[pl.ds(0, lags)] = sums[:, :channels]
+    kernel_ref[pl.ds(lags, lags)] = sums[:, channels:]
+
+
+def behind(x, other):
+    def body(x_ref, other_ref, out_ref):
+        pass
+
+    anywhere = pl.BlockSpec(memory_space=pl.ANY)
+    return pl.pallas_call(
+        body,
+        out_shape=jax.ShapeDtypeStruct(x.shape, x.dtype),
+        in_specs=[anywhere, anywhere],
+        out_specs=anywhere,
+        input_output_aliases={0: 0},
+    )(x, other)
 
 
 def edges(first, last):
@@ -284,13 +317,13 @@
     return lax.ppermute(x, "span", [(i, i ^ 1) for i in range(size)])
 
 
-def far_parts(mine, plane):
+def total_over_rest(mine, plane):
     size = lax.axis_size("span")
     count = lax.axis_size("tm")
     if size > 2:
         mine = xor_sum(mine, "span", list(range(0, size, 2)))
-    steps = range(plane, count, plane)
-    return [mine] + [lax.ppermute(mine, "tm", [(i, i ^ k) for i in range(count)]) for k in steps]
+    mine = xor_sum(mine, "tm", list(range(0, count, plane)))
+    return xor_sum(mine, "tm", list(range(plane)))
 
 
 def local(frames, cotangent, spatial_weight, temporal_kernel):
@@ -304,8 +337,9 @@
     area = rows * width
     act_bytes = channels * area * 2
     flops = 18 * channels * channels * area
-    half = -(-(9 * channels * channels) // (128 * 16)) * 8
+    half = -(-(9 * channels * channels + count * channels) // (128 * 16)) * 8
     side = jnp.full((8, 128), 1 - lax.axis_index("span") % 2, F32)
+    mine = lax.broadcasted_iota(jnp.int32, (8, width), 1) - lax.axis_index("tm") * group
     part = pltpu.VMEM((rows + 2, 3 * channels, width), F32)
     whole = jax.ShapeDtypeStruct(shape, BF16)
     native = jax.ShapeDtypeStruct((channels, rows, width), BF16)
@@ -320,67 +354,69 @@
     weight = spatial_weight.transpose(0, 2, 1, 3).reshape(3 * channels, 3 * channels)
     weight_back = spatial_weight.transpose(0, 3, 1, 2).reshape(3 * channels, 3 * channels)
     coef = lax.dynamic_slice_in_dim(temporal_kernel, lax.axis_index("tm") * group, group, 0)
+    weight, weight_back = lax.optimization_barrier((weight, weight_back))
     coef = jnp.broadcast_to(coef.astype(F32)[:, :, None], (group, count, width))
-    active, slope, x = call(
+    active, slope = call(
         forward_body,
-        (native, jax.ShapeDtypeStruct(shape, F32), jax.ShapeDtypeStruct(padded, BF16)),
-        [part, pltpu.VMEM(shape, BF16)],
+        (native, jax.ShapeDtypeStruct(shape, F32)),
+        [pltpu.VMEM(padded, BF16), part, pltpu.VMEM(shape, BF16)],
         flops,
         4 * act_bytes,
     )(x_before, frame, x_after, weight)
-    back = call(
-        back_body, jax.ShapeDtypeStruct(tile, BF16), [], 17 * channels * area, 2 * act_bytes
-    )(coef, cot_tile)
-    back, slope = lax.optimization_barrier((back, slope))
-    back = exchange(back)
-    active, back = lax.optimization_barrier((active, back))
-    act_tile = exchange(active.reshape(tile))
-    dhidden, keep, give = call(
+    packed = (count, 2, group, rows, width)
+    [out] = call(
+        back_body,
+        [jax.ShapeDtypeStruct(packed, BF16)],
+        [],
+        17 * channels * area,
+        4 * act_bytes,
+    )(coef, cot_tile, active)
+    got = exchange(out)
+    [along] = call(
+        along_body, [jax.ShapeDtypeStruct(tile, BF16)], [], 17 * channels * area, 2 * act_bytes
+    )(coef, got)
+    d_edges, keep, give = call(
         weight_grad_body,
-        (whole, *[jax.ShapeDtypeStruct((half, 128), F32)] * 2),
+        (
+            jax.ShapeDtypeStruct((2, channels, width), BF16),
+            *[jax.ShapeDtypeStruct((half, 128), F32)] * 2,
+        ),
         [
             pltpu.VMEM((rows + 4, channels, width), BF16),
             pltpu.VMEM((3 * channels, 3 * channels), F32),
             pltpu.VMEM((2 * half, 128), F32),
             pltpu.VMEM(shape, BF16),
+            pltpu.VMEM(padded, BF16),
+            pltpu.VMEM((group, count, 8, width), F32),
         ],
         flops,
         5 * act_bytes,
-    )(side, back.reshape(native.shape), slope, x)
-    d_before, d_after = edges(dhidden[0], dhidden[-1])
-    input_grad = call(
+    )(side, mine, got, slope, x_before, frame, x_after, cot_tile)
+    d_before, d_after = edges(d_edges[0], d_edges[1])
+    [input_grad] = call(
         input_grad_body,
-        native,
-        [pltpu.VMEM(padded, BF16), part, pltpu.VMEM(shape, F32)],
+        [native],
+        [pltpu.VMEM(padded, BF16), part, pltpu.VMEM(shape, F32), pltpu.VMEM(shape, BF16)],
         flops,
         4 * act_bytes,
-    )(d_before, dhidden, d_after, weight_back, cot)
-    weight_mine = keep + swap_cores(give)
-    packed = jax.ShapeDtypeStruct((count, group * rows + count, width), BF16)
-    along = call(
-        along_body,
-        packed,
-        [pltpu.VMEM((group, count, 8, width), F32)],
-        34 * channels * area,
-        3 * act_bytes,
-    )(coef, cot_tile, act_tile)
-    weight_parts = far_parts(weight_mine, plane)
-    along, *weight_parts = lax.optimization_barrier((along, *weight_parts))
-    along = exchange(along)
-    weight_mine = xor_sum(tree_sum(weight_parts), "tm", list(range(plane)))
-    weight_mine, input_grad = lax.optimization_barrier((weight_mine, input_grad))
-    weight_total = call(
+    )(d_before, d_after, weight_back, got, slope, cot)
+    sums = keep + swap_cores(give)
+    along = exchange(behind(along, sums[:8])).reshape(native.shape)
+    sums = total_over_rest(sums, plane)
+    [block_output] = call(block_output_body, [native], [], channels * area, 3 * act_bytes)(
+        frame, along, along
+    )
+    sums, input_grad = lax.optimization_barrier((sums, input_grad))
+    weight_total, kernel_total = call(
         functools.partial(unpack_body, gscale),
-        jax.ShapeDtypeStruct(spatial_weight.shape, F32),
+        (
+            jax.ShapeDtypeStruct(spatial_weight.shape, F32),
+            jax.ShapeDtypeStruct((count, channels), F32),
+        ),
         [pltpu.VMEM((2 * half, 128), F32)],
         0,
         act_bytes,
-    )(side, weight_mine, swap_cores(weight_mine))
-    kernel_sum = call(
-        kernel_sums_body, jax.ShapeDtypeStruct((count, channels), F32), [], 0, 0
-    )(along)
-    block_output = call(block_output_body, native, [], 0, 0)(frame, along)
-    kernel_total = xor_sum(kernel_sum, "span", list(range(lax.axis_size("span")))) * gscale
+    )(side, sums, swap_cores(sums))
     return (
         block_output[None],
         input_grad[None],

time: 89.4 us -> 83.7 us (0.936)
  blocking collectives: 18.1 us -> 0 us
  waiting for transfers between devices: 28.5 us -> 41.9 us
    all_to_all x1 -> x0, blocking collectives: 18.1 us -> none  [exchange(): return lax.all_to_all(x, 'tm', split_axis=0, concat_axis=0, tiled=True)]
    all_to_all x3, waiting for transfers between devices: 20.5 us -> 36.2 us  [exchange(): return lax.all_to_all(x, 'tm', split_axis=0, concat_axis=0, tiled=True)]
    ppermute x4 -> x6, starting transfers between devices: 3.62 us -> 8.92 us  [xor_sum(): lax.ppermute(x, axis, [(i, i ^ k) for i in range(size)])]
    ppermute x3 -> x0, starting transfers between devices: 4.45 us -> none  [far_parts(): lax.ppermute(mine, 'tm', [(i, i ^ k) for i in range(count)])]
    unnamed x20 -> x14, local copies, waits for them, and re-layouts: 4.86 us -> 3.55 us
    ppermute x4 -> x6, waiting for transfers between devices: 5.49 us -> 4.43 us  [xor_sum(): lax.ppermute(x, axis, [(i, i ^ k) for i in range(size)])]
    all_to_all x3, starting transfers between devices: 17.5 us -> 16.5 us  [exchange(): return lax.all_to_all(x, 'tm', split_axis=0, concat_axis=0, tiled=True)]
    ppermute x3 -> x0, waiting for transfers between devices: 0.96 us -> none  [far_parts(): lax.ppermute(mine, 'tm', [(i, i ^ k) for i in range(count)])]
  transfers between devices with their start and end apart: 14 -> 13, of which waited for: 9 -> 8; matrix products, arithmetic and copies ran while one was open for 1% -> 2% of each run, Pallas kernels for 10% -> 6%
where the time goes in v3:
time: 83.7 us; the launch traced here: 83.2 us
  waiting for transfers between devices  41.9 us (50%)
  starting transfers between devices  25.6 us (31%)
  Pallas kernels  8.9 us (11%)
  local copies, waits for them, and re-layouts  4.92 us (6%)
  other arithmetic  1.02 us (1%)
  between operations  0.88 us (1%)
    all_to_all x3, waiting for transfers between devices, exchange(): return lax.all_to_all(x, 'tm', split_axis=0, concat_axis=0, tiled=True)  36.2 us
    all_to_all x3, starting transfers between devices, exchange(): return lax.all_to_all(x, 'tm', split_axis=0, concat_axis=0, tiled=True)  16.5 us
    ppermute x6, starting transfers between devices, xor_sum(): lax.ppermute(x, axis, [(i, i ^ k) for i in range(size)])  8.92 us
    pallas_call x7, Pallas kernels, run(): pl.pallas_call(body, out_shape=out, in_specs=specs(operands, hbm_in), out...  8.9 us
    ppermute x6, waiting for transfers between devices, xor_sum(): lax.ppermute(x, axis, [(i, i ^ k) for i in range(size)])  4.43 us
    unnamed x14, local copies, waits for them, and re-layouts  3.55 us
  transfers between devices with their start and end apart: 13, of which 8 were waited for; matrix products, arithmetic and copies ran while one was open for 2% of the time, Pallas kernels for 6%

profile of v3, /device:TPU:0, one launch (start us, length us, event | category | flops | bytes accessed | tf_op | source)
XLA Modules:
  0.0 83.2 jit_solution(18347867821620971901)
XLA Ops:
  0.6 0.0 copy-start
  0.6 0.0 copy-start.2
  0.7 8.5 %all-to-all-start = ((bf16[16,4,32,128]{3,2,1,0:T(8,128)(2,1)}), bf16[16,4,32,128]{3,2,1,0:T(8,128)(2,1)S(1)}, u32[]{:S(2)}, u32[]{:S(2)}) async-start(bf16[16,4,32,128]{3,2,1,0:T(8,128)(2,1)} %bitcast.21), calls=%async_computation | async-start | bytes 1048576 | tf_op jit(solution)/shard_map/all_to_all | solution.py:349
  9.1 0.0 copy-done.2
  9.1 0.0 copy-start.5
  9.1 0.2 copy.33
  9.4 0.1 collective-permute-start
  9.5 0.0 copy-done
  9.5 0.1 constant_dynamic-slice_fusion
  9.6 0.1 copy.31
  9.6 0.4 copy-done.5
  10.0 0.1 copy.25
  10.2 0.2 reshape.22.weight_ref
  10.3 0.2 copy.26
  10.5 0.2 reshape.23.weight_ref
  10.7 0.0 collective-permute-done
  10.7 1.5 %shard_map.75 = (bf16[64,32,128]{2,1,0:T(8,128)(2,1)S(1)}, f32[32,64,128]{2,1,0:T(8,128)S(1)}) custom-call(bf16[64,128]{1,0:T(8,128)(2,1)S(1)} %get-tuple-element.29.before_ref, bf16[64,32,128]{2,1,0:T(8,128)(2,1)S(1)} %bitcast.16, bf16[64,128]{1,0:T(8,128)(2,1)S(1)} %get-tuple-element.28.after_ref, bf16[192,192]{1,0:T(8,128)(2,1)S(1)} %reshape.22.weight_ref), custom_call_target="tpu_custom_call" | custom-call | flops 301989888 | bytes 2097152 | tf_op jit(solution)/shard_map/pallas_call | solution.py:23
  12.2 12.1 %all-to-all-done.cot_ref = bf16[16,4,32,128]{3,2,1,0:T(8,128)(2,1)S(1)} async-done(((bf16[16,4,32,128]{3,2,1,0:T(8,128)(2,1)}), bf16[16,4,32,128]{3,2,1,0:T(8,128)(2,1)S(1)}, u32[]{:S(2)}, u32[]{:S(2)}) %all-to-all-start) | async-done | bytes 524320 | tf_op jit(solution)/shard_map/all_to_all | solution.py:349
  24.3 0.1 broadcast_in_dim.15.coef_ref
  24.3 0.7 shard_map.76
  25.1 0.0 copy-start.3
  25.1 1.0 %copy-done.3 = bf16[16,2,4,32,128]{4,3,2,1,0:T(8,128)(2,1)} copy-done((bf16[16,2,4,32,128]{4,3,2,1,0:T(8,128)(2,1)}, bf16[16,2,4,32,128]{4,3,2,1,0:T(8,128)(2,1)S(1)}, u32[]{:S(2)}) %copy-start.3) | copy-done | bytes 1048600
  26.1 3.9 %all-to-all-start.1 = ((bf16[16,2,4,32,128]{4,3,2,1,0:T(8,128)(2,1)}), bf16[16,2,4,32,128]{4,3,2,1,0:T(8,128)(2,1)S(1)}, u32[]{:S(2)}, u32[]{:S(2)}) async-start(bf16[16,2,4,32,128]{4,3,2,1,0:T(8,128)(2,1)} %copy-done.3), calls=%async_computation.1 | async-start | bytes 2097152 | tf_op jit(solution)/shard_map/all_to_all | solution.py:349
  30.0 23.7 %all-to-all-done.1.got_ref = bf16[16,2,4,32,128]{4,3,2,1,0:T(8,128)(2,1)S(1)} async-done(((bf16[16,2,4,32,128]{4,3,2,1,0:T(8,128)(2,1)}), bf16[16,2,4,32,128]{4,3,2,1,0:T(8,128)(2,1)S(1)}, u32[]{:S(2)}, u32[]{:S(2)}) %all-to-all-start.1) | async-done | bytes 1048608 | tf_op jit(solution)/shard_map/all_to_all | solution.py:349
  53.7 2.0 %shard_map.78 = (bf16[2,64,128]{2,1,0:T(8,128)(2,1)S(1)}, f32[152,128]{1,0:T(8,128)S(1)}, f32[152,128]{1,0:T(8,128)S(1)}) custom-call(f32[8,128]{1,0:T(8,128)S(1)} %broadcast_in_dim.16.side_ref, s32[8,128]{1,0:T(8,128)S(1)} %iota.7.mine_ref, bf16[16,2,4,32,128]{4,3,2,1,0:T(8,128)(2,1)S(1)} %all-to-all-done.1.got_ref, ...), custom_call_target="tpu_custom_call" | custom-call | flops 301989888 | bytes 2621440 | tf_op jit(solution)/shard_map/pallas_call | solution.py:23
  55.7 0.0 collective-permute-start.1
  55.7 0.7 shard_map.77.x_ref
  56.4 0.0 copy-start.1
  56.5 0.8 copy-done.1
  57.2 0.0 collective-permute-done.1
  57.3 0.6 slice.22.other_ref
  57.9 2.8 %collective-permute-start.3 = (f32[152,128]{1,0:T(8,128)S(1)}, f32[152,128]{1,0:T(8,128)S(1)}, u32[]{:S(2)}, u32[]{:S(2)}) collective-permute-start(f32[152,128]{1,0:T(8,128)S(1)} %add.30), channel_id=1, source_target_pairs={{0,16},{2,18},{4,20},{6,22},{8,24},{10,26},{12,28},{14,30},{16,0},... | collective-permute-start | bytes 233480 | tf_op jit(solution)/shard_map/ppermute | solution.py:312
  60.6 2.6 %collective-permute-start.4 = (f32[152,128]{1,0:T(8,128)S(1)}, f32[152,128]{1,0:T(8,128)}, u32[]{:S(2)}, u32[]{:S(2)}) collective-permute-start(f32[152,128]{1,0:T(8,128)S(1)} %add.30), channel_id=1, source_target_pairs={{0,24},{2,26},{4,28},{6,30},{8,16},{10,18},{12,20},{14,22},{16,8},... | collective-permute-start | bytes 233480 | tf_op jit(solution)/shard_map/ppermute | solution.py:312
  63.2 0.0 collective-permute-start.2
  63.2 4.1 %all-to-all-start.2 = ((bf16[16,4,32,128]{3,2,1,0:T(8,128)(2,1)}), bf16[16,4,32,128]{3,2,1,0:T(8,128)(2,1)S(1)}, u32[]{:S(2)}, u32[]{:S(2)}) async-start(bf16[16,4,32,128]{3,2,1,0:T(8,128)(2,1)} %shard_map.79), calls=%async_computation.2 | async-start | bytes 1048576 | tf_op jit(solution)/shard_map/all_to_all | solution.py:349
  67.3 0.1 collective-permute-start.8
  67.4 0.0 collective-permute-done.3
  67.4 0.7 collective-permute-done.4
  68.2 1.0 %collective-permute-done.2 = f32[152,128]{1,0:T(8,128)} collective-permute-done((f32[152,128]{1,0:T(8,128)S(1)}, f32[152,128]{1,0:T(8,128)}, u32[]{:S(2)}, u32[]{:S(2)}) %collective-permute-start.2) | collective-permute-done | bytes 77856 | tf_op jit(solution)/shard_map/ppermute | solution.py:312
  69.1 0.9 %add_add_fusion.1 = f32[152,128]{1,0:T(8,128)S(1)} fusion(f32[152,128]{1,0:T(8,128)S(1)} %collective-permute-done.3, f32[152,128]{1,0:T(8,128)} %collective-permute-done.4, f32[152,128]{1,0:T(8,128)S(1)} %add.30, f32[152,128]{1,0:T(8,128)} %collective-permute-done.2), kind=kLoop, calls=%fused_computation.2 | loop fusion | flops 58368 | bytes 389120 | tf_op jit(solution)/shard_map/add | solution.py:306
  70.1 1.3 %collective-permute-start.6 = (f32[152,128]{1,0:T(8,128)S(1)}, f32[152,128]{1,0:T(8,128)S(1)}, u32[]{:S(2)}, u32[]{:S(2)}) collective-permute-start(f32[152,128]{1,0:T(8,128)S(1)} %add_add_fusion.1), channel_id=1, source_target_pairs={{0,4},{2,6},{4,0},{6,2},{8,12},{10,14},{12,8},{14,10},{16,20},{18,... | collective-permute-start | bytes 233480 | tf_op jit(solution)/shard_map/ppermute | solution.py:312
  71.4 1.0 %collective-permute-start.7 = (f32[152,128]{1,0:T(8,128)S(1)}, f32[152,128]{1,0:T(8,128)S(1)}, u32[]{:S(2)}, u32[]{:S(2)}) collective-permute-start(f32[152,128]{1,0:T(8,128)S(1)} %add_add_fusion.1), channel_id=1, source_target_pairs={{0,6},{2,4},{4,2},{6,0},{8,14},{10,12},{12,10},{14,8},{16,22},{18,... | collective-permute-start | bytes 233480 | tf_op jit(solution)/shard_map/ppermute | solution.py:312
  72.4 1.3 %collective-permute-start.5 = (f32[152,128]{1,0:T(8,128)S(1)}, f32[152,128]{1,0:T(8,128)S(1)}, u32[]{:S(2)}, u32[]{:S(2)}) collective-permute-start(f32[152,128]{1,0:T(8,128)S(1)} %add_add_fusion.1), channel_id=1, source_target_pairs={{0,2},{2,0},{4,6},{6,4},{8,10},{10,8},{12,14},{14,12},{16,18},{18,... | collective-permute-start | bytes 233480 | tf_op jit(solution)/shard_map/ppermute | solution.py:312
  73.6 0.0 collective-permute-done.8
  73.6 0.0 copy-start.4
  73.7 1.0 %copy-done.4 = bf16[1,64,32,128]{3,2,1,0:T(8,128)(2,1)S(1)} copy-done((bf16[1,64,32,128]{3,2,1,0:T(8,128)(2,1)S(1)}, bf16[1,64,32,128]{3,2,1,0:T(8,128)(2,1)}, u32[]{:S(2)}) %copy-start.4) | copy-done | bytes 524312
  74.7 2.2 %shard_map.81 = bf16[64,32,128]{2,1,0:T(8,128)(2,1)} custom-call(bf16[64,128]{1,0:T(8,128)(2,1)S(1)} %get-tuple-element.27.before_ref, bf16[64,128]{1,0:T(8,128)(2,1)S(1)} %get-tuple-element.26.after_ref, bf16[192,192]{1,0:T(8,128)(2,1)S(1)} %reshape.23.weight_ref, bf16[16,2,4,32,128]{4,3,2,1,0:T(8,128)(2,1)S(1)} %all-to-all-done.1.got_ref, ...), custom_call_target="tpu_custom_call" | custom-call | flops 301989888 | bytes 2097152 | tf_op jit(solution)/shard_map/pallas_call | solution.py:23
  76.9 0.0 collective-permute-done.6
  76.9 2.6 %collective-permute-done.7 = f32[152,128]{1,0:T(8,128)S(1)} collective-permute-done((f32[152,128]{1,0:T(8,128)S(1)}, f32[152,128]{1,0:T(8,128)S(1)}, u32[]{:S(2)}, u32[]{:S(2)}) %collective-permute-start.7) | collective-permute-done | bytes 77856 | tf_op jit(solution)/shard_map/ppermute | solution.py:312
  79.5 0.2 collective-permute-done.5
  79.7 0.1 collective-permute-start.9
  79.8 1.3 %collective-permute-done.9.other_ref = f32[152,128]{1,0:T(8,128)S(1)} collective-permute-done((f32[152,128]{1,0:T(8,128)S(1)}, f32[152,128]{1,0:T(8,128)S(1)}, u32[]{:S(2)}, u32[]{:S(2)}) %collective-permute-start.9) | collective-permute-done | bytes 77856 | tf_op jit(solution)/shard_map/ppermute | solution.py:317
  81.0 0.8 shard_map.82
  81.9 0.4 all-to-all-done.2
  82.3 0.9 %shard_map.80 = bf16[64,32,128]{2,1,0:T(8,128)(2,1)} custom-call(bf16[64,32,128]{2,1,0:T(8,128)(2,1)S(1)} %bitcast.18, bf16[64,32,128]{2,1,0:T(8,128)(2,1)S(1)} %bitcast.19, bf16[64,32,128]{2,1,0:T(8,128)(2,1)S(1)} %bitcast.20), custom_call_target="tpu_custom_call" | custom-call | flops 262144 | bytes 1572864 | tf_op jit(solution)/shard_map/pallas_call | solution.py:23
  (10 shorter events, 0.1 us)
Async XLA Ops:
  0.6 8.8 %copy-start = (bf16[64,16]{0,1:T(8,128)(2,1)S(1)}, bf16[64,16]{0,1:T(8,128)(2,1)}, u32[]{:S(2)}) copy-start(bf16[64,16]{0,1:T(8,128)(2,1)} %param.7) | copy-start | bytes 6148
  0.6 8.5 %copy-start.2 = (bf16[1,64,32,128]{3,2,1,0:T(8,128)(2,1)S(1)}, bf16[1,64,32,128]{3,2,1,0:T(8,128)(2,1)}, u32[]{:S(2)}) copy-start(bf16[1,64,32,128]{3,2,1,0:T(8,128)(2,1)} %param.4) | copy-start | bytes 1572868
  0.7 23.6 %all-to-all-start = ((bf16[16,4,32,128]{3,2,1,0:T(8,128)(2,1)}), bf16[16,4,32,128]{3,2,1,0:T(8,128)(2,1)S(1)}, u32[]{:S(2)}, u32[]{:S(2)}) async-start(bf16[16,4,32,128]{3,2,1,0:T(8,128)(2,1)} %bitcast.21), calls=%async_computation | async-start | bytes 1048576 | tf_op jit(solution)/shard_map/all_to_all | solution.py:349
  9.1 0.9 %copy-start.5 = (bf16[3,3,64,64]{3,2,1,0:T(8,128)(2,1)S(1)}, bf16[3,3,64,64]{3,2,1,0:T(8,128)(2,1)}, u32[]{:S(2)}) copy-start(bf16[3,3,64,64]{3,2,1,0:T(8,128)(2,1)} %param.6) | copy-start | bytes 221188
  9.4 1.3 %collective-permute-start = (bf16[64,128]{1,0:T(8,128)(2,1)S(1)}, bf16[64,128]{1,0:T(8,128)(2,1)S(1)}, u32[]{:S(2)}, u32[]{:S(2)}) collective-permute-start(bf16[64,128]{1,0:T(8,128)(2,1)S(1)} %fusion), channel_id=1, source_target_pairs={{0,1},{1,0},{2,3},{3,2},{4,5},{5,4},{6,7},{7,6},{8,9},{9,8},{10,11... | collective-permute-start | bytes 49160 | tf_op jit(solution)/shard_map/ppermute | solution.py:317
  25.1 1.0 %copy-start.3 = (bf16[16,2,4,32,128]{4,3,2,1,0:T(8,128)(2,1)}, bf16[16,2,4,32,128]{4,3,2,1,0:T(8,128)(2,1)S(1)}, u32[]{:S(2)}) copy-start(bf16[16,2,4,32,128]{4,3,2,1,0:T(8,128)(2,1)S(1)} %shard_map.76) | copy-start | bytes 3145732
  26.1 27.6 %all-to-all-start.1 = ((bf16[16,2,4,32,128]{4,3,2,1,0:T(8,128)(2,1)}), bf16[16,2,4,32,128]{4,3,2,1,0:T(8,128)(2,1)S(1)}, u32[]{:S(2)}, u32[]{:S(2)}) async-start(bf16[16,2,4,32,128]{4,3,2,1,0:T(8,128)(2,1)} %copy-done.3), calls=%async_computation.1 | async-start | bytes 2097152 | tf_op jit(solution)/shard_map/all_to_all | solution.py:349
  55.7 1.5 %collective-permute-start.1 = (f32[152,128]{1,0:T(8,128)S(1)}, f32[152,128]{1,0:T(8,128)S(1)}, u32[]{:S(2)}, u32[]{:S(2)}) collective-permute-start(f32[152,128]{1,0:T(8,128)S(1)} %get-tuple-element.19), channel_id=1, source_target_pairs={{0,1},{1,0},{2,3},{3,2},{4,5},{5,4},{6,7},{7,6},{8,9},{9,8},{10,11... | collective-permute-start | bytes 233480 | tf_op jit(solution)/shard_map/ppermute | solution.py:317
  56.4 0.8 copy-start.1
  57.9 9.6 %collective-permute-start.3 = (f32[152,128]{1,0:T(8,128)S(1)}, f32[152,128]{1,0:T(8,128)S(1)}, u32[]{:S(2)}, u32[]{:S(2)}) collective-permute-start(f32[152,128]{1,0:T(8,128)S(1)} %add.30), channel_id=1, source_target_pairs={{0,16},{2,18},{4,20},{6,22},{8,24},{10,26},{12,28},{14,30},{16,0},... | collective-permute-start | bytes 233480 | tf_op jit(solution)/shard_map/ppermute | solution.py:312
  60.6 7.6 %collective-permute-start.4 = (f32[152,128]{1,0:T(8,128)S(1)}, f32[152,128]{1,0:T(8,128)}, u32[]{:S(2)}, u32[]{:S(2)}) collective-permute-start(f32[152,128]{1,0:T(8,128)S(1)} %add.30), channel_id=1, source_target_pairs={{0,24},{2,26},{4,28},{6,30},{8,16},{10,18},{12,20},{14,22},{16,8},... | collective-permute-start | bytes 233480 | tf_op jit(solution)/shard_map/ppermute | solution.py:312
  63.2 5.9 %collective-permute-start.2 = (f32[152,128]{1,0:T(8,128)S(1)}, f32[152,128]{1,0:T(8,128)}, u32[]{:S(2)}, u32[]{:S(2)}) collective-permute-start(f32[152,128]{1,0:T(8,128)S(1)} %add.30), channel_id=1, source_target_pairs={{0,8},{2,10},{4,12},{6,14},{8,0},{10,2},{12,4},{14,6},{16,24},{18,... | collective-permute-start | bytes 233480 | tf_op jit(solution)/shard_map/ppermute | solution.py:312
  63.2 19.1 %all-to-all-start.2 = ((bf16[16,4,32,128]{3,2,1,0:T(8,128)(2,1)}), bf16[16,4,32,128]{3,2,1,0:T(8,128)(2,1)S(1)}, u32[]{:S(2)}, u32[]{:S(2)}) async-start(bf16[16,4,32,128]{3,2,1,0:T(8,128)(2,1)} %shard_map.79), calls=%async_computation.2 | async-start | bytes 1048576 | tf_op jit(solution)/shard_map/all_to_all | solution.py:349
  67.3 6.3 %collective-permute-start.8 = (bf16[64,128]{1,0:T(8,128)(2,1)S(1)}, bf16[64,128]{1,0:T(8,128)(2,1)S(1)}, u32[]{:S(2)}, u32[]{:S(2)}) collective-permute-start(bf16[64,128]{1,0:T(8,128)(2,1)S(1)} %select_bitcast_fusion), channel_id=1, source_target_pairs={{0,1},{1,0},{2,3},{3,2},{4,5},{5,4},{6,7},{7,6},{8,9},{9,8},{10,11... | collective-permute-start | bytes 49160 | tf_op jit(solution)/shard_map/ppermute | solution.py:317
  70.1 6.9 %collective-permute-start.6 = (f32[152,128]{1,0:T(8,128)S(1)}, f32[152,128]{1,0:T(8,128)S(1)}, u32[]{:S(2)}, u32[]{:S(2)}) collective-permute-start(f32[152,128]{1,0:T(8,128)S(1)} %add_add_fusion.1), channel_id=1, source_target_pairs={{0,4},{2,6},{4,0},{6,2},{8,12},{10,14},{12,8},{14,10},{16,20},{18,... | collective-permute-start | bytes 233480 | tf_op jit(solution)/shard_map/ppermute | solution.py:312
  71.4 8.1 %collective-permute-start.7 = (f32[152,128]{1,0:T(8,128)S(1)}, f32[152,128]{1,0:T(8,128)S(1)}, u32[]{:S(2)}, u32[]{:S(2)}) collective-permute-start(f32[152,128]{1,0:T(8,128)S(1)} %add_add_fusion.1), channel_id=1, source_target_pairs={{0,6},{2,4},{4,2},{6,0},{8,14},{10,12},{12,10},{14,8},{16,22},{18,... | collective-permute-start | bytes 233480 | tf_op jit(solution)/shard_map/ppermute | solution.py:312
  72.4 7.3 %collective-permute-start.5 = (f32[152,128]{1,0:T(8,128)S(1)}, f32[152,128]{1,0:T(8,128)S(1)}, u32[]{:S(2)}, u32[]{:S(2)}) collective-permute-start(f32[152,128]{1,0:T(8,128)S(1)} %add_add_fusion.1), channel_id=1, source_target_pairs={{0,2},{2,0},{4,6},{6,4},{8,10},{10,8},{12,14},{14,12},{16,18},{18,... | collective-permute-start | bytes 233480 | tf_op jit(solution)/shard_map/ppermute | solution.py:312
  73.6 1.0 %copy-start.4 = (bf16[1,64,32,128]{3,2,1,0:T(8,128)(2,1)S(1)}, bf16[1,64,32,128]{3,2,1,0:T(8,128)(2,1)}, u32[]{:S(2)}) copy-start(bf16[1,64,32,128]{3,2,1,0:T(8,128)(2,1)} %param.5) | copy-start | bytes 1572868
  79.7 1.3 %collective-permute-start.9 = (f32[152,128]{1,0:T(8,128)S(1)}, f32[152,128]{1,0:T(8,128)S(1)}, u32[]{:S(2)}, u32[]{:S(2)}) collective-permute-start(f32[152,128]{1,0:T(8,128)S(1)} %add_add_fusion.mine_ref), channel_id=1, source_target_pairs={{0,1},{1,0},{2,3},{3,2},{4,5},{5,4},{6,7},{7,6},{8,9},{9,8},{10,11... | collective-permute-start | bytes 233480 | tf_op jit(solution)/shard_map/ppermute | solution.py:317

commit v4 on v3

--- a/solution.py
+++ b/solution.py
@@ -214,24 +214,17 @@
     dhidden_rows(got_ref, slope_ref, turn_ref, dpad_ref, 2)
     edge_ref[0] = dpad_ref[2]
     edge_ref[1] = dpad_ref[rows + 1]
-    grad_ref[...] = jnp.zeros_like(grad_ref)
-
-    def two(step, carry):
-        left, right = [], []
-        for k in range(2):
-            row = 2 * step + k
-            x = pad_ref[row]
-            right.append(jnp.concatenate([shifted(x, True), x, shifted(x, False)], axis=0))
-            left.append(jnp.concatenate([dpad_ref[row + 2], dpad_ref[row + 1], dpad_ref[row]], axis=0))
-        grad_ref[...] += lax.dot_general(
-            jnp.concatenate(left, axis=1),
-            jnp.concatenate(right, axis=1),
-            (((1,), (1,)), ((), ())),
-            preferred_element_type=F32,
-        )
-        return carry
-
-    lax.fori_loop(0, (rows + 2) // 2, two, 0, unroll=True)
+    left, right = [], []
+    for row in range(rows + 2):
+        x = pad_ref[row]
+        right.append(jnp.concatenate([shifted(x, True), x, shifted(x, False)], axis=0))
+        left.append(jnp.concatenate([dpad_ref[row + 2], dpad_ref[row + 1], dpad_ref[row]], axis=0))
+    grad_ref[...] = lax.dot_general(
+        jnp.concatenate(left, axis=1),
+        jnp.concatenate(right, axis=1),
+        (((1,), (1,)), ((), ())),
+        preferred_element_type=F32,
+    )
     tall = 3 * channels
     pack_ref[pl.ds(0, tall)] = grad_ref[:, : 2 * channels]
     pack_ref[pl.ds(tall, tall // 2)] = jnp.concatenate(
@@ -275,20 +268,6 @@
     kernel_ref[pl.ds(lags, lags)] = sums[:, channels:]
 
 
-def behind(x, other):
-    def body(x_ref, other_ref, out_ref):
-        pass
-
-    anywhere = pl.BlockSpec(memory_space=pl.ANY)
-    return pl.pallas_call(
-        body,
-        out_shape=jax.ShapeDtypeStruct(x.shape, x.dtype),
-        in_specs=[anywhere, anywhere],
-        out_specs=anywhere,
-        input_output_aliases={0: 0},
-    )(x, other)
-
-
 def edges(first, last):
     size = lax.axis_size("span")
     if size == 2:
@@ -317,13 +296,13 @@
     return lax.ppermute(x, "span", [(i, i ^ 1) for i in range(size)])
 
 
-def total_over_rest(mine, plane):
+def over_planes(mine, plane):
     size = lax.axis_size("span")
     count = lax.axis_size("tm")
     if size > 2:
         mine = xor_sum(mine, "span", list(range(0, size, 2)))
-    mine = xor_sum(mine, "tm", list(range(0, count, plane)))
-    return xor_sum(mine, "tm", list(range(plane)))
+    steps = range(plane, count, plane)
+    return [mine] + [lax.ppermute(mine, "tm", [(i, i ^ k) for i in range(count)]) for k in steps]
 
 
 def local(frames, cotangent, spatial_weight, temporal_kernel):
@@ -400,9 +379,11 @@
         flops,
         4 * act_bytes,
     )(d_before, d_after, weight_back, got, slope, cot)
-    sums = keep + swap_cores(give)
-    along = exchange(behind(along, sums[:8])).reshape(native.shape)
-    sums = total_over_rest(sums, plane)
+    received = swap_cores(give)
+    planes = over_planes(keep + received, plane)
+    along, received = lax.optimization_barrier((along, received))
+    along = exchange(along).reshape(native.shape)
+    sums = xor_sum(tree_sum(planes), "tm", list(range(plane)))
     [block_output] = call(block_output_body, [native], [], channels * area, 3 * act_bytes)(
         frame, along, along
     )

time: 83.7 us -> 83 us (level)
    ppermute x0 -> x3, starting transfers between devices: none -> 5.43 us  [over_planes(): lax.ppermute(mine, 'tm', [(i, i ^ k) for i in range(count)])]
    ppermute x6 -> x3, starting transfers between devices: 8.92 us -> 3.55 us  [xor_sum(): lax.ppermute(x, axis, [(i, i ^ k) for i in range(size)])]
    ppermute x0 -> x3, waiting for transfers between devices: none -> 1.69 us  [over_planes(): lax.ppermute(mine, 'tm', [(i, i ^ k) for i in range(count)])]
    ppermute x6 -> x3, waiting for transfers between devices: 4.43 us -> 2.74 us  [xor_sum(): lax.ppermute(x, axis, [(i, i ^ k) for i in range(size)])]
where the time goes in v4:
time: 83 us; the launch traced here: 82.5 us
  waiting for transfers between devices  41.9 us (50%)
  starting transfers between devices  25.7 us (31%)
  Pallas kernels  8.76 us (11%)
  local copies, waits for them, and re-layouts  4.33 us (5%)
  other arithmetic  1.02 us (1%)
  between operations  0.87 us (1%)
    all_to_all x3, waiting for transfers between devices, exchange(): return lax.all_to_all(x, 'tm', split_axis=0, concat_axis=0, tiled=True)  36.2 us
    all_to_all x3, starting transfers between devices, exchange(): return lax.all_to_all(x, 'tm', split_axis=0, concat_axis=0, tiled=True)  16.5 us
    pallas_call x7, Pallas kernels, run(): pl.pallas_call(body, out_shape=out, in_specs=specs(operands, hbm_in), out...  8.76 us
    ppermute x3, starting transfers between devices, over_planes(): lax.ppermute(mine, 'tm', [(i, i ^ k) for i in range(count)])  5.43 us
    unnamed x14, local copies, waits for them, and re-layouts  3.55 us
    ppermute x3, starting transfers between devices, xor_sum(): lax.ppermute(x, axis, [(i, i ^ k) for i in range(size)])  3.55 us
    ppermute x3, waiting for transfers between devices, xor_sum(): lax.ppermute(x, axis, [(i, i ^ k) for i in range(size)])  2.74 us
    ppermute x3, waiting for transfers between devices, over_planes(): lax.ppermute(mine, 'tm', [(i, i ^ k) for i in range(count)])  1.69 us
  transfers between devices with their start and end apart: 13, of which 8 were waited for; matrix products, arithmetic and copies ran while one was open for 2% of the time, Pallas kernels for 6%

profile of v4, /device:TPU:0, one launch (start us, length us, event | category | flops | bytes accessed | tf_op | source)
XLA Modules:
  0.0 82.5 jit_solution(5927797289174065020)
XLA Ops:
  0.6 0.0 copy-start
  0.6 0.0 copy-start.1
  0.7 8.5 %all-to-all-start = ((bf16[16,4,32,128]{3,2,1,0:T(8,128)(2,1)}), bf16[16,4,32,128]{3,2,1,0:T(8,128)(2,1)S(1)}, u32[]{:S(2)}, u32[]{:S(2)}) async-start(bf16[16,4,32,128]{3,2,1,0:T(8,128)(2,1)} %bitcast.21), calls=%async_computation | async-start | bytes 1048576 | tf_op jit(solution)/shard_map/all_to_all | solution.py:328
  9.1 0.0 copy-done.1
  9.1 0.0 copy-start.5
  9.1 0.2 copy.32
  9.4 0.1 collective-permute-start
  9.5 0.0 copy-done
  9.5 0.1 constant_dynamic-slice_fusion
  9.6 0.1 copy.30
  9.6 0.4 copy-done.5
  10.0 0.1 copy.24
  10.2 0.2 reshape.22.weight_ref
  10.3 0.2 copy.25
  10.5 0.2 reshape.23.weight_ref
  10.7 0.0 collective-permute-done
  10.7 1.5 %shard_map.75 = (bf16[64,32,128]{2,1,0:T(8,128)(2,1)S(1)}, f32[32,64,128]{2,1,0:T(8,128)S(1)}) custom-call(bf16[64,128]{1,0:T(8,128)(2,1)S(1)} %get-tuple-element.31.before_ref, bf16[64,32,128]{2,1,0:T(8,128)(2,1)S(1)} %bitcast.16, bf16[64,128]{1,0:T(8,128)(2,1)S(1)} %get-tuple-element.30.after_ref, bf16[192,192]{1,0:T(8,128)(2,1)S(1)} %reshape.22.weight_ref), custom_call_target="tpu_custom_call" | custom-call | flops 301989888 | bytes 2097152 | tf_op jit(solution)/shard_map/pallas_call | solution.py:23
  12.2 12.1 %all-to-all-done.cot_ref = bf16[16,4,32,128]{3,2,1,0:T(8,128)(2,1)S(1)} async-done(((bf16[16,4,32,128]{3,2,1,0:T(8,128)(2,1)}), bf16[16,4,32,128]{3,2,1,0:T(8,128)(2,1)S(1)}, u32[]{:S(2)}, u32[]{:S(2)}) %all-to-all-start) | async-done | bytes 524320 | tf_op jit(solution)/shard_map/all_to_all | solution.py:328
  24.3 0.1 broadcast_in_dim.15.coef_ref
  24.3 0.7 shard_map.76
  25.1 0.0 copy-start.2
  25.1 1.0 %copy-done.2 = bf16[16,2,4,32,128]{4,3,2,1,0:T(8,128)(2,1)} copy-done((bf16[16,2,4,32,128]{4,3,2,1,0:T(8,128)(2,1)}, bf16[16,2,4,32,128]{4,3,2,1,0:T(8,128)(2,1)S(1)}, u32[]{:S(2)}) %copy-start.2) | copy-done | bytes 1048600
  26.1 3.9 %all-to-all-start.1 = ((bf16[16,2,4,32,128]{4,3,2,1,0:T(8,128)(2,1)}), bf16[16,2,4,32,128]{4,3,2,1,0:T(8,128)(2,1)S(1)}, u32[]{:S(2)}, u32[]{:S(2)}) async-start(bf16[16,2,4,32,128]{4,3,2,1,0:T(8,128)(2,1)} %copy-done.2), calls=%async_computation.1 | async-start | bytes 2097152 | tf_op jit(solution)/shard_map/all_to_all | solution.py:328
  30.0 23.7 %all-to-all-done.1.got_ref = bf16[16,2,4,32,128]{4,3,2,1,0:T(8,128)(2,1)S(1)} async-done(((bf16[16,2,4,32,128]{4,3,2,1,0:T(8,128)(2,1)}), bf16[16,2,4,32,128]{4,3,2,1,0:T(8,128)(2,1)S(1)}, u32[]{:S(2)}, u32[]{:S(2)}) %all-to-all-start.1) | async-done | bytes 1048608 | tf_op jit(solution)/shard_map/all_to_all | solution.py:328
  53.7 1.9 %shard_map.78 = (bf16[2,64,128]{2,1,0:T(8,128)(2,1)S(1)}, f32[152,128]{1,0:T(8,128)S(1)}, f32[152,128]{1,0:T(8,128)S(1)}) custom-call(f32[8,128]{1,0:T(8,128)S(1)} %broadcast_in_dim.16.side_ref, s32[8,128]{1,0:T(8,128)S(1)} %iota.7.mine_ref, bf16[16,2,4,32,128]{4,3,2,1,0:T(8,128)(2,1)S(1)} %all-to-all-done.1.got_ref, ...), custom_call_target="tpu_custom_call" | custom-call | flops 301989888 | bytes 2621440 | tf_op jit(solution)/shard_map/pallas_call | solution.py:23
  55.5 0.0 collective-permute-start.1
  55.6 0.7 shard_map.77
  56.3 0.0 copy-start.4
  56.3 0.8 copy-done.4
  57.1 0.0 collective-permute-done.1
  57.1 2.8 %collective-permute-start.3 = (f32[152,128]{1,0:T(8,128)S(1)}, f32[152,128]{1,0:T(8,128)S(1)}, u32[]{:S(2)}, u32[]{:S(2)}) collective-permute-start(f32[152,128]{1,0:T(8,128)S(1)} %add.30), channel_id=1, source_target_pairs={{0,16},{2,18},{4,20},{6,22},{8,24},{10,26},{12,28},{14,30},{16,0},... | collective-permute-start | bytes 233480 | tf_op jit(solution)/shard_map/ppermute | solution.py:305
  59.9 2.6 %collective-permute-start.4 = (f32[152,128]{1,0:T(8,128)S(1)}, f32[152,128]{1,0:T(8,128)}, u32[]{:S(2)}, u32[]{:S(2)}) collective-permute-start(f32[152,128]{1,0:T(8,128)S(1)} %add.30), channel_id=1, source_target_pairs={{0,24},{2,26},{4,28},{6,30},{8,16},{10,18},{12,20},{14,22},{16,8},... | collective-permute-start | bytes 233480 | tf_op jit(solution)/shard_map/ppermute | solution.py:305
  62.5 0.0 collective-permute-start.2
  62.5 4.1 %all-to-all-start.2 = ((bf16[16,4,32,128]{3,2,1,0:T(8,128)(2,1)}), bf16[16,4,32,128]{3,2,1,0:T(8,128)(2,1)S(1)}, u32[]{:S(2)}, u32[]{:S(2)}) async-start(bf16[16,4,32,128]{3,2,1,0:T(8,128)(2,1)} %copy-done.4), calls=%async_computation.2 | async-start | bytes 1048576 | tf_op jit(solution)/shard_map/all_to_all | solution.py:328
  66.7 0.1 collective-permute-start.8
  66.8 0.0 collective-permute-done.3
  66.8 0.7 collective-permute-done.4
  67.5 1.0 %collective-permute-done.2 = f32[152,128]{1,0:T(8,128)} collective-permute-done((f32[152,128]{1,0:T(8,128)S(1)}, f32[152,128]{1,0:T(8,128)}, u32[]{:S(2)}, u32[]{:S(2)}) %collective-permute-start.2) | collective-permute-done | bytes 77856 | tf_op jit(solution)/shard_map/ppermute | solution.py:305
  68.5 0.9 %add_add_fusion.1 = f32[152,128]{1,0:T(8,128)S(1)} fusion(f32[152,128]{1,0:T(8,128)S(1)} %collective-permute-done.3, f32[152,128]{1,0:T(8,128)} %collective-permute-done.4, f32[152,128]{1,0:T(8,128)S(1)} %add.30, f32[152,128]{1,0:T(8,128)} %collective-permute-done.2), kind=kLoop, calls=%fused_computation.2 | loop fusion | flops 58368 | bytes 389120 | tf_op jit(solution)/shard_map/add | solution.py:285
  69.4 1.3 %collective-permute-start.6 = (f32[152,128]{1,0:T(8,128)S(1)}, f32[152,128]{1,0:T(8,128)S(1)}, u32[]{:S(2)}, u32[]{:S(2)}) collective-permute-start(f32[152,128]{1,0:T(8,128)S(1)} %add_add_fusion.1), channel_id=1, source_target_pairs={{0,4},{2,6},{4,0},{6,2},{8,12},{10,14},{12,8},{14,10},{16,20},{18,... | collective-permute-start | bytes 233480 | tf_op jit(solution)/shard_map/ppermute | solution.py:291
  70.7 1.0 %collective-permute-start.7 = (f32[152,128]{1,0:T(8,128)S(1)}, f32[152,128]{1,0:T(8,128)S(1)}, u32[]{:S(2)}, u32[]{:S(2)}) collective-permute-start(f32[152,128]{1,0:T(8,128)S(1)} %add_add_fusion.1), channel_id=1, source_target_pairs={{0,6},{2,4},{4,2},{6,0},{8,14},{10,12},{12,10},{14,8},{16,22},{18,... | collective-permute-start | bytes 233480 | tf_op jit(solution)/shard_map/ppermute | solution.py:291
  71.7 1.3 %collective-permute-start.5 = (f32[152,128]{1,0:T(8,128)S(1)}, f32[152,128]{1,0:T(8,128)S(1)}, u32[]{:S(2)}, u32[]{:S(2)}) collective-permute-start(f32[152,128]{1,0:T(8,128)S(1)} %add_add_fusion.1), channel_id=1, source_target_pairs={{0,2},{2,0},{4,6},{6,4},{8,10},{10,8},{12,14},{14,12},{16,18},{18,... | collective-permute-start | bytes 233480 | tf_op jit(solution)/shard_map/ppermute | solution.py:291
  73.0 0.0 collective-permute-done.8
  73.0 0.0 copy-start.3
  73.0 1.0 %copy-done.3 = bf16[1,64,32,128]{3,2,1,0:T(8,128)(2,1)S(1)} copy-done((bf16[1,64,32,128]{3,2,1,0:T(8,128)(2,1)S(1)}, bf16[1,64,32,128]{3,2,1,0:T(8,128)(2,1)}, u32[]{:S(2)}) %copy-start.3) | copy-done | bytes 524312
  74.0 2.2 %shard_map.80 = bf16[64,32,128]{2,1,0:T(8,128)(2,1)} custom-call(bf16[64,128]{1,0:T(8,128)(2,1)S(1)} %get-tuple-element.29.before_ref, bf16[64,128]{1,0:T(8,128)(2,1)S(1)} %get-tuple-element.28.after_ref, bf16[192,192]{1,0:T(8,128)(2,1)S(1)} %reshape.23.weight_ref, bf16[16,2,4,32,128]{4,3,2,1,0:T(8,128)(2,1)S(1)} %all-to-all-done.1.got_ref, ...), custom_call_target="tpu_custom_call" | custom-call | flops 301989888 | bytes 2097152 | tf_op jit(solution)/shard_map/pallas_call | solution.py:23
  76.3 0.0 collective-permute-done.6
  76.3 2.6 %collective-permute-done.7 = f32[152,128]{1,0:T(8,128)S(1)} collective-permute-done((f32[152,128]{1,0:T(8,128)S(1)}, f32[152,128]{1,0:T(8,128)S(1)}, u32[]{:S(2)}, u32[]{:S(2)}) %collective-permute-start.7) | collective-permute-done | bytes 77856 | tf_op jit(solution)/shard_map/ppermute | solution.py:291
  78.8 0.2 collective-permute-done.5
  79.0 0.1 collective-permute-start.9
  79.1 1.3 %collective-permute-done.9.other_ref = f32[152,128]{1,0:T(8,128)S(1)} collective-permute-done((f32[152,128]{1,0:T(8,128)S(1)}, f32[152,128]{1,0:T(8,128)S(1)}, u32[]{:S(2)}, u32[]{:S(2)}) %collective-permute-start.9) | collective-permute-done | bytes 77856 | tf_op jit(solution)/shard_map/ppermute | solution.py:296
  80.4 0.8 %shard_map.81 = (f32[3,3,64,64]{3,2,1,0:T(8,128)}, f32[16,64]{1,0:T(8,128)}) custom-call(f32[8,128]{1,0:T(8,128)S(1)} %broadcast_in_dim.16.side_ref, f32[152,128]{1,0:T(8,128)S(1)} %add_add_fusion.mine_ref, f32[152,128]{1,0:T(8,128)S(1)} %collective-permute-done.9.other_ref), custom_call_target="tpu_custom_call" | custom-call | bytes 524288 | tf_op jit(solution)/shard_map/pallas_call | solution.py:23
  81.2 0.4 all-to-all-done.2
  81.6 0.9 %shard_map.79 = bf16[64,32,128]{2,1,0:T(8,128)(2,1)} custom-call(bf16[64,32,128]{2,1,0:T(8,128)(2,1)S(1)} %bitcast.18, bf16[64,32,128]{2,1,0:T(8,128)(2,1)S(1)} %bitcast.19, bf16[64,32,128]{2,1,0:T(8,128)(2,1)S(1)} %bitcast.20), custom_call_target="tpu_custom_call" | custom-call | flops 262144 | bytes 1572864 | tf_op jit(solution)/shard_map/pallas_call | solution.py:23
  (9 shorter events, 0.1 us)
Async XLA Ops:
  0.6 8.8 %copy-start = (bf16[64,16]{0,1:T(8,128)(2,1)S(1)}, bf16[64,16]{0,1:T(8,128)(2,1)}, u32[]{:S(2)}) copy-start(bf16[64,16]{0,1:T(8,128)(2,1)} %param.7) | copy-start | bytes 6148
  0.6 8.5 %copy-start.1 = (bf16[1,64,32,128]{3,2,1,0:T(8,128)(2,1)S(1)}, bf16[1,64,32,128]{3,2,1,0:T(8,128)(2,1)}, u32[]{:S(2)}) copy-start(bf16[1,64,32,128]{3,2,1,0:T(8,128)(2,1)} %param.4) | copy-start | bytes 1572868
  0.7 23.6 %all-to-all-start = ((bf16[16,4,32,128]{3,2,1,0:T(8,128)(2,1)}), bf16[16,4,32,128]{3,2,1,0:T(8,128)(2,1)S(1)}, u32[]{:S(2)}, u32[]{:S(2)}) async-start(bf16[16,4,32,128]{3,2,1,0:T(8,128)(2,1)} %bitcast.21), calls=%async_computation | async-start | bytes 1048576 | tf_op jit(solution)/shard_map/all_to_all | solution.py:328
  9.1 0.9 %copy-start.5 = (bf16[3,3,64,64]{3,2,1,0:T(8,128)(2,1)S(1)}, bf16[3,3,64,64]{3,2,1,0:T(8,128)(2,1)}, u32[]{:S(2)}) copy-start(bf16[3,3,64,64]{3,2,1,0:T(8,128)(2,1)} %param.6) | copy-start | bytes 221188
  9.4 1.3 %collective-permute-start = (bf16[64,128]{1,0:T(8,128)(2,1)S(1)}, bf16[64,128]{1,0:T(8,128)(2,1)S(1)}, u32[]{:S(2)}, u32[]{:S(2)}) collective-permute-start(bf16[64,128]{1,0:T(8,128)(2,1)S(1)} %fusion), channel_id=1, source_target_pairs={{0,1},{1,0},{2,3},{3,2},{4,5},{5,4},{6,7},{7,6},{8,9},{9,8},{10,11... | collective-permute-start | bytes 49160 | tf_op jit(solution)/shard_map/ppermute | solution.py:296
  25.1 1.0 %copy-start.2 = (bf16[16,2,4,32,128]{4,3,2,1,0:T(8,128)(2,1)}, bf16[16,2,4,32,128]{4,3,2,1,0:T(8,128)(2,1)S(1)}, u32[]{:S(2)}) copy-start(bf16[16,2,4,32,128]{4,3,2,1,0:T(8,128)(2,1)S(1)} %shard_map.76) | copy-start | bytes 3145732
  26.1 27.6 %all-to-all-start.1 = ((bf16[16,2,4,32,128]{4,3,2,1,0:T(8,128)(2,1)}), bf16[16,2,4,32,128]{4,3,2,1,0:T(8,128)(2,1)S(1)}, u32[]{:S(2)}, u32[]{:S(2)}) async-start(bf16[16,2,4,32,128]{4,3,2,1,0:T(8,128)(2,1)} %copy-done.2), calls=%async_computation.1 | async-start | bytes 2097152 | tf_op jit(solution)/shard_map/all_to_all | solution.py:328
  55.5 1.5 %collective-permute-start.1 = (f32[152,128]{1,0:T(8,128)S(1)}, f32[152,128]{1,0:T(8,128)S(1)}, u32[]{:S(2)}, u32[]{:S(2)}) collective-permute-start(f32[152,128]{1,0:T(8,128)S(1)} %get-tuple-element.19), channel_id=1, source_target_pairs={{0,1},{1,0},{2,3},{3,2},{4,5},{5,4},{6,7},{7,6},{8,9},{9,8},{10,11... | collective-permute-start | bytes 233480 | tf_op jit(solution)/shard_map/ppermute | solution.py:296
  56.3 0.8 copy-start.4
  57.1 9.6 %collective-permute-start.3 = (f32[152,128]{1,0:T(8,128)S(1)}, f32[152,128]{1,0:T(8,128)S(1)}, u32[]{:S(2)}, u32[]{:S(2)}) collective-permute-start(f32[152,128]{1,0:T(8,128)S(1)} %add.30), channel_id=1, source_target_pairs={{0,16},{2,18},{4,20},{6,22},{8,24},{10,26},{12,28},{14,30},{16,0},... | collective-permute-start | bytes 233480 | tf_op jit(solution)/shard_map/ppermute | solution.py:305
  59.9 7.6 %collective-permute-start.4 = (f32[152,128]{1,0:T(8,128)S(1)}, f32[152,128]{1,0:T(8,128)}, u32[]{:S(2)}, u32[]{:S(2)}) collective-permute-start(f32[152,128]{1,0:T(8,128)S(1)} %add.30), channel_id=1, source_target_pairs={{0,24},{2,26},{4,28},{6,30},{8,16},{10,18},{12,20},{14,22},{16,8},... | collective-permute-start | bytes 233480 | tf_op jit(solution)/shard_map/ppermute | solution.py:305
  62.5 5.9 %collective-permute-start.2 = (f32[152,128]{1,0:T(8,128)S(1)}, f32[152,128]{1,0:T(8,128)}, u32[]{:S(2)}, u32[]{:S(2)}) collective-permute-start(f32[152,128]{1,0:T(8,128)S(1)} %add.30), channel_id=1, source_target_pairs={{0,8},{2,10},{4,12},{6,14},{8,0},{10,2},{12,4},{14,6},{16,24},{18,... | collective-permute-start | bytes 233480 | tf_op jit(solution)/shard_map/ppermute | solution.py:305
  62.5 19.1 %all-to-all-start.2 = ((bf16[16,4,32,128]{3,2,1,0:T(8,128)(2,1)}), bf16[16,4,32,128]{3,2,1,0:T(8,128)(2,1)S(1)}, u32[]{:S(2)}, u32[]{:S(2)}) async-start(bf16[16,4,32,128]{3,2,1,0:T(8,128)(2,1)} %copy-done.4), calls=%async_computation.2 | async-start | bytes 1048576 | tf_op jit(solution)/shard_map/all_to_all | solution.py:328
  66.7 6.3 %collective-permute-start.8 = (bf16[64,128]{1,0:T(8,128)(2,1)S(1)}, bf16[64,128]{1,0:T(8,128)(2,1)S(1)}, u32[]{:S(2)}, u32[]{:S(2)}) collective-permute-start(bf16[64,128]{1,0:T(8,128)(2,1)S(1)} %select_bitcast_fusion), channel_id=1, source_target_pairs={{0,1},{1,0},{2,3},{3,2},{4,5},{5,4},{6,7},{7,6},{8,9},{9,8},{10,11... | collective-permute-start | bytes 49160 | tf_op jit(solution)/shard_map/ppermute | solution.py:296
  69.4 6.9 %collective-permute-start.6 = (f32[152,128]{1,0:T(8,128)S(1)}, f32[152,128]{1,0:T(8,128)S(1)}, u32[]{:S(2)}, u32[]{:S(2)}) collective-permute-start(f32[152,128]{1,0:T(8,128)S(1)} %add_add_fusion.1), channel_id=1, source_target_pairs={{0,4},{2,6},{4,0},{6,2},{8,12},{10,14},{12,8},{14,10},{16,20},{18,... | collective-permute-start | bytes 233480 | tf_op jit(solution)/shard_map/ppermute | solution.py:291
  70.7 8.1 %collective-permute-start.7 = (f32[152,128]{1,0:T(8,128)S(1)}, f32[152,128]{1,0:T(8,128)S(1)}, u32[]{:S(2)}, u32[]{:S(2)}) collective-permute-start(f32[152,128]{1,0:T(8,128)S(1)} %add_add_fusion.1), channel_id=1, source_target_pairs={{0,6},{2,4},{4,2},{6,0},{8,14},{10,12},{12,10},{14,8},{16,22},{18,... | collective-permute-start | bytes 233480 | tf_op jit(solution)/shard_map/ppermute | solution.py:291
  71.7 7.3 %collective-permute-start.5 = (f32[152,128]{1,0:T(8,128)S(1)}, f32[152,128]{1,0:T(8,128)S(1)}, u32[]{:S(2)}, u32[]{:S(2)}) collective-permute-start(f32[152,128]{1,0:T(8,128)S(1)} %add_add_fusion.1), channel_id=1, source_target_pairs={{0,2},{2,0},{4,6},{6,4},{8,10},{10,8},{12,14},{14,12},{16,18},{18,... | collective-permute-start | bytes 233480 | tf_op jit(solution)/shard_map/ppermute | solution.py:291
  73.0 1.0 %copy-start.3 = (bf16[1,64,32,128]{3,2,1,0:T(8,128)(2,1)S(1)}, bf16[1,64,32,128]{3,2,1,0:T(8,128)(2,1)}, u32[]{:S(2)}) copy-start(bf16[1,64,32,128]{3,2,1,0:T(8,128)(2,1)} %param.5) | copy-start | bytes 1572868
  79.0 1.3 %collective-permute-start.9 = (f32[152,128]{1,0:T(8,128)S(1)}, f32[152,128]{1,0:T(8,128)S(1)}, u32[]{:S(2)}, u32[]{:S(2)}) collective-permute-start(f32[152,128]{1,0:T(8,128)S(1)} %add_add_fusion.mine_ref), channel_id=1, source_target_pairs={{0,1},{1,0},{2,3},{3,2},{4,5},{5,4},{6,7},{7,6},{8,9},{9,8},{10,11... | collective-permute-start | bytes 233480 | tf_op jit(solution)/shard_map/ppermute | solution.py:296

commit v5 on v4

--- a/solution.py
+++ b/solution.py
@@ -12,10 +12,10 @@
 VMEM_LIMIT = 16 * 1024 * 1024
 
 
-def call(body, out, scratch, flops, nbytes, hbm_in=(), hbm_out=()):
+def call(body, out, scratch, flops, nbytes, hbm_in=(), hbm_out=(), alias=None):
     def specs(arrays, outside):
         return [
-            pl.BlockSpec(memory_space=pltpu.HBM if k in outside else pltpu.VMEM)
+            pl.BlockSpec(memory_space=pl.ANY if k in outside else pltpu.VMEM)
             for k in range(len(arrays))
         ]
 
@@ -26,11 +26,34 @@
             in_specs=specs(operands, hbm_in),
             out_specs=specs(out, hbm_out),
             scratch_shapes=scratch,
+            input_output_aliases=alias or {},
             compiler_params=pltpu.CompilerParams(vmem_limit_bytes=VMEM_LIMIT),
             cost_estimate=pl.CostEstimate(flops=flops, bytes_accessed=nbytes, transcendentals=0),
         )(*operands)
 
     return run
+
+
+def in_place(body, coef, values, base):
+    vmem, anywhere = pl.BlockSpec(memory_space=pltpu.VMEM), pl.BlockSpec(memory_space=pl.ANY)
+    frames, (group, rows, width) = base.shape[0], base.shape[-3:]
+    return pl.pallas_call(
+        body,
+        out_shape=jax.ShapeDtypeStruct(base.shape, BF16),
+        in_specs=[vmem, vmem, anywhere],
+        out_specs=anywhere,
+        scratch_shapes=[
+            pltpu.VMEM((group, frames, rows, width), BF16),
+            pltpu.SemaphoreType.DMA((group,)),
+        ],
+        input_output_aliases={2: 0},
+        compiler_params=pltpu.CompilerParams(vmem_limit_bytes=VMEM_LIMIT),
+        cost_estimate=pl.CostEstimate(
+            flops=17 * group * rows * width * frames,
+            bytes_accessed=4 * group * rows * width * frames,
+            transcendentals=0,
+        ),
+    )(coef, values, base)
 
 
 def shifted(x, back):
@@ -74,8 +97,8 @@
 
 
 def forward_body(
-    before_ref, x_ref, after_ref, weight_ref,
-    active_ref, slope_ref, pad_ref, part_ref, act_ref,
+    before_ref, x_ref, after_ref, weight_ref, blank_ref,
+    base_ref, slope_ref, pad_ref, part_ref, act_ref, turn_ref, sem,
 ):
     channels, rows, width = x_ref.shape
     fill_padded(pad_ref, before_ref, swapped(x_ref[...]), after_ref)
@@ -93,7 +116,10 @@
         return carry
 
     lax.fori_loop(0, rows, one, 0, unroll=4)
-    active_ref[...] = swapped(act_ref[...])
+    turn_ref[...] = swapped(act_ref[...]).reshape(turn_ref.shape)
+    send = pltpu.make_async_copy(turn_ref, base_ref.at[:, 1], sem)
+    send.start()
+    send.wait()
 
 
 def input_grad_body(
@@ -130,21 +156,37 @@
     lax.fori_loop(0, group * per, one, 0)
 
 
-def back_body(coef_ref, cot_ref, active_ref, out_ref):
-    frames, group = cot_ref.shape[:2]
-    for owner in range(frames):
-        out_ref[owner, 1] = active_ref[pl.ds(owner * group, group)]
-
-    def one(chan, some):
-        cot = [cot_ref[t, chan, some].astype(F32) for t in range(frames)]
-        coef = [coef_ref[chan, pl.ds(l, 1)] for l in range(frames)]
-        for r in range(frames):
-            total = coef[0] * cot[r]
-            for t in range(r + 1, frames):
-                total = total + coef[t - r] * cot[t]
-            out_ref[r, 0, chan, some] = total.astype(BF16)
-
-    chunks_of(cot_ref.shape, one)
+def toeplitz_chunk(coef_ref, chan, values, store, forward):
+    frames = len(values)
+    coef = [coef_ref[chan, pl.ds(l, 1)] for l in range(frames)]
+    for t in range(frames):
+        total = coef[0] * values[t]
+        for r in range(t) if forward else range(t + 1, frames):
+            total = total + coef[abs(t - r)] * values[r]
+        store(t, total.astype(BF16))
+
+
+def sums_to_hbm(coef_ref, load, targets, held_ref, sems, forward):
+    group, frames, rows, width = held_ref.shape
+    sends = []
+    for chan in range(group):
+        for start in range(0, rows, 16):
+            some = pl.ds(start, 16)
+            values = [load(t, chan, some).astype(F32) for t in range(frames)]
+
+            def store(t, value, chan=chan, some=some):
+                held_ref[chan, t, some] = value
+
+            toeplitz_chunk(coef_ref, chan, values, store, forward)
+        sends.append(pltpu.make_async_copy(held_ref.at[chan], targets[chan], sems.at[chan]))
+        sends[-1].start()
+    for send in sends:
+        send.wait()
+
+
+def back_body(coef_ref, cot_ref, base_ref, out_ref, held_ref, sems):
+    targets = [out_ref.at[:, 0, chan] for chan in range(held_ref.shape[0])]
+    sums_to_hbm(coef_ref, lambda t, c, s: cot_ref[t, c, s], targets, held_ref, sems, False)
 
 
 def along_body(coef_ref, got_ref, along_ref):
@@ -335,21 +377,24 @@
     coef = lax.dynamic_slice_in_dim(temporal_kernel, lax.axis_index("tm") * group, group, 0)
     weight, weight_back = lax.optimization_barrier((weight, weight_back))
     coef = jnp.broadcast_to(coef.astype(F32)[:, :, None], (group, count, width))
-    active, slope = call(
+    packed = (count, 2, group, rows, width)
+    base, slope = call(
         forward_body,
-        (native, jax.ShapeDtypeStruct(shape, F32)),
-        [pltpu.VMEM(padded, BF16), part, pltpu.VMEM(shape, BF16)],
+        (jax.ShapeDtypeStruct(packed, BF16), jax.ShapeDtypeStruct(shape, F32)),
+        [
+            pltpu.VMEM(padded, BF16),
+            part,
+            pltpu.VMEM(shape, BF16),
+            pltpu.VMEM(tile, BF16),
+            pltpu.SemaphoreType.DMA,
+        ],
         flops,
         4 * act_bytes,
-    )(x_before, frame, x_after, weight)
-    packed = (count, 2, group, rows, width)
-    [out] = call(
-        back_body,
-        [jax.ShapeDtypeStruct(packed, BF16)],
-        [],
-        17 * channels * area,
-        4 * act_bytes,
-    )(coef, cot_tile, active)
+        hbm_in=(4,),
+        hbm_out=(0,),
+        alias={4: 0},
+    )(x_before, frame, x_after, weight, jnp.zeros(packed, BF16))
+    out = in_place(back_body, coef, cot_tile, base)
     got = exchange(out)
     [along] = call(
         along_body, [jax.ShapeDtypeStruct(tile, BF16)], [], 17 * channels * area, 2 * act_bytes

time: 83 us -> 83.3 us (level)
  waiting for transfers between devices: 41.9 us -> 39.7 us
  Pallas kernels: 8.76 us -> 10.1 us
    all_to_all x3, waiting for transfers between devices: 36.2 us -> 34.1 us  [exchange(): return lax.all_to_all(x, 'tm', split_axis=0, concat_axis=0, tiled=True)]
    pallas_call x0 -> x1, Pallas kernels: none -> 1.3 us  [in_place(): pl.pallas_call(body, out_shape=jax.ShapeDtypeStruct(base.shape, BF16), in...]
    broadcast_in_dim x0 -> x1, local copies, waits for them, and re-layouts: none -> 1.24 us  [local(): jnp.zeros(packed, BF16)]
    unnamed x14 -> x12, local copies, waits for them, and re-layouts: 3.55 us -> 2.64 us
    pallas_call x7 -> x6, Pallas kernels: 8.76 us -> 8.83 us  [run(): pl.pallas_call(body, out_shape=out, in_specs=specs(operands, hbm_in), out...]
  transfers between devices with their start and end apart: 13 -> 13, of which waited for: 8 -> 6; matrix products, arithmetic and copies ran while one was open for 2% -> 4% of each run, Pallas kernels for 6% -> 7%
where the time goes in v5:
time: 83.3 us; the launch traced here: 82.8 us
  waiting for transfers between devices  39.7 us (48%)
  starting transfers between devices  26.4 us (32%)
  Pallas kernels  10.1 us (12%)
  local copies, waits for them, and re-layouts  4.66 us (6%)
  other arithmetic  1.02 us (1%)
  between operations  0.87 us (1%)
    all_to_all x3, waiting for transfers between devices, exchange(): return lax.all_to_all(x, 'tm', split_axis=0, concat_axis=0, tiled=True)  34.1 us
    all_to_all x3, starting transfers between devices, exchange(): return lax.all_to_all(x, 'tm', split_axis=0, concat_axis=0, tiled=True)  17.1 us
    pallas_call x6, Pallas kernels, run(): pl.pallas_call(body, out_shape=out, in_specs=specs(operands, hbm_in), out...  8.83 us
    ppermute x3, starting transfers between devices, over_planes(): lax.ppermute(mine, 'tm', [(i, i ^ k) for i in range(count)])  5.51 us
    ppermute x3, starting transfers between devices, xor_sum(): lax.ppermute(x, axis, [(i, i ^ k) for i in range(size)])  3.55 us
    unnamed x12, local copies, waits for them, and re-layouts  2.64 us
    ppermute x3, waiting for transfers between devices, xor_sum(): lax.ppermute(x, axis, [(i, i ^ k) for i in range(size)])  2.59 us
    ppermute x3, waiting for transfers between devices, over_planes(): lax.ppermute(mine, 'tm', [(i, i ^ k) for i in range(count)])  1.8 us
  transfers between devices with their start and end apart: 13, of which 6 were waited for; matrix products, arithmetic and copies ran while one was open for 4% of the time, Pallas kernels for 7%

profile of v5, /device:TPU:0, one launch (start us, length us, event | category | flops | bytes accessed | tf_op | source)
XLA Modules:
  0.0 82.8 jit_solution(11411287716003991652)
XLA Ops:
  0.6 0.0 copy-start
  0.6 0.0 copy-start.1
  0.7 8.5 %all-to-all-start = ((bf16[16,4,32,128]{3,2,1,0:T(8,128)(2,1)}), bf16[16,4,32,128]{3,2,1,0:T(8,128)(2,1)S(1)}, u32[]{:S(2)}, u32[]{:S(2)}) async-start(bf16[16,4,32,128]{3,2,1,0:T(8,128)(2,1)} %bitcast.21), calls=%async_computation | async-start | bytes 1048576 | tf_op jit(solution)/shard_map/all_to_all | solution.py:370
  9.1 0.0 copy-done.1
  9.1 0.0 copy-start.4
  9.1 0.2 copy.34
  9.4 0.1 collective-permute-start
  9.5 0.0 copy-done
  9.5 0.1 constant_dynamic-slice_fusion
  9.6 0.5 copy-done.4
  10.0 0.1 copy.26
  10.2 0.2 reshape.22.weight_ref
  10.3 0.2 copy.27
  10.5 0.2 reshape.23.weight_ref
  10.7 0.1 copy.32
  10.8 0.0 collective-permute-done
  10.8 1.2 %broadcast_in_dim.19.blank_ref = bf16[16,2,4,32,128]{4,3,2,1,0:T(8,128)(2,1)} broadcast(bf16[]{:T(256)} %constant.27.clone.1), dimensions={} | broadcast | bytes 1048578 | tf_op jit(solution)/shard_map/broadcast_in_dim | solution.py:396
  12.0 2.3 %shard_map.75 = (bf16[16,2,4,32,128]{4,3,2,1,0:T(8,128)(2,1)}, f32[32,64,128]{2,1,0:T(8,128)S(1)}) custom-call(bf16[64,128]{1,0:T(8,128)(2,1)S(1)} %get-tuple-element.31.before_ref, bf16[64,32,128]{2,1,0:T(8,128)(2,1)S(1)} %bitcast.16, bf16[64,128]{1,0:T(8,128)(2,1)S(1)} %get-tuple-element.30.after_ref, ...), custom_call_target="tpu_custom_call", output_to_operand_aliasing={{0}: (4, {})} | custom-call | flops 301989888 | bytes 2097152 | tf_op jit(solution)/shard_map/pallas_call | solution.py:23
  14.3 9.9 %all-to-all-done.cot_ref = bf16[16,4,32,128]{3,2,1,0:T(8,128)(2,1)S(1)} async-done(((bf16[16,4,32,128]{3,2,1,0:T(8,128)(2,1)}), bf16[16,4,32,128]{3,2,1,0:T(8,128)(2,1)S(1)}, u32[]{:S(2)}, u32[]{:S(2)}) %all-to-all-start) | async-done | bytes 524320 | tf_op jit(solution)/shard_map/all_to_all | solution.py:370
  24.3 0.1 broadcast_in_dim.18.coef_ref
  24.3 1.3 %shard_map.76 = bf16[16,2,4,32,128]{4,3,2,1,0:T(8,128)(2,1)} custom-call(f32[4,16,128]{2,1,0:T(8,128)S(1)} %broadcast_in_dim.18.coef_ref, bf16[16,4,32,128]{3,2,1,0:T(8,128)(2,1)S(1)} %all-to-all-done.cot_ref, bf16[16,2,4,32,128]{4,3,2,1,0:T(8,128)(2,1)} %get-tuple-element.17.base_ref), custom_call_target="tpu_custom_call", output_to_operand_aliasing={{}: (2, {})} | custom-call | flops 4456448 | bytes 1048576 | tf_op jit(solution)/shard_map/pallas_call | solution.py:40
  25.6 3.9 %all-to-all-start.1 = ((bf16[16,2,4,32,128]{4,3,2,1,0:T(8,128)(2,1)}), bf16[16,2,4,32,128]{4,3,2,1,0:T(8,128)(2,1)S(1)}, u32[]{:S(2)}, u32[]{:S(2)}) async-start(bf16[16,2,4,32,128]{4,3,2,1,0:T(8,128)(2,1)} %shard_map.76), calls=%async_computation.1 | async-start | bytes 2097152 | tf_op jit(solution)/shard_map/all_to_all | solution.py:370
  29.6 23.7 %all-to-all-done.1.got_ref = bf16[16,2,4,32,128]{4,3,2,1,0:T(8,128)(2,1)S(1)} async-done(((bf16[16,2,4,32,128]{4,3,2,1,0:T(8,128)(2,1)}), bf16[16,2,4,32,128]{4,3,2,1,0:T(8,128)(2,1)S(1)}, u32[]{:S(2)}, u32[]{:S(2)}) %all-to-all-start.1) | async-done | bytes 1048608 | tf_op jit(solution)/shard_map/all_to_all | solution.py:370
  53.2 1.9 %shard_map.78 = (bf16[2,64,128]{2,1,0:T(8,128)(2,1)S(1)}, f32[152,128]{1,0:T(8,128)S(1)}, f32[152,128]{1,0:T(8,128)S(1)}) custom-call(f32[8,128]{1,0:T(8,128)S(1)} %broadcast_in_dim.20.side_ref, s32[8,128]{1,0:T(8,128)S(1)} %iota.7.mine_ref, bf16[16,2,4,32,128]{4,3,2,1,0:T(8,128)(2,1)S(1)} %all-to-all-done.1.got_ref, ...), custom_call_target="tpu_custom_call" | custom-call | flops 301989888 | bytes 2621440 | tf_op jit(solution)/shard_map/pallas_call | solution.py:23
  55.1 0.0 collective-permute-start.1
  55.1 0.7 shard_map.77
  55.9 0.0 copy-start.3
  55.9 0.8 copy-done.3
  56.6 0.0 collective-permute-done.1
  56.7 3.1 %collective-permute-start.2 = (f32[152,128]{1,0:T(8,128)S(1)}, f32[152,128]{1,0:T(8,128)S(1)}, u32[]{:S(2)}, u32[]{:S(2)}) collective-permute-start(f32[152,128]{1,0:T(8,128)S(1)} %add.30), channel_id=1, source_target_pairs={{0,8},{2,10},{4,12},{6,14},{8,0},{10,2},{12,4},{14,6},{16,24},{18,... | collective-permute-start | bytes 233480 | tf_op jit(solution)/shard_map/ppermute | solution.py:347
  59.7 0.4 collective-permute-start.3
  60.1 2.1 %collective-permute-start.4 = (f32[152,128]{1,0:T(8,128)S(1)}, f32[152,128]{1,0:T(8,128)}, u32[]{:S(2)}, u32[]{:S(2)}) collective-permute-start(f32[152,128]{1,0:T(8,128)S(1)} %add.30), channel_id=1, source_target_pairs={{0,24},{2,26},{4,28},{6,30},{8,16},{10,18},{12,20},{14,22},{16,8},... | collective-permute-start | bytes 233480 | tf_op jit(solution)/shard_map/ppermute | solution.py:347
  62.2 4.7 %all-to-all-start.2 = ((bf16[16,4,32,128]{3,2,1,0:T(8,128)(2,1)}), bf16[16,4,32,128]{3,2,1,0:T(8,128)(2,1)S(1)}, u32[]{:S(2)}, u32[]{:S(2)}) async-start(bf16[16,4,32,128]{3,2,1,0:T(8,128)(2,1)} %copy-done.3), calls=%async_computation.2 | async-start | bytes 1048576 | tf_op jit(solution)/shard_map/all_to_all | solution.py:370
  66.9 0.1 collective-permute-start.8
  67.0 0.0 collective-permute-done.2
  67.0 1.8 %collective-permute-done.3 = f32[152,128]{1,0:T(8,128)} collective-permute-done((f32[152,128]{1,0:T(8,128)S(1)}, f32[152,128]{1,0:T(8,128)}, u32[]{:S(2)}, u32[]{:S(2)}) %collective-permute-start.3) | collective-permute-done | bytes 77856 | tf_op jit(solution)/shard_map/ppermute | solution.py:347
  68.8 0.0 collective-permute-done.4
  68.8 0.9 %add_add_fusion.1 = f32[152,128]{1,0:T(8,128)S(1)} fusion(f32[152,128]{1,0:T(8,128)} %collective-permute-done.3, f32[152,128]{1,0:T(8,128)} %collective-permute-done.4, f32[152,128]{1,0:T(8,128)S(1)} %add.30, f32[152,128]{1,0:T(8,128)S(1)} %collective-permute-done.2), kind=kLoop, calls=%fused_computation.2 | loop fusion | flops 58368 | bytes 389120 | tf_op jit(solution)/shard_map/add | solution.py:327
  69.8 1.0 %collective-permute-start.5 = (f32[152,128]{1,0:T(8,128)S(1)}, f32[152,128]{1,0:T(8,128)S(1)}, u32[]{:S(2)}, u32[]{:S(2)}) collective-permute-start(f32[152,128]{1,0:T(8,128)S(1)} %add_add_fusion.1), channel_id=1, source_target_pairs={{0,2},{2,0},{4,6},{6,4},{8,10},{10,8},{12,14},{14,12},{16,18},{18,... | collective-permute-start | bytes 233480 | tf_op jit(solution)/shard_map/ppermute | solution.py:333
  70.8 0.7 collective-permute-start.6
  71.5 1.8 %collective-permute-start.7 = (f32[152,128]{1,0:T(8,128)S(1)}, f32[152,128]{1,0:T(8,128)S(1)}, u32[]{:S(2)}, u32[]{:S(2)}) collective-permute-start(f32[152,128]{1,0:T(8,128)S(1)} %add_add_fusion.1), channel_id=1, source_target_pairs={{0,6},{2,4},{4,2},{6,0},{8,14},{10,12},{12,10},{14,8},{16,22},{18,... | collective-permute-start | bytes 233480 | tf_op jit(solution)/shard_map/ppermute | solution.py:333
  73.3 0.0 collective-permute-done.8
  73.4 0.0 copy-start.2
  73.4 1.0 %copy-done.2 = bf16[1,64,32,128]{3,2,1,0:T(8,128)(2,1)S(1)} copy-done((bf16[1,64,32,128]{3,2,1,0:T(8,128)(2,1)S(1)}, bf16[1,64,32,128]{3,2,1,0:T(8,128)(2,1)}, u32[]{:S(2)}) %copy-start.2) | copy-done | bytes 524312
  74.4 2.2 %shard_map.80 = bf16[64,32,128]{2,1,0:T(8,128)(2,1)} custom-call(bf16[64,128]{1,0:T(8,128)(2,1)S(1)} %get-tuple-element.29.before_ref, bf16[64,128]{1,0:T(8,128)(2,1)S(1)} %get-tuple-element.28.after_ref, bf16[192,192]{1,0:T(8,128)(2,1)S(1)} %reshape.23.weight_ref, bf16[16,2,4,32,128]{4,3,2,1,0:T(8,128)(2,1)S(1)} %all-to-all-done.1.got_ref, ...), custom_call_target="tpu_custom_call" | custom-call | flops 301989888 | bytes 2097152 | tf_op jit(solution)/shard_map/pallas_call | solution.py:23
  76.6 0.0 collective-permute-done.5
  76.6 0.0 collective-permute-done.6
  76.6 2.6 %collective-permute-done.7 = f32[152,128]{1,0:T(8,128)S(1)} collective-permute-done((f32[152,128]{1,0:T(8,128)S(1)}, f32[152,128]{1,0:T(8,128)S(1)}, u32[]{:S(2)}, u32[]{:S(2)}) %collective-permute-start.7) | collective-permute-done | bytes 77856 | tf_op jit(solution)/shard_map/ppermute | solution.py:333
  79.3 0.1 collective-permute-start.9
  79.3 1.3 %collective-permute-done.9.other_ref = f32[152,128]{1,0:T(8,128)S(1)} collective-permute-done((f32[152,128]{1,0:T(8,128)S(1)}, f32[152,128]{1,0:T(8,128)S(1)}, u32[]{:S(2)}, u32[]{:S(2)}) %collective-permute-start.9) | collective-permute-done | bytes 77856 | tf_op jit(solution)/shard_map/ppermute | solution.py:338
  80.6 0.8 shard_map.81
  81.4 0.5 all-to-all-done.2
  81.9 0.9 %shard_map.79 = bf16[64,32,128]{2,1,0:T(8,128)(2,1)} custom-call(bf16[64,32,128]{2,1,0:T(8,128)(2,1)S(1)} %bitcast.18, bf16[64,32,128]{2,1,0:T(8,128)(2,1)S(1)} %bitcast.19, bf16[64,32,128]{2,1,0:T(8,128)(2,1)S(1)} %bitcast.20), custom_call_target="tpu_custom_call" | custom-call | flops 262144 | bytes 1572864 | tf_op jit(solution)/shard_map/pallas_call | solution.py:23
  (9 shorter events, 0.1 us)
Async XLA Ops:
  0.6 8.8 %copy-start = (bf16[64,16]{0,1:T(8,128)(2,1)S(1)}, bf16[64,16]{0,1:T(8,128)(2,1)}, u32[]{:S(2)}) copy-start(bf16[64,16]{0,1:T(8,128)(2,1)} %param.7) | copy-start | bytes 6148
  0.6 8.5 %copy-start.1 = (bf16[1,64,32,128]{3,2,1,0:T(8,128)(2,1)S(1)}, bf16[1,64,32,128]{3,2,1,0:T(8,128)(2,1)}, u32[]{:S(2)}) copy-start(bf16[1,64,32,128]{3,2,1,0:T(8,128)(2,1)} %param.4) | copy-start | bytes 1572868
  0.7 23.6 %all-to-all-start = ((bf16[16,4,32,128]{3,2,1,0:T(8,128)(2,1)}), bf16[16,4,32,128]{3,2,1,0:T(8,128)(2,1)S(1)}, u32[]{:S(2)}, u32[]{:S(2)}) async-start(bf16[16,4,32,128]{3,2,1,0:T(8,128)(2,1)} %bitcast.21), calls=%async_computation | async-start | bytes 1048576 | tf_op jit(solution)/shard_map/all_to_all | solution.py:370
  9.1 0.9 %copy-start.4 = (bf16[3,3,64,64]{3,2,1,0:T(8,128)(2,1)S(1)}, bf16[3,3,64,64]{3,2,1,0:T(8,128)(2,1)}, u32[]{:S(2)}) copy-start(bf16[3,3,64,64]{3,2,1,0:T(8,128)(2,1)} %param.6) | copy-start | bytes 221188
  9.4 1.4 %collective-permute-start = (bf16[64,128]{1,0:T(8,128)(2,1)S(1)}, bf16[64,128]{1,0:T(8,128)(2,1)S(1)}, u32[]{:S(2)}, u32[]{:S(2)}) collective-permute-start(bf16[64,128]{1,0:T(8,128)(2,1)S(1)} %fusion), channel_id=1, source_target_pairs={{0,1},{1,0},{2,3},{3,2},{4,5},{5,4},{6,7},{7,6},{8,9},{9,8},{10,11... | collective-permute-start | bytes 49160 | tf_op jit(solution)/shard_map/ppermute | solution.py:338
  25.6 27.6 %all-to-all-start.1 = ((bf16[16,2,4,32,128]{4,3,2,1,0:T(8,128)(2,1)}), bf16[16,2,4,32,128]{4,3,2,1,0:T(8,128)(2,1)S(1)}, u32[]{:S(2)}, u32[]{:S(2)}) async-start(bf16[16,2,4,32,128]{4,3,2,1,0:T(8,128)(2,1)} %shard_map.76), calls=%async_computation.1 | async-start | bytes 2097152 | tf_op jit(solution)/shard_map/all_to_all | solution.py:370
  55.1 1.5 %collective-permute-start.1 = (f32[152,128]{1,0:T(8,128)S(1)}, f32[152,128]{1,0:T(8,128)S(1)}, u32[]{:S(2)}, u32[]{:S(2)}) collective-permute-start(f32[152,128]{1,0:T(8,128)S(1)} %get-tuple-element.19), channel_id=1, source_target_pairs={{0,1},{1,0},{2,3},{3,2},{4,5},{5,4},{6,7},{7,6},{8,9},{9,8},{10,11... | collective-permute-start | bytes 233480 | tf_op jit(solution)/shard_map/ppermute | solution.py:338
  55.9 0.8 copy-start.3
  56.7 10.4 %collective-permute-start.2 = (f32[152,128]{1,0:T(8,128)S(1)}, f32[152,128]{1,0:T(8,128)S(1)}, u32[]{:S(2)}, u32[]{:S(2)}) collective-permute-start(f32[152,128]{1,0:T(8,128)S(1)} %add.30), channel_id=1, source_target_pairs={{0,8},{2,10},{4,12},{6,14},{8,0},{10,2},{12,4},{14,6},{16,24},{18,... | collective-permute-start | bytes 233480 | tf_op jit(solution)/shard_map/ppermute | solution.py:347
  59.7 9.1 %collective-permute-start.3 = (f32[152,128]{1,0:T(8,128)S(1)}, f32[152,128]{1,0:T(8,128)}, u32[]{:S(2)}, u32[]{:S(2)}) collective-permute-start(f32[152,128]{1,0:T(8,128)S(1)} %add.30), channel_id=1, source_target_pairs={{0,16},{2,18},{4,20},{6,22},{8,24},{10,26},{12,28},{14,30},{16,0},... | collective-permute-start | bytes 233480 | tf_op jit(solution)/shard_map/ppermute | solution.py:347
  60.1 8.7 %collective-permute-start.4 = (f32[152,128]{1,0:T(8,128)S(1)}, f32[152,128]{1,0:T(8,128)}, u32[]{:S(2)}, u32[]{:S(2)}) collective-permute-start(f32[152,128]{1,0:T(8,128)S(1)} %add.30), channel_id=1, source_target_pairs={{0,24},{2,26},{4,28},{6,30},{8,16},{10,18},{12,20},{14,22},{16,8},... | collective-permute-start | bytes 233480 | tf_op jit(solution)/shard_map/ppermute | solution.py:347
  62.2 19.7 %all-to-all-start.2 = ((bf16[16,4,32,128]{3,2,1,0:T(8,128)(2,1)}), bf16[16,4,32,128]{3,2,1,0:T(8,128)(2,1)S(1)}, u32[]{:S(2)}, u32[]{:S(2)}) async-start(bf16[16,4,32,128]{3,2,1,0:T(8,128)(2,1)} %copy-done.3), calls=%async_computation.2 | async-start | bytes 1048576 | tf_op jit(solution)/shard_map/all_to_all | solution.py:370
  66.9 6.4 %collective-permute-start.8 = (bf16[64,128]{1,0:T(8,128)(2,1)S(1)}, bf16[64,128]{1,0:T(8,128)(2,1)S(1)}, u32[]{:S(2)}, u32[]{:S(2)}) collective-permute-start(bf16[64,128]{1,0:T(8,128)(2,1)S(1)} %select_bitcast_fusion), channel_id=1, source_target_pairs={{0,1},{1,0},{2,3},{3,2},{4,5},{5,4},{6,7},{7,6},{8,9},{9,8},{10,11... | collective-permute-start | bytes 49160 | tf_op jit(solution)/shard_map/ppermute | solution.py:338
  69.8 6.9 %collective-permute-start.5 = (f32[152,128]{1,0:T(8,128)S(1)}, f32[152,128]{1,0:T(8,128)S(1)}, u32[]{:S(2)}, u32[]{:S(2)}) collective-permute-start(f32[152,128]{1,0:T(8,128)S(1)} %add_add_fusion.1), channel_id=1, source_target_pairs={{0,2},{2,0},{4,6},{6,4},{8,10},{10,8},{12,14},{14,12},{16,18},{18,... | collective-permute-start | bytes 233480 | tf_op jit(solution)/shard_map/ppermute | solution.py:333
  70.8 5.8 %collective-permute-start.6 = (f32[152,128]{1,0:T(8,128)S(1)}, f32[152,128]{1,0:T(8,128)S(1)}, u32[]{:S(2)}, u32[]{:S(2)}) collective-permute-start(f32[152,128]{1,0:T(8,128)S(1)} %add_add_fusion.1), channel_id=1, source_target_pairs={{0,4},{2,6},{4,0},{6,2},{8,12},{10,14},{12,8},{14,10},{16,20},{18,... | collective-permute-start | bytes 233480 | tf_op jit(solution)/shard_map/ppermute | solution.py:333
  71.5 7.7 %collective-permute-start.7 = (f32[152,128]{1,0:T(8,128)S(1)}, f32[152,128]{1,0:T(8,128)S(1)}, u32[]{:S(2)}, u32[]{:S(2)}) collective-permute-start(f32[152,128]{1,0:T(8,128)S(1)} %add_add_fusion.1), channel_id=1, source_target_pairs={{0,6},{2,4},{4,2},{6,0},{8,14},{10,12},{12,10},{14,8},{16,22},{18,... | collective-permute-start | bytes 233480 | tf_op jit(solution)/shard_map/ppermute | solution.py:333
  73.4 1.0 %copy-start.2 = (bf16[1,64,32,128]{3,2,1,0:T(8,128)(2,1)S(1)}, bf16[1,64,32,128]{3,2,1,0:T(8,128)(2,1)}, u32[]{:S(2)}) copy-start(bf16[1,64,32,128]{3,2,1,0:T(8,128)(2,1)} %param.5) | copy-start | bytes 1572868
  79.3 1.3 %collective-permute-start.9 = (f32[152,128]{1,0:T(8,128)S(1)}, f32[152,128]{1,0:T(8,128)S(1)}, u32[]{:S(2)}, u32[]{:S(2)}) collective-permute-start(f32[152,128]{1,0:T(8,128)S(1)} %add_add_fusion.mine_ref), channel_id=1, source_target_pairs={{0,1},{1,0},{2,3},{3,2},{4,5},{5,4},{6,7},{7,6},{8,9},{9,8},{10,11... | collective-permute-start | bytes 233480 | tf_op jit(solution)/shard_map/ppermute | solution.py:338

commit v6 on v5

--- a/solution.py
+++ b/solution.py
@@ -189,8 +189,10 @@
     sums_to_hbm(coef_ref, lambda t, c, s: cot_ref[t, c, s], targets, held_ref, sems, False)
 
 
-def along_body(coef_ref, got_ref, along_ref):
-    frames, _, group, rows, width = got_ref.shape
+def along_body(coef_ref, mine_ref, keep_ref, cot_ref, got_ref, along_ref, pack_ref, sum_ref):
+    frames, group, rows, width = cot_ref.shape
+    channels = width // 2
+    sum_ref[...] = jnp.zeros_like(sum_ref)
 
     def one(chan, some):
         act = [got_ref[t, 1, chan, some].astype(F32) for t in range(frames)]
@@ -200,16 +202,6 @@
             for r in range(t):
                 total = total + coef[t - r] * act[r]
             along_ref[t, chan, some] = total.astype(BF16)
-
-    chunks_of(along_ref.shape, one)
-
-
-def kernel_sums(cot_ref, got_ref, mine_ref, sum_ref):
-    frames, group, rows, width = cot_ref.shape
-    sum_ref[...] = jnp.zeros_like(sum_ref)
-
-    def one(chan, some):
-        act = [got_ref[t, 1, chan, some].astype(F32) for t in range(frames)]
         cot = [cot_ref[t, chan, some].astype(F32) for t in range(frames)]
         for lag in range(frames):
             total = cot[lag] * act[0]
@@ -223,7 +215,10 @@
     for chan in range(group):
         sums = jnp.sum(jnp.sum(sum_ref[chan], axis=1), axis=1, keepdims=True)
         both = jnp.where(lane == chan, sums, both)
-    return both
+    lags = frames // 2
+    half = keep_ref.shape[0]
+    pack_ref[pl.ds(0, half)] = keep_ref[...]
+    pack_ref[pl.ds(half, lags)] = jnp.concatenate([both[:lags, :channels], both[lags:, :channels]], axis=1)
 
 
 def block_output_body(x_ref, even_ref, odd_ref, out_ref):
@@ -244,9 +239,9 @@
 
 
 def weight_grad_body(
-    side_ref, mine_ref, got_ref, slope_ref, before_ref, x_ref, after_ref, cot_ref,
+    side_ref, got_ref, slope_ref, before_ref, x_ref, after_ref,
     edge_ref, keep_ref, give_ref,
-    dpad_ref, grad_ref, pack_ref, turn_ref, pad_ref, sum_ref,
+    dpad_ref, grad_ref, pack_ref, turn_ref, pad_ref,
 ):
     rows, channels, width = slope_ref.shape
     fill_padded(pad_ref, before_ref, swapped(x_ref[...]), after_ref)
@@ -274,25 +269,21 @@
     )
     half = keep_ref.shape[0]
     done = tall + tall // 2
-    sums = kernel_sums(cot_ref, got_ref, mine_ref, sum_ref)
-    lags = sums.shape[0] // 2
-    pack_ref[pl.ds(done, lags)] = jnp.concatenate(
-        [sums[:lags, :channels], sums[lags:, :channels]], axis=1
-    )
-    done += lags
     if 2 * half > done:
         pack_ref[pl.ds(done, 2 * half - done)] = jnp.zeros((2 * half - done, 2 * channels), F32)
     first = side_ref[pl.ds(0, 1)] > 0
     low, high = pack_ref[pl.ds(0, half)], pack_ref[pl.ds(half, half)]
     keep_ref[...] = jnp.where(first, low, high)
-    give_ref[...] = jnp.where(first, high, low)
+    give_ref[pl.ds(0, half)] = jnp.where(first, high, low)
+    rest = give_ref.shape[0] - half
+    give_ref[pl.ds(half, rest)] = jnp.zeros((rest, 2 * channels), F32)
 
 
 def unpack_body(gscale, side_ref, mine_ref, other_ref, weight_ref, kernel_ref, pack_ref):
     channels = weight_ref.shape[2]
-    half = mine_ref.shape[0]
+    half = pack_ref.shape[0] // 2
     first = side_ref[pl.ds(0, 1)] > 0
-    mine, other = mine_ref[...] * gscale, other_ref[...] * gscale
+    mine, other = mine_ref[pl.ds(0, half)] * gscale, other_ref[pl.ds(0, half)] * gscale
     pack_ref[pl.ds(0, half)] = jnp.where(first, mine, other)
     pack_ref[pl.ds(half, half)] = jnp.where(first, other, mine)
     tall = 3 * channels
@@ -305,7 +296,7 @@
     for a in range(3):
         weight_ref[a, 2] = last[a * channels : (a + 1) * channels]
     lags = kernel_ref.shape[0] // 2
-    sums = pack_ref[pl.ds(tall + tall // 2, lags)]
+    sums = (mine_ref[pl.ds(half, lags)] + other_ref[pl.ds(half, lags)]) * gscale
     kernel_ref[pl.ds(0, lags)] = sums[:, :channels]
     kernel_ref[pl.ds(lags, lags)] = sums[:, channels:]
 
@@ -358,7 +349,7 @@
     area = rows * width
     act_bytes = channels * area * 2
     flops = 18 * channels * channels * area
-    half = -(-(9 * channels * channels + count * channels) // (128 * 16)) * 8
+    half = -(-(9 * channels * channels) // (128 * 16)) * 8
     side = jnp.full((8, 128), 1 - lax.axis_index("span") % 2, F32)
     mine = lax.broadcasted_iota(jnp.int32, (8, width), 1) - lax.axis_index("tm") * group
     part = pltpu.VMEM((rows + 2, 3 * channels, width), F32)
@@ -396,14 +387,12 @@
     )(x_before, frame, x_after, weight, jnp.zeros(packed, BF16))
     out = in_place(back_body, coef, cot_tile, base)
     got = exchange(out)
-    [along] = call(
-        along_body, [jax.ShapeDtypeStruct(tile, BF16)], [], 17 * channels * area, 2 * act_bytes
-    )(coef, got)
     d_edges, keep, give = call(
         weight_grad_body,
         (
             jax.ShapeDtypeStruct((2, channels, width), BF16),
-            *[jax.ShapeDtypeStruct((half, 128), F32)] * 2,
+            jax.ShapeDtypeStruct((half, 128), F32),
+            jax.ShapeDtypeStruct((half + count // 2, 128), F32),
         ),
         [
             pltpu.VMEM((rows + 4, channels, width), BF16),
@@ -411,11 +400,17 @@
             pltpu.VMEM((2 * half, 128), F32),
             pltpu.VMEM(shape, BF16),
             pltpu.VMEM(padded, BF16),
-            pltpu.VMEM((group, count, 8, width), F32),
         ],
         flops,
         5 * act_bytes,
-    )(side, mine, got, slope, x_before, frame, x_after, cot_tile)
+    )(side, got, slope, x_before, frame, x_after)
+    along, kept = call(
+        along_body,
+        (jax.ShapeDtypeStruct(tile, BF16), jax.ShapeDtypeStruct((half + count // 2, width), F32)),
+        [pltpu.VMEM((group, count, 8, width), F32)],
+        34 * channels * area,
+        3 * act_bytes,
+    )(coef, mine, keep, cot_tile, got)
     d_before, d_after = edges(d_edges[0], d_edges[1])
     [input_grad] = call(
         input_grad_body,
@@ -425,7 +420,7 @@
         4 * act_bytes,
     )(d_before, d_after, weight_back, got, slope, cot)
     received = swap_cores(give)
-    planes = over_planes(keep + received, plane)
+    planes = over_planes(kept + received, plane)
     along, received = lax.optimization_barrier((along, received))
     along = exchange(along).reshape(native.shape)
     sums = xor_sum(tree_sum(planes), "tm", list(range(plane)))

time: 83.3 us -> 83.3 us (level)
  transfers between devices with their start and end apart: 13 -> 13, of which waited for: 6 -> 6; matrix products, arithmetic and copies ran while one was open for 4% -> 4% of each run, Pallas kernels for 7% -> 8%
where the time goes in v6:
time: 83.3 us; the launch traced here: 82.7 us
  waiting for transfers between devices  39.7 us (48%)
  starting transfers between devices  26.5 us (32%)
  Pallas kernels  10 us (12%)
  local copies, waits for them, and re-layouts  4.68 us (6%)
  other arithmetic  1.01 us (1%)
  between operations  0.86 us (1%)
    all_to_all x3, waiting for transfers between devices, exchange(): return lax.all_to_all(x, 'tm', split_axis=0, concat_axis=0, tiled=True)  34.1 us
    all_to_all x3, starting transfers between devices, exchange(): return lax.all_to_all(x, 'tm', split_axis=0, concat_axis=0, tiled=True)  17.1 us
    pallas_call x6, Pallas kernels, run(): pl.pallas_call(body, out_shape=out, in_specs=specs(operands, hbm_in), out...  8.7 us
    ppermute x3, starting transfers between devices, over_planes(): lax.ppermute(mine, 'tm', [(i, i ^ k) for i in range(count)])  5.52 us
    ppermute x3, starting transfers between devices, xor_sum(): lax.ppermute(x, axis, [(i, i ^ k) for i in range(size)])  3.55 us
    unnamed x12, local copies, waits for them, and re-layouts  2.65 us
    ppermute x3, waiting for transfers between devices, xor_sum(): lax.ppermute(x, axis, [(i, i ^ k) for i in range(size)])  2.54 us
    ppermute x3, waiting for transfers between devices, over_planes(): lax.ppermute(mine, 'tm', [(i, i ^ k) for i in range(count)])  1.78 us
  transfers between devices with their start and end apart: 13, of which 6 were waited for; matrix products, arithmetic and copies ran while one was open for 4% of the time, Pallas kernels for 8%

profile of v6, /device:TPU:0, one launch (start us, length us, event | category | flops | bytes accessed | tf_op | source)
XLA Modules:
  0.0 82.7 jit_solution(5275804899158939658)
XLA Ops:
  0.6 0.0 copy-start
  0.6 0.0 copy-start.1
  0.7 8.5 %all-to-all-start = ((bf16[16,4,32,128]{3,2,1,0:T(8,128)(2,1)}), bf16[16,4,32,128]{3,2,1,0:T(8,128)(2,1)S(1)}, u32[]{:S(2)}, u32[]{:S(2)}) async-start(bf16[16,4,32,128]{3,2,1,0:T(8,128)(2,1)} %bitcast.21), calls=%async_computation | async-start | bytes 1048576 | tf_op jit(solution)/shard_map/all_to_all | solution.py:361
  9.1 0.0 copy-done.1
  9.1 0.0 copy-start.4
  9.1 0.2 copy.34
  9.4 0.1 collective-permute-start
  9.5 0.0 copy-done
  9.5 0.1 constant_dynamic-slice_fusion
  9.6 0.5 copy-done.4
  10.0 0.1 copy.26
  10.2 0.2 reshape.22.weight_ref
  10.3 0.2 copy.27
  10.5 0.2 reshape.23.weight_ref
  10.7 0.1 copy.32
  10.8 0.0 collective-permute-done
  10.8 1.3 %broadcast_in_dim.20.blank_ref = bf16[16,2,4,32,128]{4,3,2,1,0:T(8,128)(2,1)} broadcast(bf16[]{:T(256)} %constant.29.clone.1), dimensions={} | broadcast | bytes 1048578 | tf_op jit(solution)/shard_map/broadcast_in_dim | solution.py:387
  12.0 2.3 %shard_map.75 = (bf16[16,2,4,32,128]{4,3,2,1,0:T(8,128)(2,1)}, f32[32,64,128]{2,1,0:T(8,128)S(1)}) custom-call(bf16[64,128]{1,0:T(8,128)(2,1)S(1)} %get-tuple-element.35.before_ref, bf16[64,32,128]{2,1,0:T(8,128)(2,1)S(1)} %bitcast.16, bf16[64,128]{1,0:T(8,128)(2,1)S(1)} %get-tuple-element.34.after_ref, ...), custom_call_target="tpu_custom_call", output_to_operand_aliasing={{0}: (4, {})} | custom-call | flops 301989888 | bytes 2097152 | tf_op jit(solution)/shard_map/pallas_call | solution.py:23
  14.4 9.9 %all-to-all-done.cot_ref = bf16[16,4,32,128]{3,2,1,0:T(8,128)(2,1)S(1)} async-done(((bf16[16,4,32,128]{3,2,1,0:T(8,128)(2,1)}), bf16[16,4,32,128]{3,2,1,0:T(8,128)(2,1)S(1)}, u32[]{:S(2)}, u32[]{:S(2)}) %all-to-all-start) | async-done | bytes 524320 | tf_op jit(solution)/shard_map/all_to_all | solution.py:361
  24.3 0.1 broadcast_in_dim.18.coef_ref
  24.3 1.3 %shard_map.76 = bf16[16,2,4,32,128]{4,3,2,1,0:T(8,128)(2,1)} custom-call(f32[4,16,128]{2,1,0:T(8,128)S(1)} %broadcast_in_dim.18.coef_ref, bf16[16,4,32,128]{3,2,1,0:T(8,128)(2,1)S(1)} %all-to-all-done.cot_ref, bf16[16,2,4,32,128]{4,3,2,1,0:T(8,128)(2,1)} %get-tuple-element.19.base_ref), custom_call_target="tpu_custom_call", output_to_operand_aliasing={{}: (2, {})} | custom-call | flops 4456448 | bytes 1048576 | tf_op jit(solution)/shard_map/pallas_call | solution.py:40
  25.7 3.9 %all-to-all-start.1 = ((bf16[16,2,4,32,128]{4,3,2,1,0:T(8,128)(2,1)}), bf16[16,2,4,32,128]{4,3,2,1,0:T(8,128)(2,1)S(1)}, u32[]{:S(2)}, u32[]{:S(2)}) async-start(bf16[16,2,4,32,128]{4,3,2,1,0:T(8,128)(2,1)} %shard_map.76), calls=%async_computation.1 | async-start | bytes 2097152 | tf_op jit(solution)/shard_map/all_to_all | solution.py:361
  29.6 23.7 %all-to-all-done.1.got_ref = bf16[16,2,4,32,128]{4,3,2,1,0:T(8,128)(2,1)S(1)} async-done(((bf16[16,2,4,32,128]{4,3,2,1,0:T(8,128)(2,1)}), bf16[16,2,4,32,128]{4,3,2,1,0:T(8,128)(2,1)S(1)}, u32[]{:S(2)}, u32[]{:S(2)}) %all-to-all-start.1) | async-done | bytes 1048608 | tf_op jit(solution)/shard_map/all_to_all | solution.py:361
  53.3 1.2 %shard_map.77 = (bf16[2,64,128]{2,1,0:T(8,128)(2,1)S(1)}, f32[144,128]{1,0:T(8,128)S(1)}, f32[152,128]{1,0:T(8,128)S(1)}) custom-call(f32[8,128]{1,0:T(8,128)S(1)} %broadcast_in_dim.19.side_ref, bf16[16,2,4,32,128]{4,3,2,1,0:T(8,128)(2,1)S(1)} %all-to-all-done.1.got_ref, f32[32,64,128]{2,1,0:T(8,128)S(1)} %get-tuple-element.20.slope_ref, ...), custom_call_target="tpu_custom_call" | custom-call | flops 301989888 | bytes 2621440 | tf_op jit(solution)/shard_map/pallas_call | solution.py:23
  54.5 0.1 collective-permute-start.1
  54.6 1.2 %shard_map.78 = (bf16[16,4,32,128]{3,2,1,0:T(8,128)(2,1)S(1)}, f32[152,128]{1,0:T(8,128)S(1)}) custom-call(f32[4,16,128]{2,1,0:T(8,128)S(1)} %broadcast_in_dim.18.coef_ref, s32[8,128]{1,0:T(8,128)S(1)} %iota.7.mine_ref, f32[144,128]{1,0:T(8,128)S(1)} %get-tuple-element.21.keep_ref, bf16[16,4,32,128]{3,2,1,0:T(8,128)(2,1)S(1)} %all-to-all-done.cot_ref, ...), custom_call_target="tpu_custom_call" | custom-call | flops 8912896 | bytes 1572864 | tf_op jit(solution)/shard_map/pallas_call | solution.py:23
  55.8 0.0 copy-start.3
  55.8 0.8 copy-done.3
  56.6 0.0 collective-permute-done.1
  56.6 3.1 %collective-permute-start.2 = (f32[152,128]{1,0:T(8,128)S(1)}, f32[152,128]{1,0:T(8,128)S(1)}, u32[]{:S(2)}, u32[]{:S(2)}) collective-permute-start(f32[152,128]{1,0:T(8,128)S(1)} %add.30), channel_id=1, source_target_pairs={{0,8},{2,10},{4,12},{6,14},{8,0},{10,2},{12,4},{14,6},{16,24},{18,... | collective-permute-start | bytes 233480 | tf_op jit(solution)/shard_map/ppermute | solution.py:338
  59.7 0.4 collective-permute-start.3
  60.1 2.1 %collective-permute-start.4 = (f32[152,128]{1,0:T(8,128)S(1)}, f32[152,128]{1,0:T(8,128)}, u32[]{:S(2)}, u32[]{:S(2)}) collective-permute-start(f32[152,128]{1,0:T(8,128)S(1)} %add.30), channel_id=1, source_target_pairs={{0,24},{2,26},{4,28},{6,30},{8,16},{10,18},{12,20},{14,22},{16,8},... | collective-permute-start | bytes 233480 | tf_op jit(solution)/shard_map/ppermute | solution.py:338
  62.1 4.7 %all-to-all-start.2 = ((bf16[16,4,32,128]{3,2,1,0:T(8,128)(2,1)}), bf16[16,4,32,128]{3,2,1,0:T(8,128)(2,1)S(1)}, u32[]{:S(2)}, u32[]{:S(2)}) async-start(bf16[16,4,32,128]{3,2,1,0:T(8,128)(2,1)} %copy-done.3), calls=%async_computation.2 | async-start | bytes 1048576 | tf_op jit(solution)/shard_map/all_to_all | solution.py:361
  66.9 0.1 collective-permute-start.8
  67.0 0.0 collective-permute-done.2
  67.0 1.8 %collective-permute-done.3 = f32[152,128]{1,0:T(8,128)} collective-permute-done((f32[152,128]{1,0:T(8,128)S(1)}, f32[152,128]{1,0:T(8,128)}, u32[]{:S(2)}, u32[]{:S(2)}) %collective-permute-start.3) | collective-permute-done | bytes 77856 | tf_op jit(solution)/shard_map/ppermute | solution.py:338
  68.8 0.0 collective-permute-done.4
  68.8 0.9 %add_add_fusion.1 = f32[152,128]{1,0:T(8,128)S(1)} fusion(f32[152,128]{1,0:T(8,128)} %collective-permute-done.3, f32[152,128]{1,0:T(8,128)} %collective-permute-done.4, f32[152,128]{1,0:T(8,128)S(1)} %add.30, f32[152,128]{1,0:T(8,128)S(1)} %collective-permute-done.2), kind=kLoop, calls=%fused_computation.2 | loop fusion | flops 58368 | bytes 389120 | tf_op jit(solution)/shard_map/add | solution.py:318
  69.7 1.0 %collective-permute-start.5 = (f32[152,128]{1,0:T(8,128)S(1)}, f32[152,128]{1,0:T(8,128)S(1)}, u32[]{:S(2)}, u32[]{:S(2)}) collective-permute-start(f32[152,128]{1,0:T(8,128)S(1)} %add_add_fusion.1), channel_id=1, source_target_pairs={{0,2},{2,0},{4,6},{6,4},{8,10},{10,8},{12,14},{14,12},{16,18},{18,... | collective-permute-start | bytes 233480 | tf_op jit(solution)/shard_map/ppermute | solution.py:324
  70.8 0.7 collective-permute-start.6
  71.5 1.8 %collective-permute-start.7 = (f32[152,128]{1,0:T(8,128)S(1)}, f32[152,128]{1,0:T(8,128)S(1)}, u32[]{:S(2)}, u32[]{:S(2)}) collective-permute-start(f32[152,128]{1,0:T(8,128)S(1)} %add_add_fusion.1), channel_id=1, source_target_pairs={{0,6},{2,4},{4,2},{6,0},{8,14},{10,12},{12,10},{14,8},{16,22},{18,... | collective-permute-start | bytes 233480 | tf_op jit(solution)/shard_map/ppermute | solution.py:324
  73.3 0.0 collective-permute-done.8
  73.3 0.0 copy-start.2
  73.3 1.0 %copy-done.2 = bf16[1,64,32,128]{3,2,1,0:T(8,128)(2,1)S(1)} copy-done((bf16[1,64,32,128]{3,2,1,0:T(8,128)(2,1)S(1)}, bf16[1,64,32,128]{3,2,1,0:T(8,128)(2,1)}, u32[]{:S(2)}) %copy-start.2) | copy-done | bytes 524312
  74.3 2.2 %shard_map.80 = bf16[64,32,128]{2,1,0:T(8,128)(2,1)} custom-call(bf16[64,128]{1,0:T(8,128)(2,1)S(1)} %get-tuple-element.33.before_ref, bf16[64,128]{1,0:T(8,128)(2,1)S(1)} %get-tuple-element.32.after_ref, bf16[192,192]{1,0:T(8,128)(2,1)S(1)} %reshape.23.weight_ref, bf16[16,2,4,32,128]{4,3,2,1,0:T(8,128)(2,1)S(1)} %all-to-all-done.1.got_ref, ...), custom_call_target="tpu_custom_call" | custom-call | flops 301989888 | bytes 2097152 | tf_op jit(solution)/shard_map/pallas_call | solution.py:23
  76.6 0.0 collective-permute-done.5
  76.6 0.0 collective-permute-done.6
  76.6 2.5 %collective-permute-done.7 = f32[152,128]{1,0:T(8,128)S(1)} collective-permute-done((f32[152,128]{1,0:T(8,128)S(1)}, f32[152,128]{1,0:T(8,128)S(1)}, u32[]{:S(2)}, u32[]{:S(2)}) %collective-permute-start.7) | collective-permute-done | bytes 77856 | tf_op jit(solution)/shard_map/ppermute | solution.py:324
  79.1 0.1 collective-permute-start.9
  79.2 1.3 %collective-permute-done.9.other_ref = f32[152,128]{1,0:T(8,128)S(1)} collective-permute-done((f32[152,128]{1,0:T(8,128)S(1)}, f32[152,128]{1,0:T(8,128)S(1)}, u32[]{:S(2)}, u32[]{:S(2)}) %collective-permute-start.9) | collective-permute-done | bytes 77856 | tf_op jit(solution)/shard_map/ppermute | solution.py:329
  80.5 0.8 shard_map.81
  81.3 0.5 all-to-all-done.2
  81.8 0.9 %shard_map.79 = bf16[64,32,128]{2,1,0:T(8,128)(2,1)} custom-call(bf16[64,32,128]{2,1,0:T(8,128)(2,1)S(1)} %bitcast.18, bf16[64,32,128]{2,1,0:T(8,128)(2,1)S(1)} %bitcast.19, bf16[64,32,128]{2,1,0:T(8,128)(2,1)S(1)} %bitcast.20), custom_call_target="tpu_custom_call" | custom-call | flops 262144 | bytes 1572864 | tf_op jit(solution)/shard_map/pallas_call | solution.py:23
  (9 shorter events, 0.1 us)
Async XLA Ops:
  0.6 8.8 %copy-start = (bf16[64,16]{0,1:T(8,128)(2,1)S(1)}, bf16[64,16]{0,1:T(8,128)(2,1)}, u32[]{:S(2)}) copy-start(bf16[64,16]{0,1:T(8,128)(2,1)} %param.7) | copy-start | bytes 6148
  0.6 8.5 %copy-start.1 = (bf16[1,64,32,128]{3,2,1,0:T(8,128)(2,1)S(1)}, bf16[1,64,32,128]{3,2,1,0:T(8,128)(2,1)}, u32[]{:S(2)}) copy-start(bf16[1,64,32,128]{3,2,1,0:T(8,128)(2,1)} %param.4) | copy-start | bytes 1572868
  0.7 23.6 %all-to-all-start = ((bf16[16,4,32,128]{3,2,1,0:T(8,128)(2,1)}), bf16[16,4,32,128]{3,2,1,0:T(8,128)(2,1)S(1)}, u32[]{:S(2)}, u32[]{:S(2)}) async-start(bf16[16,4,32,128]{3,2,1,0:T(8,128)(2,1)} %bitcast.21), calls=%async_computation | async-start | bytes 1048576 | tf_op jit(solution)/shard_map/all_to_all | solution.py:361
  9.1 0.9 %copy-start.4 = (bf16[3,3,64,64]{3,2,1,0:T(8,128)(2,1)S(1)}, bf16[3,3,64,64]{3,2,1,0:T(8,128)(2,1)}, u32[]{:S(2)}) copy-start(bf16[3,3,64,64]{3,2,1,0:T(8,128)(2,1)} %param.6) | copy-start | bytes 221188
  9.4 1.4 %collective-permute-start = (bf16[64,128]{1,0:T(8,128)(2,1)S(1)}, bf16[64,128]{1,0:T(8,128)(2,1)S(1)}, u32[]{:S(2)}, u32[]{:S(2)}) collective-permute-start(bf16[64,128]{1,0:T(8,128)(2,1)S(1)} %fusion), channel_id=1, source_target_pairs={{0,1},{1,0},{2,3},{3,2},{4,5},{5,4},{6,7},{7,6},{8,9},{9,8},{10,11... | collective-permute-start | bytes 49160 | tf_op jit(solution)/shard_map/ppermute | solution.py:329
  25.7 27.6 %all-to-all-start.1 = ((bf16[16,2,4,32,128]{4,3,2,1,0:T(8,128)(2,1)}), bf16[16,2,4,32,128]{4,3,2,1,0:T(8,128)(2,1)S(1)}, u32[]{:S(2)}, u32[]{:S(2)}) async-start(bf16[16,2,4,32,128]{4,3,2,1,0:T(8,128)(2,1)} %shard_map.76), calls=%async_computation.1 | async-start | bytes 2097152 | tf_op jit(solution)/shard_map/all_to_all | solution.py:361
  54.5 2.1 %collective-permute-start.1 = (f32[152,128]{1,0:T(8,128)S(1)}, f32[152,128]{1,0:T(8,128)S(1)}, u32[]{:S(2)}, u32[]{:S(2)}) collective-permute-start(f32[152,128]{1,0:T(8,128)S(1)} %get-tuple-element.23), channel_id=1, source_target_pairs={{0,1},{1,0},{2,3},{3,2},{4,5},{5,4},{6,7},{7,6},{8,9},{9,8},{10,11... | collective-permute-start | bytes 233480 | tf_op jit(solution)/shard_map/ppermute | solution.py:329
  55.8 0.8 copy-start.3
  56.6 10.4 %collective-permute-start.2 = (f32[152,128]{1,0:T(8,128)S(1)}, f32[152,128]{1,0:T(8,128)S(1)}, u32[]{:S(2)}, u32[]{:S(2)}) collective-permute-start(f32[152,128]{1,0:T(8,128)S(1)} %add.30), channel_id=1, source_target_pairs={{0,8},{2,10},{4,12},{6,14},{8,0},{10,2},{12,4},{14,6},{16,24},{18,... | collective-permute-start | bytes 233480 | tf_op jit(solution)/shard_map/ppermute | solution.py:338
  59.7 9.1 %collective-permute-start.3 = (f32[152,128]{1,0:T(8,128)S(1)}, f32[152,128]{1,0:T(8,128)}, u32[]{:S(2)}, u32[]{:S(2)}) collective-permute-start(f32[152,128]{1,0:T(8,128)S(1)} %add.30), channel_id=1, source_target_pairs={{0,16},{2,18},{4,20},{6,22},{8,24},{10,26},{12,28},{14,30},{16,0},... | collective-permute-start | bytes 233480 | tf_op jit(solution)/shard_map/ppermute | solution.py:338
  60.1 8.7 %collective-permute-start.4 = (f32[152,128]{1,0:T(8,128)S(1)}, f32[152,128]{1,0:T(8,128)}, u32[]{:S(2)}, u32[]{:S(2)}) collective-permute-start(f32[152,128]{1,0:T(8,128)S(1)} %add.30), channel_id=1, source_target_pairs={{0,24},{2,26},{4,28},{6,30},{8,16},{10,18},{12,20},{14,22},{16,8},... | collective-permute-start | bytes 233480 | tf_op jit(solution)/shard_map/ppermute | solution.py:338
  62.1 19.7 %all-to-all-start.2 = ((bf16[16,4,32,128]{3,2,1,0:T(8,128)(2,1)}), bf16[16,4,32,128]{3,2,1,0:T(8,128)(2,1)S(1)}, u32[]{:S(2)}, u32[]{:S(2)}) async-start(bf16[16,4,32,128]{3,2,1,0:T(8,128)(2,1)} %copy-done.3), calls=%async_computation.2 | async-start | bytes 1048576 | tf_op jit(solution)/shard_map/all_to_all | solution.py:361
  66.9 6.4 %collective-permute-start.8 = (bf16[64,128]{1,0:T(8,128)(2,1)S(1)}, bf16[64,128]{1,0:T(8,128)(2,1)S(1)}, u32[]{:S(2)}, u32[]{:S(2)}) collective-permute-start(bf16[64,128]{1,0:T(8,128)(2,1)S(1)} %select_bitcast_fusion), channel_id=1, source_target_pairs={{0,1},{1,0},{2,3},{3,2},{4,5},{5,4},{6,7},{7,6},{8,9},{9,8},{10,11... | collective-permute-start | bytes 49160 | tf_op jit(solution)/shard_map/ppermute | solution.py:329
  69.7 6.9 %collective-permute-start.5 = (f32[152,128]{1,0:T(8,128)S(1)}, f32[152,128]{1,0:T(8,128)S(1)}, u32[]{:S(2)}, u32[]{:S(2)}) collective-permute-start(f32[152,128]{1,0:T(8,128)S(1)} %add_add_fusion.1), channel_id=1, source_target_pairs={{0,2},{2,0},{4,6},{6,4},{8,10},{10,8},{12,14},{14,12},{16,18},{18,... | collective-permute-start | bytes 233480 | tf_op jit(solution)/shard_map/ppermute | solution.py:324
  70.8 5.8 %collective-permute-start.6 = (f32[152,128]{1,0:T(8,128)S(1)}, f32[152,128]{1,0:T(8,128)S(1)}, u32[]{:S(2)}, u32[]{:S(2)}) collective-permute-start(f32[152,128]{1,0:T(8,128)S(1)} %add_add_fusion.1), channel_id=1, source_target_pairs={{0,4},{2,6},{4,0},{6,2},{8,12},{10,14},{12,8},{14,10},{16,20},{18,... | collective-permute-start | bytes 233480 | tf_op jit(solution)/shard_map/ppermute | solution.py:324
  71.5 7.7 %collective-permute-start.7 = (f32[152,128]{1,0:T(8,128)S(1)}, f32[152,128]{1,0:T(8,128)S(1)}, u32[]{:S(2)}, u32[]{:S(2)}) collective-permute-start(f32[152,128]{1,0:T(8,128)S(1)} %add_add_fusion.1), channel_id=1, source_target_pairs={{0,6},{2,4},{4,2},{6,0},{8,14},{10,12},{12,10},{14,8},{16,22},{18,... | collective-permute-start | bytes 233480 | tf_op jit(solution)/shard_map/ppermute | solution.py:324
  73.3 1.0 %copy-start.2 = (bf16[1,64,32,128]{3,2,1,0:T(8,128)(2,1)S(1)}, bf16[1,64,32,128]{3,2,1,0:T(8,128)(2,1)}, u32[]{:S(2)}) copy-start(bf16[1,64,32,128]{3,2,1,0:T(8,128)(2,1)} %param.5) | copy-start | bytes 1572868
  79.1 1.3 %collective-permute-start.9 = (f32[152,128]{1,0:T(8,128)S(1)}, f32[152,128]{1,0:T(8,128)S(1)}, u32[]{:S(2)}, u32[]{:S(2)}) collective-permute-start(f32[152,128]{1,0:T(8,128)S(1)} %add_add_fusion.mine_ref), channel_id=1, source_target_pairs={{0,1},{1,0},{2,3},{3,2},{4,5},{5,4},{6,7},{7,6},{8,9},{9,8},{10,11... | collective-permute-start | bytes 233480 | tf_op jit(solution)/shard_map/ppermute | solution.py:329
